TPU v7x, 128 devices: a whole 4x4x4 slice. The times are simulated.
128 devices in a mesh: emit: 2 (over x_hi), slab: 64 (over z, y, x_lo, core).
Axes of the slice: x: 4 (x_hi: 2, x_lo: 2; x = x_hi * 2 + x_lo), y: 4, z: 4, core: 2. Of those that a mesh axis runs over, the one named last changes fastest.
Arguments:
- sound_speed: float32 [256, 256, 256], P('slab'), may hold values from 0.7 to 1.4
- density: float32 [256, 256, 256], P('slab'), may hold values from 0.8 to 1.8
- absorption: float32 [256, 256, 256], P('slab'), may hold values from 0.05 to 1
- pressure_start: float32 [2, 256, 256, 256], P('emit', 'slab'), may hold values from -6 to 6
- velocity_start: float32 [2, 3, 256, 256, 256], P('emit', None, 'slab'), may hold values from -3 to 3
- adjoint_pressure: float32 [2, 256, 256, 256], P('emit', 'slab'), may hold values from -6 to 6
- adjoint_velocity: float32 [2, 3, 256, 256, 256], P('emit', None, 'slab'), may hold values from -6 to 6
- emitter_voxel: int32 [2, 256], P('emit'), may hold values from 0 to 16777215
- emitter_delay: int32 [2, 256], P('emit'), may hold values from 0 to 62
- drive_waveform_samples: float32 [64], replicated, may hold values from -8 to 8
- recorded_pressures: float32 [2, 2, 1024], P('emit'), may hold values from -6 to 6
- sensor_flat_position: int32 [1024], replicated, may hold values from 0 to 16777215
Outputs:
- grad_speed: float32 [256, 256, 256], P('slab')
- grad_density: float32 [256, 256, 256], P('slab')
Inputs may be any that keep to these rules, and one draw needn't show every extreme that they name: `emitter_voxel`: flat index x * 256 * 256 + y * 256 + z of a voxel. `sensor_flat_position`: flat index x * 256 * 256 + y * 256 + z of a voxel.
All inputs are finite; a program needn't handle non-finite values.
Results may differ from a plain program's by a relative error of at most 0.0001.
Values sent between devices are 32-bit elements; how exact they have to be, the bound alone decides.
No kernel may reach another device: no remote copies, remote signals or barrier semaphores. Data moves between devices by JAX's collectives and lax.ppermute only.
A program may use at most 128 MiB of HBM per device.

v0:
```python
import math

import jax
import jax.numpy as jnp
from jax import lax
from jax.sharding import PartitionSpec as P

STEPS = 2


time_step = 0.2


def deriv_matrix(length):
    halfway = length // 2
    modes = jnp.arange(1, halfway, dtype=jnp.int32)
    points = jnp.arange(length, dtype=jnp.int32)
    shifted = modes[None, :] * (2 * points[:, None] + 1) % (2 * length)
    unshifted = modes[None, :] * (2 * points[:, None]) % (2 * length)
    factor = math.pi / length
    wavenumber = modes.astype(jnp.float32) * (2.0 * factor)
    shift_angle = shifted.astype(jnp.float32) * factor
    plain_angle = unshifted.astype(jnp.float32) * factor
    cosine_part = jnp.cos(shift_angle) * wavenumber[None, :]
    sine_part = jnp.sin(shift_angle) * wavenumber[None, :]
    matrix = jnp.dot(cosine_part, jnp.sin(plain_angle).T, precision=lax.Precision.HIGHEST)
    matrix = matrix - jnp.dot(sine_part, jnp.cos(plain_angle).T, precision=lax.Precision.HIGHEST)
    return matrix * (2.0 / length)


def along_second(matrix, volume):
    return jnp.einsum("ij,ajc->aic", matrix, volume, precision=lax.Precision.HIGHEST)


def along_third(matrix, volume):
    return jnp.einsum("abj,ij->abi", volume, matrix, precision=lax.Precision.HIGHEST)


def stacked_first(matrix, stacked):
    return jnp.einsum("ij,mjbc->mibc", matrix, stacked, precision=lax.Precision.HIGHEST)


def x_apply(matrix, stacked):
    applied = stacked_first(
        matrix, lax.all_to_all(stacked, "slab", split_axis=2, concat_axis=1, tiled=True)
    )
    return lax.all_to_all(applied, "slab", split_axis=1, concat_axis=2, tiled=True)


def local_index(voxels, offset, cell_count):
    local_voxel = voxels - offset
    inside = (local_voxel >= 0) & (local_voxel < cell_count)
    return (jnp.clip(local_voxel, 0, cell_count - 1), inside)


def local(
    sound_speed,
    density,
    absorption,
    pressure_start,
    velocity_start,
    adjoint_pressure,
    adjoint_velocity,
    emitter_voxel,
    emitter_delay,
    drive_waveform_samples,
    recorded_pressures,
    sensor_flat_position,
):
    slab_count = lax.axis_size("slab")
    slab_index = lax.axis_index("slab")
    local_x, width_y, width_z = sound_speed.shape
    matrix_x = deriv_matrix(local_x * slab_count)
    matrix_y = deriv_matrix(width_y)
    matrix_z = deriv_matrix(width_z)
    lattice_layout = sound_speed.shape
    cell_count = local_x * width_y * width_z
    offset = slab_index * cell_count
    transmitter_number, transmitter_within_domain = local_index(
        emitter_voxel[0], offset, cell_count
    )
    recv_index, recv_inside = local_index(sensor_flat_position, offset, cell_count)
    sample_ids = jnp.arange(drive_waveform_samples.shape[0], dtype=jnp.int32)
    compressibility_modulus = density * sound_speed * sound_speed
    inverse_density = 1.0 / density
    retained_snapshots = 1.0 - time_step * absorption
    pressure_tension = pressure_start[0]
    vel_x, vel_y, vel_z = (velocity_start[0, 0], velocity_start[0, 1], velocity_start[0, 2])
    adj_p = adjoint_pressure[0]
    adj_x, adj_y, adj_z = (adjoint_velocity[0, 0], adjoint_velocity[0, 1], adjoint_velocity[0, 2])
    saved = []
    residuals = []
    for loop_tally in range(STEPS):
        previous = pressure_tension
        vel_y = vel_y - time_step * inverse_density * along_second(matrix_y, pressure_tension)
        vel_z = vel_z - time_step * inverse_density * along_third(matrix_z, pressure_tension)
        div_rest = along_second(matrix_y.T, vel_y) + along_third(matrix_z.T, vel_z)
        grad_x = x_apply(matrix_x, pressure_tension[None])[0]
        vel_x = vel_x - time_step * inverse_density * grad_x
        div_x = x_apply(matrix_x.T, vel_x[None])[0]
        divergence = div_x + div_rest
        pressure_tension = (
            retained_snapshots * pressure_tension + time_step * compressibility_modulus * divergence
        )
        selected_option = sample_ids[None, :] == (emitter_delay[0] + loop_tally)[:, None]
        radiated_intensity = jnp.sum(
            jnp.where(selected_option, drive_waveform_samples[None, :], 0.0), axis=1
        )
        radiated_intensity = jnp.where(transmitter_within_domain, radiated_intensity, 0.0)
        pressure_tension = (
            pressure_tension.reshape(-1)
            .at[transmitter_number]
            .add(radiated_intensity)
            .reshape(lattice_layout)
        )
        recorded = pressure_tension.reshape(-1)[recv_index] - recorded_pressures[0, loop_tally]
        residuals.append(jnp.where(recv_inside, recorded, 0.0))
        saved.append((previous, divergence, grad_x))
    grad_bulk = jnp.zeros(lattice_layout, jnp.float32)
    grad_buoy = jnp.zeros(lattice_layout, jnp.float32)
    for loop_tally in reversed(range(STEPS)):
        previous, divergence, stored_grad = saved[loop_tally]
        adj_p = adj_p.reshape(-1).at[recv_index].add(residuals[loop_tally]).reshape(lattice_layout)
        grad_bulk = grad_bulk + time_step * divergence * adj_p
        weight = time_step * compressibility_modulus * adj_p
        adj_y = adj_y + along_second(matrix_y, weight)
        adj_z = adj_z + along_third(matrix_z, weight)
        rest_terms = (
            along_second(matrix_y, previous) * adj_y + along_third(matrix_z, previous) * adj_z
        )
        sent = jnp.stack([weight, previous])
        applied = x_apply(matrix_x, sent)
        press_grad_x = applied[1]
        adj_x = adj_x + applied[0]
        buoy_term_x = press_grad_x * adj_x
        back_x = x_apply(matrix_x.T, (inverse_density * adj_x)[None])[0]
        grad_buoy = grad_buoy - time_step * (buoy_term_x + rest_terms)
        back_rest = along_second(matrix_y.T, inverse_density * adj_y) + along_third(
            matrix_z.T, inverse_density * adj_z
        )
        adj_p = retained_snapshots * adj_p - time_step * (back_x + back_rest)
    speed_part = grad_bulk * 2.0 * density * sound_speed
    density_part = (
        grad_bulk * sound_speed * sound_speed - grad_buoy * inverse_density * inverse_density
    )
    speed_total, density_total = lax.psum((speed_part, density_part), "emit")
    return (speed_total, density_total)


def solution(mesh):
    in_specs = (
        P("slab", None, None),
        P("slab", None, None),
        P("slab", None, None),
        P("emit", "slab", None, None),
        P("emit", None, "slab", None, None),
        P("emit", "slab", None, None),
        P("emit", None, "slab", None, None),
        P("emit", None),
        P("emit", None),
        P(),
        P("emit", None, None),
        P(),
    )
    out_specs = (P("slab", None, None), P("slab", None, None))
    return jax.shard_map(local, mesh=mesh, in_specs=in_specs, out_specs=out_specs, check_vma=False)
```

profile of v0, /device:TPU:0, one launch (start us, length us, event | category | flops | bytes accessed | tf_op | source)
XLA Modules:
  0.0 620.3 jit_solution(16222227019005715433)
XLA Ops:
  10.0 10.0 %all-to-all-start = ((f32[1,4,256,256]{3,1,0,2:T(4,128)}), f32[1,4,256,256]{3,1,0,2:T(4,128)S(1)}, u32[]{:S(2)}, u32[]{:S(2)}) async-start(f32[1,4,256,256]{3,1,0,2:T(4,128)} %copy.133), calls=%async_computation | async-start | bytes 2097152 | tf_op jit(solution)/shard_map/all_to_all | solution.py:45
  22.8 15.6 %all-to-all-done = f32[1,4,256,256]{3,1,0,2:T(4,128)S(1)} async-done(((f32[1,4,256,256]{3,1,0,2:T(4,128)}), f32[1,4,256,256]{3,1,0,2:T(4,128)S(1)}, u32[]{:S(2)}, u32[]{:S(2)}) %all-to-all-start) | async-done | bytes 1048608 | tf_op jit(solution)/shard_map/all_to_all | solution.py:45
  40.7 22.6 %all_to_all.216 = f32[1,256,4,256]{3,2,0,1:T(4,128)S(1)} all-to-all(f32[1,256,4,256]{3,2,0,1:T(4,128)S(1)} %copy.135), channel_id=1, replica_groups=mesh['emit'=2,'slab'=64] {'slab'}, dimensions={1} | all-to-all | bytes 2097152 | tf_op jit(solution)/shard_map/all_to_all | solution.py:47
  68.1 4.8 all-to-all-start.2
  73.1 18.2 %all-to-all-done.2 = f32[1,4,256,256]{3,1,0,2:T(4,128)S(1)} async-done(((f32[1,4,256,256]{3,1,0,2:T(4,128)}), f32[1,4,256,256]{3,1,0,2:T(4,128)S(1)}, u32[]{:S(2)}, u32[]{:S(2)}) %all-to-all-start.2) | async-done | bytes 1048608 | tf_op jit(solution)/shard_map/all_to_all | solution.py:45
  94.7 5.5 all-to-all-start.3
  107.0 11.5 %all-to-all-done.3 = f32[1,256,4,256]{3,2,0,1:T(4,128)} async-done(((f32[1,256,4,256]{3,2,0,1:T(4,128)}), f32[1,256,4,256]{3,2,0,1:T(4,128)}, u32[]{:S(2)}, u32[]{:S(2)}) %all-to-all-start.3) | async-done | bytes 1048608 | tf_op jit(solution)/shard_map/all_to_all | solution.py:47
  121.3 5.5 fusion.31
  133.2 22.5 %all_to_all.217 = f32[1,4,256,256]{3,1,0,2:T(4,128)S(1)} all-to-all(f32[1,4,256,256]{3,1,0,2:T(4,128)S(1)} %copy.145), channel_id=1, replica_groups=mesh['emit'=2,'slab'=64] {'slab'}, dimensions={2} | all-to-all | bytes 2097152 | tf_op jit(solution)/shard_map/all_to_all | solution.py:45
  161.3 23.1 %all_to_all.218 = f32[1,256,4,256]{3,2,0,1:T(4,128)S(1)} all-to-all(f32[1,256,4,256]{3,2,0,1:T(4,128)} %copy.148), channel_id=1, replica_groups=mesh['emit'=2,'slab'=64] {'slab'}, dimensions={1} | all-to-all | bytes 2097152 | tf_op jit(solution)/shard_map/all_to_all | solution.py:47
  191.9 5.6 all-to-all-start.6
  200.4 6.2 gather_fusion.1
  206.6 9.3 %all-to-all-done.6 = f32[1,4,256,256]{3,1,0,2:T(4,128)} async-done(((f32[1,4,256,256]{3,1,0,2:T(4,128)}), f32[1,4,256,256]{3,1,0,2:T(4,128)}, u32[]{:S(2)}, u32[]{:S(2)}) %all-to-all-start.6) | async-done | bytes 1048608 | tf_op jit(solution)/shard_map/all_to_all | solution.py:45
  222.7 5.9 all-to-all-start.7
  237.7 9.1 %all-to-all-done.7 = f32[1,256,4,256]{3,2,0,1:T(4,128)} async-done(((f32[1,256,4,256]{3,2,0,1:T(4,128)}), f32[1,256,4,256]{3,2,0,1:T(4,128)}, u32[]{:S(2)}, u32[]{:S(2)}) %all-to-all-start.7) | async-done | bytes 1048608 | tf_op jit(solution)/shard_map/all_to_all | solution.py:47
  251.9 5.4 multiply_add_fusion.1
  260.6 6.2 gather_fusion
  266.7 9.7 %scatter_fusion.2 = f32[262144]{0:T(1024)} fusion(f32[262144]{0:T(1024)} %bitcast.98, s32[1024]{0:T(1024)S(1)} %get-tuple-element.11, f32[1024]{0:T(1024)S(1)} %subtract_select_fusion.1), kind=kCustom, calls=%fused_computation.4 | custom fusion | flops 1024 | bytes 16384 | tf_op jit(solution)/shard_map/scatter-add | solution.py:123
  280.7 33.5 %all_to_all.219 = f32[2,4,256,256]{3,1,0,2:T(4,128)S(1)} all-to-all(f32[2,4,256,256]{3,1,0,2:T(4,128)S(1)} %copy.159), channel_id=1, replica_groups=mesh['emit'=2,'slab'=64] {'slab'}, dimensions={2} | all-to-all | bytes 4194304 | tf_op jit(solution)/shard_map/all_to_all | solution.py:45
  315.1 4.8 fusion.4
  322.9 34.3 %all_to_all.220 = f32[2,256,4,256]{3,2,0,1:T(4,128)S(1)} all-to-all(f32[2,256,4,256]{3,2,0,1:T(4,128)} %copy.162), channel_id=1, replica_groups=mesh['emit'=2,'slab'=64] {'slab'}, dimensions={1} | all-to-all | bytes 4194304 | tf_op jit(solution)/shard_map/all_to_all | solution.py:47
  365.2 23.2 %all_to_all.221 = f32[1,4,256,256]{3,1,0,2:T(4,128)S(1)} all-to-all(f32[1,4,256,256]{3,1,0,2:T(4,128)S(1)} %copy.165), channel_id=1, replica_groups=mesh['emit'=2,'slab'=64] {'slab'}, dimensions={2} | all-to-all | bytes 2097152 | tf_op jit(solution)/shard_map/all_to_all | solution.py:45
  394.0 5.5 all-to-all-start.11
  408.1 9.7 %all-to-all-done.11 = f32[1,256,4,256]{3,2,0,1:T(4,128)} async-done(((f32[1,256,4,256]{3,2,0,1:T(4,128)}), f32[1,256,4,256]{3,2,0,1:T(4,128)}, u32[]{:S(2)}, u32[]{:S(2)}) %all-to-all-start.11) | async-done | bytes 1048608 | tf_op jit(solution)/shard_map/all_to_all | solution.py:47
  428.0 10.0 %scatter_fusion.3 = f32[262144]{0:T(1024)} fusion(f32[262144]{0:T(1024)} %bitcast.246, s32[1024]{0:T(1024)S(1)} %get-tuple-element.11, f32[1024]{0:T(1024)S(1)} %get-tuple-element.8), kind=kCustom, calls=%fused_computation.5 | custom fusion | flops 1024 | bytes 16384 | tf_op jit(solution)/shard_map/scatter-add | solution.py:123
  440.5 4.0 multiply_multiply_fusion.3
  446.1 33.4 %all_to_all.222 = f32[2,4,256,256]{3,1,0,2:T(4,128)S(1)} all-to-all(f32[2,4,256,256]{3,1,0,2:T(4,128)S(1)} %copy.175), channel_id=1, replica_groups=mesh['emit'=2,'slab'=64] {'slab'}, dimensions={2} | all-to-all | bytes 4194304 | tf_op jit(solution)/shard_map/all_to_all | solution.py:45
  480.2 4.8 fusion.7
  488.0 5.6 all-to-all-start.13
  502.5 20.4 %all-to-all-done.13 = f32[2,256,4,256]{3,2,0,1:T(4,128)} async-done(((f32[2,256,4,256]{3,2,0,1:T(4,128)}), f32[2,256,4,256]{3,2,0,1:T(4,128)}, u32[]{:S(2)}, u32[]{:S(2)}) %all-to-all-start.13) | async-done | bytes 2097184 | tf_op jit(solution)/shard_map/all_to_all | solution.py:47
  532.9 8.2 %fusion.26 = f32[4,256,256]{2,1,0:T(8,128)} fusion(f32[4,256,256]{2,1,0:T(8,128)} %fusion.25, f32[4,256,256]{2,1,0:T(8,128)S(1)} %copy-done.4, f32[4,256,256]{2,1,0:T(8,128)} %fusion.14, f32[4,256,256]{2,1,0:T(8,128)} %param.12, f32[4,256,256]{2,1,0:T(8,128)} %get-tuple-element.7, f32[4,256,256]{2,1,0:T(8,128)} %squeeze.72, f32[4,256,256]{2,1,0:T(8,128)} %squeeze.73, ...), kind=kOutput, calls=%fused_computation.48 | convolution fusion | flops 811335680 | bytes 18087936 | tf_op jit(solution)/shard_map/ij,ajc->aic/dot_general | solution.py:32
  541.1 68.5 %all-reduce.3.cloned.1.call-done = (f32[4,256,256]{2,1,0:T(8,128)}, f32[4,256,256]{2,1,0:T(8,128)}) async-done(((f32[4,256,256]{2,1,0:T(8,128)}, f32[4,256,256]{2,1,0:T(8,128)}), (f32[4,256,256]{2,1,0:T(8,128)}, f32[4,256,256]{2,1,0:T(8,128)})) %all-reduce.3.cloned.1.call-update) | async-done | bytes 2097168 | tf_op jit(solution)/shard_map/psum | solution.py:146
  (132 shorter events, 142.7 us)
Async XLA Ops:
  10.0 28.4 %all-to-all-start = ((f32[1,4,256,256]{3,1,0,2:T(4,128)}), f32[1,4,256,256]{3,1,0,2:T(4,128)S(1)}, u32[]{:S(2)}, u32[]{:S(2)}) async-start(f32[1,4,256,256]{3,1,0,2:T(4,128)} %copy.133), calls=%async_computation | async-start | bytes 2097152 | tf_op jit(solution)/shard_map/all_to_all | solution.py:45
  63.3 1.2 copy-start
  64.6 3.5 copy-start.9
  66.4 6.5 %copy-start.16 = (s32[1,256]{1,0:T(1,128)S(1)}, s32[1,256]{1,0:T(1,128)}, u32[]{:S(2)}) copy-start(s32[1,256]{1,0:T(1,128)} %param.19) | copy-start | bytes 3076
  66.4 6.5 %copy-start.17 = (s32[1,256]{1,0:T(1,128)S(1)}, s32[1,256]{1,0:T(1,128)}, u32[]{:S(2)}) copy-start(s32[1,256]{1,0:T(1,128)} %param.20) | copy-start | bytes 3076
  66.4 6.6 %copy-start.18 = (f32[64]{0:T(128)S(1)}, f32[64]{0:T(128)}, u32[]{:S(2)}) copy-start(f32[64]{0:T(128)} %param.21) | copy-start | bytes 772
  68.1 23.2 %all-to-all-start.2 = ((f32[1,4,256,256]{3,1,0,2:T(4,128)}), f32[1,4,256,256]{3,1,0,2:T(4,128)S(1)}, u32[]{:S(2)}, u32[]{:S(2)}) async-start(f32[1,4,256,256]{3,1,0,2:T(4,128)} %copy.137), calls=%async_computation.2 | async-start | bytes 2097152 | tf_op jit(solution)/shard_map/all_to_all | solution.py:45
  93.4 6.9 %copy-start.1 = (f32[1,4,256,256]{3,2,1,0:T(8,128)S(1)}, f32[1,4,256,256]{3,2,1,0:T(8,128)}, u32[]{:S(2)}) copy-start(f32[1,4,256,256]{3,2,1,0:T(8,128)} %param.15) | copy-start | bytes 3145732
  94.7 23.8 %all-to-all-start.3 = ((f32[1,256,4,256]{3,2,0,1:T(4,128)}), f32[1,256,4,256]{3,2,0,1:T(4,128)}, u32[]{:S(2)}, u32[]{:S(2)}) async-start(f32[1,256,4,256]{3,2,0,1:T(4,128)} %copy.140), calls=%async_computation.3 | async-start | bytes 2097152 | tf_op jit(solution)/shard_map/all_to_all | solution.py:47
  103.3 3.7 copy-start.11
  191.9 8.4 %copy-start.14 = (s32[1024]{0:T(1024)S(1)}, s32[1024]{0:T(1024)}, u32[]{:S(2)}) copy-start(s32[1024]{0:T(1024)} %param.23) | copy-start | bytes 12292
  191.9 8.4 %copy-start.15 = (f32[1,2,1024]{2,1,0:T(2,128)S(1)}, f32[1,2,1024]{2,1,0:T(2,128)}, u32[]{:S(2)}) copy-start(f32[1,2,1024]{2,1,0:T(2,128)} %param.22) | copy-start | bytes 24580
  191.9 23.9 %all-to-all-start.6 = ((f32[1,4,256,256]{3,1,0,2:T(4,128)}), f32[1,4,256,256]{3,1,0,2:T(4,128)}, u32[]{:S(2)}, u32[]{:S(2)}) async-start(f32[1,4,256,256]{3,1,0,2:T(4,128)} %copy.150), calls=%async_computation.6 | async-start | bytes 2097152 | tf_op jit(solution)/shard_map/all_to_all | solution.py:45
  222.7 24.2 %all-to-all-start.7 = ((f32[1,256,4,256]{3,2,0,1:T(4,128)}), f32[1,256,4,256]{3,2,0,1:T(4,128)}, u32[]{:S(2)}, u32[]{:S(2)}) async-start(f32[1,256,4,256]{3,2,0,1:T(4,128)} %copy.153), calls=%async_computation.7 | async-start | bytes 2097152 | tf_op jit(solution)/shard_map/all_to_all | solution.py:47
  229.9 2.4 copy-start.6
  229.9 4.5 copy-start.12
  232.3 2.1 copy-start.8
  246.8 5.0 copy-start.3
  278.0 1.2 copy-start.10
  394.0 23.8 %all-to-all-start.11 = ((f32[1,256,4,256]{3,2,0,1:T(4,128)}), f32[1,256,4,256]{3,2,0,1:T(4,128)}, u32[]{:S(2)}, u32[]{:S(2)}) async-start(f32[1,256,4,256]{3,2,0,1:T(4,128)} %copy.168), calls=%async_computation.11 | async-start | bytes 2097152 | tf_op jit(solution)/shard_map/all_to_all | solution.py:47
  401.7 1.0 copy-start.7
  440.5 4.1 copy-start.2
  488.0 34.9 %all-to-all-start.13 = ((f32[2,256,4,256]{3,2,0,1:T(4,128)}), f32[2,256,4,256]{3,2,0,1:T(4,128)}, u32[]{:S(2)}, u32[]{:S(2)}) async-start(f32[2,256,4,256]{3,2,0,1:T(4,128)} %copy.178), calls=%async_computation.13 | async-start | bytes 4194304 | tf_op jit(solution)/shard_map/all_to_all | solution.py:47
  493.6 116.0 %all-reduce.3.cloned.1.call-start = ((), (), s32[]{:S(2)}) async-start(), calls=%async_computation.14 | async-start | bytes 4194304 | tf_op jit(solution)/shard_map/psum | solution.py:146
  493.9 5.1 copy-start.5
  527.9 5.1 copy-start.4
  609.6 2.4 copy-start.13
Sparse Core Ops, SparseCore 0:
  541.3 68.3 all-reduce.2
where the time goes:
time: 631 us; the launch traced here: 620 us
  blocking collectives  193 us (31%)
  waiting for transfers between devices  162 us (26%)
  local copies, waits for them, and re-layouts  99.8 us (16%)
  matrix products  71.9 us (11%)
  starting transfers between devices  43.3 us (7%)
  other arithmetic  35.4 us (6%)
  between operations  15 us (2%)
    all_to_all x4, blocking collectives, x_apply(): lax.all_to_all(stacked, 'slab', split_axis=2, concat_axis=1, tiled=True)  113 us
    all_to_all x3, blocking collectives, x_apply(): lax.all_to_all(applied, 'slab', split_axis=1, concat_axis=2, tiled=True)  80 us
    psum x1, waiting for transfers between devices, local(): speed_total, density_total = lax.psum((speed_part, density_part), 'emit')  68.5 us
    all_to_all x4, waiting for transfers between devices, x_apply(): lax.all_to_all(applied, 'slab', split_axis=1, concat_axis=2, tiled=True)  50.7 us
    all_to_all x3, waiting for transfers between devices, x_apply(): lax.all_to_all(stacked, 'slab', split_axis=2, concat_axis=1, tiled=True)  43.1 us
    dot_general x7, matrix products, along_second(): jnp.einsum('ij,ajc->aic', matrix, volume, precision=lax.Precision.HIGHEST)  30.2 us
    all_to_all x4, starting transfers between devices, x_apply(): lax.all_to_all(applied, 'slab', split_axis=1, concat_axis=2, tiled=True)  22.5 us
    dot_general x7, matrix products, stacked_first(): jnp.einsum('ij,mjbc->mibc', matrix, stacked, precision=lax.Precision.HIGH...  20.7 us
  transfers between devices with their start and end apart: 8, of which 8 were waited for; matrix products, arithmetic and copies ran while one was open for 7% of the time, Pallas kernels for 0%

commit v1 on v0

v1 whole, which is shorter than its diff:
```python
import numpy as np
import jax
import jax.numpy as jnp
from jax import lax
from jax.experimental import pallas as pl
from jax.experimental.pallas import tpu as pltpu
from jax.sharding import PartitionSpec as P

STEPS = 2
DT = 0.2
F32 = jnp.float32
BF16 = jnp.bfloat16
ALL = ("emit", "slab")
VMEM_LIMIT = 48 * 2**20


def deriv_matrix(n):
    k = np.arange(1, n // 2, dtype=np.int64)
    pts = np.arange(n, dtype=np.int64)
    shifted = (k[None, :] * (2 * pts[:, None] + 1)) % (2 * n) * (np.pi / n)
    plain = (k[None, :] * (2 * pts[:, None])) % (2 * n) * (np.pi / n)
    w = k * (2.0 * np.pi / n)
    m = (np.cos(shifted) * w) @ np.sin(plain).T - (np.sin(shifted) * w) @ np.cos(plain).T
    return m * (2.0 / n)


def pair_const(m):
    m = m.astype(np.float32)
    return [jnp.asarray(m), jnp.asarray(np.ascontiguousarray(m.T))]


def split2(v):
    hi = v.astype(BF16)
    return hi, (v - hi.astype(F32)).astype(BF16)


def split3(v):
    hi = v.astype(BF16)
    rest = v - hi.astype(F32)
    mid = rest.astype(BF16)
    return hi, mid, (rest - mid.astype(F32)).astype(BF16)


def dot(a, b):
    return jnp.dot(a, b, preferred_element_type=F32)


def left(m, v):
    mh, ml = split2(m[...])
    h, l = split2(v)
    return dot(mh, h) + (dot(mh, l) + dot(ml, h))


def right(v, m):
    mh, ml = split2(m[...])
    h, l = split2(v)
    return dot(h, mh) + (dot(l, mh) + dot(h, ml))


def params(n_grid):
    return pltpu.CompilerParams(
        dimension_semantics=("arbitrary",) * n_grid, vmem_limit_bytes=VMEM_LIMIT
    )


def plane_onehot(pos_row, plane, ny, nz):
    local = pos_row - plane * (ny * nz)
    y = lax.broadcasted_iota(jnp.int32, (ny, pos_row.shape[1]), 0)
    return jnp.where((local >= y * nz) & (local < y * nz + nz), 1.0, 0.0).astype(BF16)


def column_onehot(pos_col, nz):
    z = lax.broadcasted_iota(jnp.int32, (pos_col.shape[0], nz), 1)
    return (pos_col & (nz - 1) if nz & (nz - 1) == 0 else lax.rem(pos_col, nz)) == z


def drive_at(delay_col, drive_row, step):
    k = lax.broadcasted_iota(jnp.int32, (delay_col.shape[0], drive_row.shape[1]), 1)
    return jnp.sum(jnp.where(delay_col + step == k, drive_row, 0.0), axis=1, keepdims=True)


def three(onehot, value_col):
    return jnp.concatenate([jnp.where(onehot, v.astype(F32), 0.0).astype(BF16) for v in split3(value_col)], axis=1)


def sum3(v, n):
    return v[:, :n] + v[:, n : 2 * n] + v[:, 2 * n :]


def start_kernel(
    ids, c, rho, alpha, p0, ux, uy, uz, vx, epos_row, epos_col, delay, drive, gm, tm,
    buf, u1y, u1z, yz0, gy0, gz0, v0, mat, rhs,
):
    i = pl.program_id(0)
    ny, nz = p0.shape[1], p0.shape[2]
    half = ny // 2

    @pl.when(i == 0)
    def _():
        rhs[...] = three(column_onehot(epos_col[...], nz), drive_at(delay[...], drive[...], 0))

    @pl.when(i < 4)
    def _():
        dens, speed, p = rho[0], c[0], p0[0]
        b = 1.0 / dens
        bulk = dens * speed * speed
        gy = left(gm, p)
        gz = right(p, tm)
        wy = uy[0] - DT * b * gy
        wz = uz[0] - DT * b * gz
        yz = left(tm, wy) + right(wz, gm)
        shot = sum3(dot(plane_onehot(epos_row[...], ids[1] * 4 + i, ny, nz), rhs[...]), nz)
        v = (1.0 - DT * alpha[0]) * p + (DT * bulk) * yz + shot
        u1y[0], u1z[0], yz0[0], gy0[0], gz0[0], v0[0] = wy, wz, yz, gy, gz, v
        for yl in range(2):
            rows = slice(yl * half, (yl + 1) * half)
            buf[:, 0, yl, :] = p[rows]
            buf[:, 0, 2 + yl, :] = ux[0, rows, :]
            buf[:, 0, 4 + yl, :] = v[rows]
            buf[:, 0, 6 + yl, :] = vx[0, rows, :]
        for xm in range(2):

            @pl.when(i == 2 * ids[0] + xm)
            def _():
                for yl in range(2):
                    rows = slice(yl * half, (yl + 1) * half)
                    mat[:, 4 * xm + yl, :] = b[rows]
                    mat[:, 4 * xm + 2 + yl, :] = bulk[rows]

    @pl.when(i == 4)
    def _():
        buf[:, 0] = mat[...]


def whole(shape):
    return pl.BlockSpec(shape, lambda i: (0,) * len(shape))


def smem():
    return pl.BlockSpec(memory_space=pltpu.SMEM)


def group_plane(shape, pick):
    block = (None,) * (len(shape) - 3) + (1,) + shape[-2:]
    return lambda a: pl.BlockSpec(block, lambda i: (0, a)[: len(shape) - 3] + (pick(i), 0, 0))


def start_call(ids, c, rho, alpha, p0, u, v, epos, delay, drive, mats, ndev):
    nx, ny, nz = c.shape
    pick = lambda i: jnp.minimum(i, 3)
    plane = pl.BlockSpec((1, ny, nz), lambda i: (pick(i), 0, 0))
    vec = group_plane(u.shape, pick)
    n_e = epos.shape[0]
    nat = jax.ShapeDtypeStruct(c.shape, F32)
    return pl.pallas_call(
        start_kernel,
        grid=(5,),
        in_specs=[smem()] + [plane] * 3
        + [group_plane(p0.shape, pick)(0), vec(0), vec(1), vec(2), vec(0)]
        + [whole((1, n_e)), whole((n_e, 1)), whole((n_e, 1)), whole((1, drive.shape[0]))]
        + [whole((ny, ny))] * 2,
        out_specs=[pl.BlockSpec((ndev, 1, 8, nz), lambda i: (0, i, 0, 0))] + [plane] * 6,
        out_shape=[jax.ShapeDtypeStruct((ndev, 5, 8, nz), F32)] + [nat] * 6,
        scratch_shapes=[pltpu.VMEM((ndev, 8, nz), F32), pltpu.VMEM((n_e, 3 * nz), BF16)],
        compiler_params=params(1),
        cost_estimate=pl.CostEstimate(flops=2 * 10**9, bytes_accessed=19 * 2**20, transcendentals=0),
        name="start",
    )(
        ids, c, rho, alpha, p0, u, u, u, v, epos.reshape(1, -1), epos.reshape(-1, 1),
        delay.reshape(-1, 1), drive.reshape(1, -1), *mats,
    )


def maps_kernel(
    ids, spos_row, spos_col, rec, epos_row, epos_col, delay, drive, cnt, d0, d1, e1, srhs, erhs
):
    i = pl.program_id(0)
    ny, nz = cnt.shape[1], cnt.shape[2]

    @pl.when(i == 0)
    def _():
        oh = column_onehot(spos_col[...], nz)
        srhs[:, :nz] = jnp.where(oh, 1.0, 0.0).astype(BF16)
        srhs[:, nz : 4 * nz] = three(oh, rec[:, 0:1])
        srhs[:, 4 * nz :] = three(oh, rec[:, 1:2])
        erhs[...] = three(column_onehot(epos_col[...], nz), drive_at(delay[...], drive[...], 1))

    plane = ids[1] * 4 + i
    s = plane_onehot(spos_row[...], plane, ny, nz)
    cnt[0] = dot(s, srhs[:, :nz])
    d0[0] = sum3(dot(s, srhs[:, nz : 4 * nz]), nz)
    d1[0] = sum3(dot(s, srhs[:, 4 * nz :]), nz)
    e1[0] = sum3(dot(plane_onehot(epos_row[...], plane, ny, nz), erhs[...]), nz)


def maps_call(ids, spos, rec, epos, delay, drive, shape):
    nx, ny, nz = shape
    plane = pl.BlockSpec((1, ny, nz), lambda i: (i, 0, 0))
    n_e, n_s = epos.shape[0], spos.shape[0]
    nat = jax.ShapeDtypeStruct(shape, F32)
    return pl.pallas_call(
        maps_kernel,
        grid=(nx,),
        in_specs=[smem(), whole((1, n_s)), whole((n_s, 1)), whole((n_s, STEPS)),
                  whole((1, n_e)), whole((n_e, 1)), whole((n_e, 1)), whole((1, drive.shape[0]))],
        out_specs=[plane] * 4,
        out_shape=[nat] * 4,
        scratch_shapes=[pltpu.VMEM((n_s, 7 * nz), BF16), pltpu.VMEM((n_e, 3 * nz), BF16)],
        compiler_params=params(1),
        cost_estimate=pl.CostEstimate(flops=4 * 10**9, bytes_accessed=5 * 2**20, transcendentals=0),
        name="maps",
    )(
        ids, spos.reshape(1, -1), spos.reshape(-1, 1), rec.T, epos.reshape(1, -1),
        epos.reshape(-1, 1), delay.reshape(-1, 1), drive.reshape(1, -1),
    )


def line_get(ref, f, yl):
    return jnp.concatenate([ref[0, :, xl, 2 * f + yl, :] for xl in range(4)], axis=0)


def mat_get(ref, f, yl):
    return jnp.concatenate(
        [ref[xl // 2, :, 0, 4 * (xl % 2) + 2 * f + yl, :] for xl in range(4)], axis=0
    )


def pair_get(ref, f, yl):
    return jnp.concatenate(
        [ref[0, :, xl // 2, 4 * (xl % 2) + 2 * f + yl, :] for xl in range(4)], axis=0
    )


def pair_put(ref, g, f, yl, v):
    n = v.shape[0] // 4
    for xl in range(4):
        ref[g, :, xl // 2, 4 * (xl % 2) + 2 * f + yl, :] = v[xl * n : (xl + 1) * n]


def forward_kernel(fields, mat, gm, tm, out, gx0, gx1):
    for yl in range(2):
        b = DT * mat_get(mat, 0, yl)
        bulk = DT * mat_get(mat, 1, yl)
        g0 = left(gm, line_get(fields, 0, yl))
        u1 = line_get(fields, 1, yl) - b * g0
        x0 = left(tm, u1)
        p1 = line_get(fields, 2, yl) + bulk * x0
        g1 = left(gm, p1)
        x1 = left(tm, u1 - b * g1)
        gx0[0, yl] = g0
        gx1[0, yl] = g1
        pair_put(out, 0, 0, yl, x0)
        pair_put(out, 0, 1, yl, x1)


def forward_call(buf, mats):
    _, ns, _, _, nz = buf.shape
    nx = 4 * ns
    line = pl.BlockSpec((1, 2, nx, nz), lambda g: (g, 0, 0, 0))
    return pl.pallas_call(
        forward_kernel,
        grid=(2,),
        in_specs=[pl.BlockSpec((1, ns, 4, 8, nz), lambda g: (g, 0, 0, 0, 0)),
                  pl.BlockSpec((2, ns, 1, 8, nz), lambda g: (0, 0, 4, 0, 0))]
        + [whole((nx, nx))] * 2,
        out_specs=[pl.BlockSpec((1, ns, 2, 8, nz), lambda g: (g, 0, 0, 0, 0)), line, line],
        out_shape=[jax.ShapeDtypeStruct((2, ns, 2, 8, nz), F32)]
        + [jax.ShapeDtypeStruct((2, 2, nx, nz), F32)] * 2,
        compiler_params=params(1),
        cost_estimate=pl.CostEstimate(flops=16 * 10**8, bytes_accessed=9 * 2**20, transcendentals=0),
        name="lines_forward",
    )(buf, buf, *mats)


def plane_get(ref, i, f, dst):
    half = dst.shape[0] // 2
    for xm in range(2):

        @pl.when(lax.rem(i, 2) == xm)
        def _():
            for yl in range(2):
                dst[yl * half : (yl + 1) * half, :] = ref[:, 0, 4 * xm + 2 * f + yl, :]


def middle_kernel(
    xs, c, rho, alpha, v0, u1y, u1z, yz0, gy0, gz0, pa, uya, uza, cnt, m0, m1, e1, gm, tm,
    buf, d0, w0, t1, t2, x0s, x1s,
):
    i = pl.program_id(0)
    half = c.shape[1] // 2
    plane_get(xs, i, 0, x0s)
    plane_get(xs, i, 1, x1s)
    x0, x1 = x0s[...], x1s[...]
    dens, speed = rho[0], c[0]
    b = 1.0 / dens
    dk = DT * (dens * speed * speed)
    keep = 1.0 - DT * alpha[0]
    p1 = v0[0] + dk * x0
    d0[0] = x0 + yz0[0]
    gy = left(gm, p1)
    gz = right(p1, tm)
    db = DT * b
    div1 = x1 + left(tm, u1y[0] - db * gy) + right(u1z[0] - db * gz, gm)
    p2 = keep * p1 + dk * div1 + e1[0]
    adj = pa[0] + (cnt[0] * p2 - m1[0])
    q = dk * adj
    ay = uya[0] + left(gm, q)
    az = uza[0] + right(q, tm)
    back = left(tm, b * ay) + right(b * az, gm)
    w = keep * adj - DT * back + (cnt[0] * p1 - m0[0])
    w0[0] = w
    t1[0] = div1 * adj
    t2[0] = (gy + gy0[0]) * ay + (gz + gz0[0]) * az
    for xm in range(2):

        @pl.when(lax.rem(i, 2) == xm)
        def _():
            for yl in range(2):
                rows = slice(yl * half, (yl + 1) * half)
                buf[:, 0, 4 * xm + yl, :] = q[rows]
                buf[:, 0, 4 * xm + 2 + yl, :] = w[rows]


def middle_call(xs, fields, pa, v, maps, mats):
    ndev, _, _, nz = xs.shape
    nx, ny, _ = fields[0].shape
    plane = pl.BlockSpec((1, ny, nz), lambda i: (i, 0, 0))
    pick = lambda i: i
    vec = group_plane(v.shape, pick)
    pair = pl.BlockSpec((ndev, 1, 8, nz), lambda i: (0, i // 2, 0, 0))
    nat = jax.ShapeDtypeStruct((nx, ny, nz), F32)
    return pl.pallas_call(
        middle_kernel,
        grid=(nx,),
        in_specs=[pair] + [plane] * len(fields) + [group_plane(pa.shape, pick)(0), vec(1), vec(2)]
        + [plane] * len(maps) + [whole((ny, ny))] * 2,
        out_specs=[pair] + [plane] * 4,
        out_shape=[jax.ShapeDtypeStruct(xs.shape, F32)] + [nat] * 4,
        scratch_shapes=[pltpu.VMEM((ny, nz), F32)] * 2,
        compiler_params=params(1),
        cost_estimate=pl.CostEstimate(flops=32 * 10**8, bytes_accessed=24 * 2**20, transcendentals=0),
        name="slab_middle",
    )(xs, *fields, pa, v, v, *maps, *mats)


def adjoint_kernel(qw, fields, mat, gx0, gx1, gm, tm, out, acc):
    g = pl.program_id(0)
    for yl in range(2):
        b = mat_get(mat, 0, yl)
        bulk = DT * mat_get(mat, 1, yl)
        ax = line_get(fields, 3, yl) + left(gm, pair_get(qw, 0, yl))
        back = left(tm, b * ax)
        q0 = bulk * (pair_get(qw, 1, yl) - DT * back)
        bx = gx1[0, yl] * ax + gx0[0, yl] * (ax + left(gm, q0))
        pair_put(out, g, 0, yl, back)

        @pl.when(g == 0)
        def _():
            acc[yl] = bx

        @pl.when(g == 1)
        def _():
            total = acc[yl] + bx
            pair_put(out, 0, 1, yl, total)
            pair_put(out, 1, 1, yl, total)


def adjoint_call(qw, buf, gx0, gx1, mats):
    _, ns, _, _, nz = buf.shape
    nx = 4 * ns
    line = pl.BlockSpec((1, 2, nx, nz), lambda g: (g, 0, 0, 0))
    return pl.pallas_call(
        adjoint_kernel,
        grid=(2,),
        in_specs=[pl.BlockSpec((1, ns, 2, 8, nz), lambda g: (g, 0, 0, 0, 0)),
                  pl.BlockSpec((1, ns, 4, 8, nz), lambda g: (g, 0, 0, 0, 0)),
                  pl.BlockSpec((2, ns, 1, 8, nz), lambda g: (0, 0, 4, 0, 0)), line, line]
        + [whole((nx, nx))] * 2,
        out_specs=whole((2, ns, 2, 8, nz)),
        out_shape=jax.ShapeDtypeStruct((2, ns, 2, 8, nz), F32),
        scratch_shapes=[pltpu.VMEM((2, nx, nz), F32)],
        compiler_params=params(1),
        cost_estimate=pl.CostEstimate(flops=12 * 10**8, bytes_accessed=11 * 2**20, transcendentals=0),
        name="lines_adjoint",
    )(qw, buf, buf, gx0, gx1, *mats)


def last_kernel(xs, c, rho, d0, w0, t1, t2, gy0, gz0, gm, tm, out, bx, xb):
    i = pl.program_id(0)
    plane_get(xs, i, 0, xb)
    plane_get(xs, i, 1, bx.at[0])
    p = w0[0] - DT * xb[...]
    q = (DT * (rho[0] * c[0] * c[0])) * p
    out[0, 0] = t1[0] + d0[0] * p
    out[1, 0] = t2[0] + gy0[0] * left(gm, q) + gz0[0] * right(q, tm)


def last_call(xs, fields, mats):
    ndev, _, _, nz = xs.shape
    nx, ny, _ = fields[0].shape
    plane = pl.BlockSpec((1, ny, nz), lambda i: (i, 0, 0))
    return pl.pallas_call(
        last_kernel,
        grid=(nx,),
        in_specs=[pl.BlockSpec((ndev, 1, 8, nz), lambda i: (0, i // 2, 0, 0))]
        + [plane] * len(fields) + [whole((ny, ny))] * 2,
        out_specs=[pl.BlockSpec((2, 1, ny, nz), lambda i: (0, i, 0, 0)), plane],
        out_shape=[jax.ShapeDtypeStruct((2, nx, ny, nz), F32), jax.ShapeDtypeStruct((nx, ny, nz), F32)],
        scratch_shapes=[pltpu.VMEM((ny, nz), F32)],
        compiler_params=params(1),
        cost_estimate=pl.CostEstimate(flops=8 * 10**8, bytes_accessed=13 * 2**20, transcendentals=0),
        name="slab_last",
    )(xs, *fields, *mats)


def change_layout(v):
    return lax.all_to_all(v, ALL, split_axis=0, concat_axis=0, tiled=True)


def local(
    sound_speed, density, absorption, pressure_start, velocity_start, adjoint_pressure,
    adjoint_velocity, emitter_voxel, emitter_delay, drive_waveform_samples, recorded_pressures,
    sensor_flat_position,
):
    n_emit, n_slab = lax.axis_size("emit"), lax.axis_size("slab")
    ndev = n_emit * n_slab
    planes, ny, nz = sound_speed.shape
    nx = planes * n_slab
    ids = jnp.stack([lax.axis_index("emit"), lax.axis_index("slab")]).astype(jnp.int32)
    mats = pair_const(deriv_matrix(ny))
    order = (4 * np.arange(n_slab)[None, :] + np.arange(4)[:, None]).reshape(-1)
    line_mats = pair_const(deriv_matrix(nx)[np.ix_(order, order)])
    epos, delay, drive = emitter_voxel[0], emitter_delay[0], drive_waveform_samples
    buf, u1y, u1z, yz0, gy0, gz0, v0 = start_call(
        ids, sound_speed, density, absorption, pressure_start, velocity_start, adjoint_velocity,
        epos, delay, drive, mats, ndev,
    )
    cnt, m0, m1, e1 = maps_call(
        ids, sensor_flat_position, recorded_pressures[0], epos, delay, drive, sound_speed.shape
    )
    lines = change_layout(buf).reshape(n_emit, n_slab, 5, 8, nz)
    xs, gx0, gx1 = forward_call(lines, line_mats)
    xs = change_layout(xs.reshape(ndev, 2, 8, nz))
    qw, d0, w0, t1, t2 = middle_call(
        xs,
        [sound_speed, density, absorption, v0, u1y, u1z, yz0, gy0, gz0],
        adjoint_pressure, adjoint_velocity, [cnt, m0, m1, e1], mats,
    )
    qw = change_layout(qw).reshape(n_emit, n_slab, 2, 8, nz)
    xs = adjoint_call(qw, lines, gx0, gx1, line_mats)
    xs = change_layout(xs.reshape(ndev, 2, 8, nz))
    t, bx = last_call(xs, [sound_speed, density, d0, w0, t1, t2, gy0, gz0], mats)
    other = lax.ppermute(t, "emit", [(0, 1), (1, 0)])
    s1 = t[0] + other[0]
    s2 = t[1] + other[1] + bx
    b = 1.0 / density
    speed_total = (2.0 * DT) * s1 * density * sound_speed
    density_total = DT * (s1 * sound_speed * sound_speed + s2 * b * b)
    return speed_total, density_total


def solution(mesh):
    in_specs = (
        P("slab", None, None), P("slab", None, None), P("slab", None, None),
        P("emit", "slab", None, None), P("emit", None, "slab", None, None),
        P("emit", "slab", None, None), P("emit", None, "slab", None, None),
        P("emit", None), P("emit", None), P(), P("emit", None, None), P(),
    )
    out_specs = (P("slab", None, None), P("slab", None, None))
    return jax.shard_map(local, mesh=mesh, in_specs=in_specs, out_specs=out_specs, check_vma=False)
```

time: 631 us -> 290 us (0.46); the launches traced: 620 us -> 289 us
  waiting for transfers between devices: 162 us -> 63.2 us
  local copies, waits for them, and re-layouts: 99.8 us -> 14.9 us
  matrix products: 71.9 us -> 0 us
  Pallas kernels: 0 us -> 51.4 us
  blocking collectives: 193 us -> 147 us
  starting transfers between devices: 43.3 us -> 8.62 us
  other arithmetic: 35.4 us -> 3.41 us
  between operations: 15 us -> 0.84 us
    all_to_all x7 -> x1, waiting for transfers between devices: 93.8 us -> 15.3 us  [change_layout(): return lax.all_to_all(v, ALL, split_axis=0, concat_axis=0, tiled=True)]
    dot_general x23 -> x0, matrix products: 71.9 us -> none  [the longest x7 30.2 us: along_second(): jnp.einsum('ij,ajc->aic', matrix, volume, precision=lax.Precision.HIGHEST)]
    psum x1 -> x0, waiting for transfers between devices: 68.5 us -> none  [local(): speed_total, density_total = lax.psum((speed_part, density_part), 'emit')]
    pallas_call x0 -> x6, Pallas kernels: none -> 51.4 us  [the longest x1 12.6 us: middle_call(): pl.pallas_call(middle_kernel, grid=(nx,), in_specs=[pair] + [plane] * len...]
    ppermute x0 -> x1, waiting for transfers between devices: none -> 48 us  [local(): other = lax.ppermute(t, 'emit', [(0, 1), (1, 0)])]
    all_to_all x7 -> x3, blocking collectives: 193 us -> 147 us  [change_layout(): return lax.all_to_all(v, ALL, split_axis=0, concat_axis=0, tiled=True)]
    all_to_all x7 -> x1, starting transfers between devices: 42.9 us -> 7.99 us  [change_layout(): return lax.all_to_all(v, ALL, split_axis=0, concat_axis=0, tiled=True)]
    scatter-add x4 -> x0, other arithmetic: 25.1 us -> none  [the longest x2 19.7 us: local(): adj_p.reshape(-1).at[recv_index].add(residuals[loop_tally])]
  transfers between devices with their start and end apart: 8 -> 2, of which waited for: 8 -> 2; matrix products, arithmetic and copies ran while one was open for 7% -> 1% of each run, Pallas kernels for 0% -> 2%
where the time goes in v1:
time: 290 us; the launch traced here: 289 us
  blocking collectives  147 us (51%)
  waiting for transfers between devices  63.2 us (22%)
  Pallas kernels  51.4 us (18%)
  local copies, waits for them, and re-layouts  14.9 us (5%)
  starting transfers between devices  8.62 us (3%)
  other arithmetic  3.41 us (1%)
    all_to_all x3, blocking collectives, change_layout(): return lax.all_to_all(v, ALL, split_axis=0, concat_axis=0, tiled=True)  147 us
    ppermute x1, waiting for transfers between devices, local(): other = lax.ppermute(t, 'emit', [(0, 1), (1, 0)])  48 us
    all_to_all x1, waiting for transfers between devices, change_layout(): return lax.all_to_all(v, ALL, split_axis=0, concat_axis=0, tiled=True)  15.3 us
    pallas_call x1, Pallas kernels, middle_call(): pl.pallas_call(middle_kernel, grid=(nx,), in_specs=[pair] + [plane] * len...  12.6 us
    unnamed x59, local copies, waits for them, and re-layouts  12.2 us
    pallas_call x1, Pallas kernels, start_call(): pl.pallas_call(start_kernel, grid=(5,), in_specs=[smem()] + [plane] * 3 +...  9.27 us
    pallas_call x1, Pallas kernels, forward_call(): pl.pallas_call(forward_kernel, grid=(2,), in_specs=[pl.BlockSpec((1, ns,...  8.71 us
    pallas_call x1, Pallas kernels, adjoint_call(): pl.pallas_call(adjoint_kernel, grid=(2,), in_specs=[pl.BlockSpec((1, ns,...  8.03 us
  transfers between devices with their start and end apart: 2, of which 2 were waited for; matrix products, arithmetic and copies ran while one was open for 1% of the time, Pallas kernels for 2%

profile of v1, /device:TPU:0, one launch (start us, length us, event | category | flops | bytes accessed | tf_op | source)
XLA Modules:
  0.0 288.9 jit_solution(17821562539922294498)
XLA Ops:
  0.6 0.8 copy.20.delay
  1.4 0.8 copy.19.epos_col
  2.3 0.1 pad_add_fusion.ids
  2.3 0.9 copy-done.4
  3.3 0.9 copy-done.6
  4.3 0.7 copy-done.24
  4.9 0.7 copy-done.26
  5.6 9.3 %start.1 = (f32[128,5,8,256]{3,2,1,0:T(8,128)}, f32[4,256,256]{2,1,0:T(8,128)S(1)}, f32[4,256,256]{2,1,0:T(8,128)S(1)}, f32[4,256,256]{2,1,0:T(8,128)S(1)}, f32[...) custom-call(s32[2]{0:T(128)S(1)} %pad_add_fusion.ids, f32[4,256,256]{2,1,0:T(8,128)} %c.5, ...), custom_call_target="tpu_custom_call" | custom-call | flops 2000000000 | bytes 19922944 | tf_op jit(solution)/shard_map/start/pallas_call | solution.py:155
  14.9 0.0 copy-start.9
  14.9 75.2 %all_to_all.20 = f32[128,5,8,256]{3,2,1,0:T(8,128)} all-to-all(f32[128,5,8,256]{3,2,1,0:T(8,128)} %get-tuple-element.23), channel_id=1, replica_groups=mesh['emit'=2,'slab'=64] {'emit','slab'}, dimensions={0} | all-to-all | bytes 10485760 | tf_op jit(solution)/shard_map/all_to_all | solution.py:417
  90.2 8.7 %lines_forward.1 = (f32[2,64,2,8,256]{4,3,2,1,0:T(8,128)}, f32[2,2,256,256]{3,2,1,0:T(8,128)S(1)}, f32[2,2,256,256]{3,2,1,0:T(8,128)S(1)}) custom-call(f32[2,64,5,8,256]{4,3,2,1,0:T(8,128)} %bitcast.33, f32[2,64,5,8,256]{4,3,2,1,0:T(8,128)} %bitcast.34, f32[256,256]{1,0:T(8,128)S(1)} %copy-done.9, f32[256,256]{1,0:T(8,128)S(1)} %copy-done.8), custom_call_target="tpu_custom_call" | custom-call | flops 1600000000 | bytes 9437184 | tf_op jit(solution)/shard_map/lines_forward/pallas_call | solution.py:260
  99.0 1.0 copy-done.10
  99.9 8.0 %all-to-all-start.1 = ((f32[128,2,8,256]{3,2,1,0:T(8,128)}), f32[128,2,8,256]{3,2,1,0:T(8,128)}, u32[]{:S(2)}, u32[]{:S(2)}) async-start(f32[128,2,8,256]{3,2,1,0:T(8,128)} %bitcast.6), calls=%async_computation.1 | async-start | bytes 4194304 | tf_op jit(solution)/shard_map/all_to_all | solution.py:417
  108.0 1.0 copy.21
  109.0 1.0 copy.22.spos_col
  110.0 1.0 copy-done.21
  111.1 1.0 copy-done.22
  112.1 6.6 %maps.1 = (f32[4,256,256]{2,1,0:T(8,128)S(1)}, f32[4,256,256]{2,1,0:T(8,128)S(1)}, f32[4,256,256]{2,1,0:T(8,128)S(1)}, f32[4,256,256]{2,1,0:T(8,128)S(1)}) custom-call(s32[2]{0:T(128)S(1)} %pad_add_fusion.ids, s32[1,1024]{1,0:T(1,128)S(1)} %bitcast.29, s32[1024,1]{1,0:T(8,128)S(1)} %copy-done.22, f32[1024,2]{1,0:T(8,128)S(1)} %bitcast.27, ...), custom_call_target="tpu_custom_call" | custom-call | flops 4000000000 | bytes 5242880 | tf_op jit(solution)/shard_map/maps/pallas_call | solution.py:201
  118.8 1.0 copy-done.15
  119.7 1.0 copy-done.16
  120.7 1.0 copy-done.17
  121.7 1.0 copy-done.18
  122.6 15.3 %all-to-all-done.1.xs = f32[128,2,8,256]{3,2,1,0:T(8,128)} async-done(((f32[128,2,8,256]{3,2,1,0:T(8,128)}), f32[128,2,8,256]{3,2,1,0:T(8,128)}, u32[]{:S(2)}, u32[]{:S(2)}) %all-to-all-start.1) | async-done | bytes 2097184 | tf_op jit(solution)/shard_map/all_to_all | solution.py:417
  137.9 12.6 %slab_middle.1 = (f32[128,2,8,256]{3,2,1,0:T(8,128)}, f32[4,256,256]{2,1,0:T(8,128)S(1)}, f32[4,256,256]{2,1,0:T(8,128)S(1)}, f32[4,256,256]{2,1,0:T(8,128)S(1)}, f32[4,256,256]{2,1,0:T(8,128)S(1)}) custom-call(f32[128,2,8,256]{3,2,1,0:T(8,128)} %all-to-all-done.1.xs, f32[4,256,256]{2,1,0:T(8,128)S(1)} %copy-done, f32[4,256,256]{2,1,0:T(8,128)} %rho.5, ...), custom_call_target="tpu_custom_call" | custom-call | flops 3200000000 | bytes 25165824 | tf_op jit(solution)/shard_map/slab_middle/pallas_call | solution.py:332
  150.5 1.0 copy-done.19
  151.5 36.1 %all_to_all.21 = f32[128,2,8,256]{3,2,1,0:T(8,128)} all-to-all(f32[128,2,8,256]{3,2,1,0:T(8,128)} %get-tuple-element.35), channel_id=1, replica_groups=mesh['emit'=2,'slab'=64] {'emit','slab'}, dimensions={0} | all-to-all | bytes 4194304 | tf_op jit(solution)/shard_map/all_to_all | solution.py:417
  187.6 8.0 %lines_adjoint.1 = f32[2,64,2,8,256]{4,3,2,1,0:T(8,128)S(1)} custom-call(f32[2,64,2,8,256]{4,3,2,1,0:T(8,128)} %bitcast.37, f32[2,64,5,8,256]{4,3,2,1,0:T(8,128)} %bitcast.35, f32[2,64,5,8,256]{4,3,2,1,0:T(8,128)} %bitcast.36, f32[2,2,256,256]{3,2,1,0:T(8,128)S(1)} %get-tuple-element.36.gx0, f32[2,2,256,256]{3,2,1,0:T(8,128)S(1)} %copy-done.11, ...), custom_call_target="tpu_custom_call" | custom-call | flops 1200000000 | bytes 11534336 | tf_op jit(solution)/shard_map/lines_adjoint/pallas_call | solution.py:372
  195.6 35.2 %all_to_all.22.xs = f32[128,2,8,256]{3,2,1,0:T(8,128)} all-to-all(f32[128,2,8,256]{3,2,1,0:T(8,128)S(1)} %bitcast.26), channel_id=1, replica_groups=mesh['emit'=2,'slab'=64] {'emit','slab'}, dimensions={0} | all-to-all | bytes 4194304 | tf_op jit(solution)/shard_map/all_to_all | solution.py:417
  230.8 6.2 %slab_last.1 = (f32[2,4,256,256]{3,2,1,0:T(8,128)}, f32[4,256,256]{2,1,0:T(8,128)S(1)}) custom-call(f32[128,2,8,256]{3,2,1,0:T(8,128)} %all_to_all.22.xs, f32[4,256,256]{2,1,0:T(8,128)S(1)} %copy-done, f32[4,256,256]{2,1,0:T(8,128)S(1)} %copy-done.1, f32[4,256,256]{2,1,0:T(8,128)S(1)} %get-tuple-element.38.d0, f32[4,256,256]{2,1,0:T(8,128)S(1)} %get-tuple-element.39.w0, ...), custom_call_target="tpu_custom_call" | custom-call | flops 800000000 | bytes 13631488 | tf_op jit(solution)/shard_map/slab_last/pallas_call | solution.py:402
  237.0 0.6 collective-permute-start
  237.6 48.0 %collective-permute-done = f32[2,4,256,256]{3,2,1,0:T(8,128)S(1)} collective-permute-done((f32[2,4,256,256]{3,2,1,0:T(8,128)}, f32[2,4,256,256]{3,2,1,0:T(8,128)S(1)}, u32[]{:S(2)}, u32[]{:S(2)}) %collective-permute-start) | collective-permute-done | bytes 2097184 | tf_op jit(solution)/shard_map/ppermute | solution.py:453
  285.6 3.3 %fusion.1 = (f32[4,256,256]{2,1,0:T(8,128)}, f32[4,256,256]{2,1,0:T(8,128)}) fusion(f32[4,256,256]{2,1,0:T(8,128)S(1)} %copy-done, f32[4,256,256]{2,1,0:T(8,128)S(1)} %get-tuple-element.43, f32[2,4,256,256]{3,2,1,0:T(8,128)S(1)} %collective-permute-done, f32[4,256,256]{2,1,0:T(8,128)S(1)} %copy-done.1, f32[2,4,256,256]{3,2,1,0:T(8,128)} %get-tuple-element.42), kind=kLoop, calls=%fused_computation.3 | loop fusion | flops 3407872 | bytes 9437184 | tf_op jit(solution)/shard_map/mul | solution.py:458
  (45 shorter events, 0.1 us)
Async XLA Ops:
  2.3 1.0 copy-start.4
  3.3 0.9 copy-start.6
  4.2 0.7 copy-start.24
  4.9 0.7 copy-start.26
  14.9 75.3 %copy-start.2 = (f32[4,256,256]{2,1,0:T(8,128)}, f32[4,256,256]{2,1,0:T(8,128)S(1)}, u32[]{:S(2)}) copy-start(f32[4,256,256]{2,1,0:T(8,128)S(1)} %get-tuple-element.29.gy0) | copy-start | bytes 3145732
  14.9 75.3 %copy-start.3 = (f32[4,256,256]{2,1,0:T(8,128)}, f32[4,256,256]{2,1,0:T(8,128)S(1)}, u32[]{:S(2)}) copy-start(f32[4,256,256]{2,1,0:T(8,128)S(1)} %get-tuple-element.30.gz0) | copy-start | bytes 3145732
  14.9 75.3 %copy-start.12 = (f32[4,256,256]{2,1,0:T(8,128)}, f32[4,256,256]{2,1,0:T(8,128)S(1)}, u32[]{:S(2)}) copy-start(f32[4,256,256]{2,1,0:T(8,128)S(1)} %get-tuple-element.26.u1y) | copy-start | bytes 3145732
  14.9 75.3 %copy-start.13 = (f32[4,256,256]{2,1,0:T(8,128)}, f32[4,256,256]{2,1,0:T(8,128)S(1)}, u32[]{:S(2)}) copy-start(f32[4,256,256]{2,1,0:T(8,128)S(1)} %get-tuple-element.27.u1z) | copy-start | bytes 3145732
  14.9 75.3 %copy-start.14 = (f32[4,256,256]{2,1,0:T(8,128)}, f32[4,256,256]{2,1,0:T(8,128)S(1)}, u32[]{:S(2)}) copy-start(f32[4,256,256]{2,1,0:T(8,128)S(1)} %get-tuple-element.28.yz0) | copy-start | bytes 3145732
  14.9 75.3 %copy-start.8 = (f32[256,256]{1,0:T(8,128)S(1)}, f32[256,256]{1,0:T(8,128)}, u32[]{:S(2)}) copy-start(f32[256,256]{1,0:T(8,128)} %constant.26.clone.tm) | copy-start | bytes 786436
  14.9 75.3 %copy-start.9 = (f32[256,256]{1,0:T(8,128)S(1)}, f32[256,256]{1,0:T(8,128)}, u32[]{:S(2)}) copy-start(f32[256,256]{1,0:T(8,128)} %constant.25.clone.gm) | copy-start | bytes 786436
  99.0 1.0 copy-start.10
  99.9 8.0 %copy-start.28 = (f32[1,2,1024]{2,1,0:T(2,128)S(1)}, f32[1,2,1024]{2,1,0:T(2,128)}, u32[]{:S(2)}) copy-start(f32[1,2,1024]{2,1,0:T(2,128)} %param.26) | copy-start | bytes 24580
  99.9 9.0 %copy-start.23 = (s32[1024]{0:T(1024)S(1)}, s32[1024]{0:T(1024)}, u32[]{:S(2)}) copy-start(s32[1024]{0:T(1024)} %param.27) | copy-start | bytes 12292
  99.9 10.1 %copy-start.25 = (s32[1,256]{1,0:T(1,128)S(1)}, s32[1,256]{1,0:T(1,128)}, u32[]{:S(2)}) copy-start(s32[1,256]{1,0:T(1,128)} %epos_row.3) | copy-start | bytes 3076
  99.9 10.1 %copy-start.27 = (f32[64]{0:T(128)S(1)}, f32[64]{0:T(128)}, u32[]{:S(2)}) copy-start(f32[64]{0:T(128)} %param.25) | copy-start | bytes 772
  99.9 38.0 %all-to-all-start.1 = ((f32[128,2,8,256]{3,2,1,0:T(8,128)}), f32[128,2,8,256]{3,2,1,0:T(8,128)}, u32[]{:S(2)}, u32[]{:S(2)}) async-start(f32[128,2,8,256]{3,2,1,0:T(8,128)} %bitcast.6), calls=%async_computation.1 | async-start | bytes 4194304 | tf_op jit(solution)/shard_map/all_to_all | solution.py:417
  110.0 1.0 copy-start.21
  111.1 1.0 copy-start.22
  112.1 25.8 %copy-start = (f32[4,256,256]{2,1,0:T(8,128)S(1)}, f32[4,256,256]{2,1,0:T(8,128)}, u32[]{:S(2)}) copy-start(f32[4,256,256]{2,1,0:T(8,128)} %c.5) | copy-start | bytes 3145732
  112.1 25.8 %copy-start.5 = (f32[256,256]{1,0:T(8,128)S(1)}, f32[256,256]{1,0:T(8,128)}, u32[]{:S(2)}) copy-start(f32[256,256]{1,0:T(8,128)} %constant.24.clone.tm) | copy-start | bytes 786436
  112.1 25.8 %copy-start.7 = (f32[256,256]{1,0:T(8,128)S(1)}, f32[256,256]{1,0:T(8,128)}, u32[]{:S(2)}) copy-start(f32[256,256]{1,0:T(8,128)} %constant.23.clone.gm) | copy-start | bytes 786436
  118.7 1.0 copy-start.15
  119.7 1.0 copy-start.16
  120.7 1.0 copy-start.17
  121.7 1.0 copy-start.18
  150.5 1.0 copy-start.19
  151.5 36.1 %copy-start.20 = (f32[4,256,256]{2,1,0:T(8,128)}, f32[4,256,256]{2,1,0:T(8,128)S(1)}, u32[]{:S(2)}) copy-start(f32[4,256,256]{2,1,0:T(8,128)S(1)} %get-tuple-element.41.t2) | copy-start | bytes 3145732
  151.5 36.1 %copy-start.11 = (f32[2,2,256,256]{3,2,1,0:T(8,128)S(1)}, f32[2,2,256,256]{3,2,1,0:T(8,128)}, u32[]{:S(2)}) copy-start(f32[2,2,256,256]{3,2,1,0:T(8,128)} %copy-done.10) | copy-start | bytes 3145732
  195.6 35.2 %copy-start.1 = (f32[4,256,256]{2,1,0:T(8,128)S(1)}, f32[4,256,256]{2,1,0:T(8,128)}, u32[]{:S(2)}) copy-start(f32[4,256,256]{2,1,0:T(8,128)} %rho.5) | copy-start | bytes 3145732
  237.0 48.6 %collective-permute-start = (f32[2,4,256,256]{3,2,1,0:T(8,128)}, f32[2,4,256,256]{3,2,1,0:T(8,128)S(1)}, u32[]{:S(2)}, u32[]{:S(2)}) collective-permute-start(f32[2,4,256,256]{3,2,1,0:T(8,128)} %get-tuple-element.42), channel_id=1, source_target_pairs={{0,64},{64,0},{1,65},{65,1},{2,66},{66,2},{3,67},{67,3},{4,68},{68... | collective-permute-start | bytes 6291464 | tf_op jit(solution)/shard_map/ppermute | solution.py:453

commit v2 on v1

v2 whole, which is shorter than its diff:
```python
import numpy as np
import jax
import jax.numpy as jnp
from jax import lax
from jax.experimental import pallas as pl
from jax.experimental.pallas import tpu as pltpu
from jax.sharding import PartitionSpec as P

STEPS = 2
DT = 0.2
F32 = jnp.float32
BF16 = jnp.bfloat16
ALL = ("emit", "slab")
MIB = 2**20


def deriv_matrix(n):
    k = np.arange(1, n // 2, dtype=np.int64)
    pts = np.arange(n, dtype=np.int64)
    shifted = (k[None, :] * (2 * pts[:, None] + 1)) % (2 * n) * (np.pi / n)
    plain = (k[None, :] * (2 * pts[:, None])) % (2 * n) * (np.pi / n)
    w = k * (2.0 * np.pi / n)
    m = (np.cos(shifted) * w) @ np.sin(plain).T - (np.sin(shifted) * w) @ np.cos(plain).T
    return m * (2.0 / n)


def pair_const(m):
    m = m.astype(np.float32)
    return [jnp.asarray(m), jnp.asarray(np.ascontiguousarray(m.T))]


def split2(v):
    hi = v.astype(BF16)
    return hi, (v - hi.astype(F32)).astype(BF16)


def split3(v):
    hi = v.astype(BF16)
    rest = v - hi.astype(F32)
    mid = rest.astype(BF16)
    return hi, mid, (rest - mid.astype(F32)).astype(BF16)


def dot(a, b):
    return jnp.dot(a, b, preferred_element_type=F32)


def left(m, v):
    mh, ml = split2(m[...])
    h, l = split2(v)
    return dot(mh, h) + (dot(mh, l) + dot(ml, h))


def right(v, m):
    mh, ml = split2(m[...])
    h, l = split2(v)
    return dot(h, mh) + (dot(l, mh) + dot(h, ml))


def params(mib):
    return pltpu.CompilerParams(
        dimension_semantics=("arbitrary",), vmem_limit_bytes=mib * MIB
    )


def cost(mflop, mib):
    return pl.CostEstimate(flops=mflop * 10**6, bytes_accessed=mib * MIB, transcendentals=0)


def swap(v):
    return jnp.swapaxes(v, 0, 1)


def whole(shape):
    return pl.BlockSpec(shape, lambda i, ids: (0,) * len(shape))


def group_plane(shape, pick, a=0):
    block = (None,) * (len(shape) - 3) + (1,) + shape[-2:]
    return pl.BlockSpec(block, lambda i, ids: (0, a)[: len(shape) - 3] + (pick(i, ids), 0, 0))


def plane_onehot(pos, plane, ny, nz):
    local = pos - plane * (ny * nz)
    y = lax.broadcasted_iota(jnp.int32, (ny, pos.shape[1]), 0) * nz
    return jnp.where((local >= y) & (local < y + nz), 1.0, 0.0).astype(BF16)


def column_onehot(pos, nz):
    z = lax.broadcasted_iota(jnp.int32, (nz, pos.shape[1]), 0)
    return lax.rem(pos, nz) == z


def drive_at(delay, drive, step):
    amp = jnp.zeros(delay.shape, F32)
    for k in range(drive.shape[0]):
        amp = jnp.where(delay + step == k, drive[k], amp)
    return amp


def three(onehot, value):
    return jnp.concatenate(
        [jnp.where(onehot, v.astype(F32), 0.0).astype(BF16) for v in split3(value)], axis=0
    )


def spread(rows, cols):
    return lax.dot_general(rows, cols, (((1,), (1,)), ((), ())), preferred_element_type=F32)


def sum3(v):
    n = v.shape[1] // 3
    return v[:, :n] + v[:, n : 2 * n] + v[:, 2 * n :]


def start_kernel(
    ids, drive, c, rho, alpha, p0, ux, uy, uz, vx, epos, delay, gm, tm,
    buf, u1y, u1z, yz0, gy0, gz0, v0, mat, cols, pack,
):
    i = pl.program_id(0)
    ny, nz = p0.shape[1], p0.shape[2]
    half = ny // 2

    @pl.when(i == 0)
    def _():
        cols[...] = three(column_onehot(epos[...], nz), drive_at(delay[...], drive, 0))

    @pl.when(i < 4)
    def _():
        dens, speed, p = rho[0], c[0], p0[0]
        b = 1.0 / dens
        bulk = dens * speed * speed
        gy = left(gm, p)
        gz = right(p, tm)
        wy = uy[0] - DT * b * gy
        wz = uz[0] - DT * b * gz
        yz = left(tm, wy) + right(wz, gm)
        shot = sum3(spread(plane_onehot(epos[...], ids[1] * 4 + i, ny, nz), cols[...]))
        v = (1.0 - DT * alpha[0]) * p + (DT * bulk) * yz + shot
        u1y[0], u1z[0], yz0[0], gy0[0], gz0[0], v0[0] = wy, wz, yz, gy, gz, v
        for f, field in enumerate((p, ux[0], v, vx[0])):
            pack[2 * f : 2 * f + 2] = field.reshape(2, half, nz)
        buf[:, 0] = swap(pack[...])
        for xm in range(2):

            @pl.when(i == 2 * ids[0] + xm)
            def _():
                mat[4 * xm : 4 * xm + 2] = b.reshape(2, half, nz)
                mat[4 * xm + 2 : 4 * xm + 4] = bulk.reshape(2, half, nz)

    @pl.when(i == 4)
    def _():
        buf[:, 0] = swap(mat[...])


def start_call(ids, c, rho, alpha, p0, u, v, epos, delay, drive, mats, ndev):
    nx, ny, nz = c.shape
    pick = lambda i, ids: jnp.minimum(i, nx - 1)
    plane = group_plane(c.shape, pick)
    n_e = epos.shape[1]
    nat = jax.ShapeDtypeStruct(c.shape, F32)
    return pl.pallas_call(
        start_kernel,
        grid_spec=pltpu.PrefetchScalarGridSpec(
            num_scalar_prefetch=1,
            grid=(nx + 1,),
            in_specs=[pl.BlockSpec(memory_space=pltpu.SMEM)] + [plane] * 3
            + [group_plane(p0.shape, pick)]
            + [group_plane(u.shape, pick, a) for a in (0, 1, 2, 0)]
            + [whole((1, n_e))] * 2 + [whole((ny, ny))] * 2,
            out_specs=[pl.BlockSpec((ndev, 1, 8, nz), lambda i, ids: (0, i, 0, 0))] + [plane] * 6,
            scratch_shapes=[pltpu.VMEM((8, ndev, nz), F32), pltpu.VMEM((3 * nz, n_e), BF16),
                            pltpu.VMEM((8, ndev, nz), F32)],
        ),
        out_shape=[jax.ShapeDtypeStruct((ndev, 5, 8, nz), F32)] + [nat] * 6,
        compiler_params=params(60),
        cost_estimate=cost(2000, 19),
        name="start",
    )(ids, drive, c, rho, alpha, p0, u, u, u, v, epos, delay, *mats)


def maps_kernel(ids, drive, spos, rec, epos, delay, cnt, d0, d1, e1, scols, ecols):
    i = pl.program_id(0)
    ny, nz = cnt.shape[1], cnt.shape[2]

    @pl.when(i == 0)
    def _():
        oh = column_onehot(spos[...], nz)
        scols[:nz] = jnp.where(oh, 1.0, 0.0).astype(BF16)
        scols[nz : 4 * nz] = three(oh, rec[0:1])
        scols[4 * nz :] = three(oh, rec[1:2])
        ecols[...] = three(column_onehot(epos[...], nz), drive_at(delay[...], drive, 1))

    plane = ids[1] * 4 + i
    s = plane_onehot(spos[...], plane, ny, nz)
    cnt[0] = spread(s, scols[:nz])
    d0[0] = sum3(spread(s, scols[nz : 4 * nz]))
    d1[0] = sum3(spread(s, scols[4 * nz :]))
    e1[0] = sum3(spread(plane_onehot(epos[...], plane, ny, nz), ecols[...]))


def maps_call(ids, spos, rec, epos, delay, drive, shape):
    nx, ny, nz = shape
    n_e, n_s = epos.shape[1], spos.shape[1]
    return pl.pallas_call(
        maps_kernel,
        grid_spec=pltpu.PrefetchScalarGridSpec(
            num_scalar_prefetch=1,
            grid=(nx,),
            in_specs=[pl.BlockSpec(memory_space=pltpu.SMEM), whole((1, n_s)),
                      pl.BlockSpec((None, STEPS, n_s), lambda i, ids: (0, 0, 0)),
                      whole((1, n_e)), whole((1, n_e))],
            out_specs=[group_plane(shape, lambda i, ids: i)] * 4,
            scratch_shapes=[pltpu.VMEM((7 * nz, n_s), BF16), pltpu.VMEM((3 * nz, n_e), BF16)],
        ),
        out_shape=[jax.ShapeDtypeStruct(shape, F32)] * 4,
        compiler_params=params(32),
        cost_estimate=cost(4000, 5),
        name="maps",
    )(ids, drive, spos, rec, epos, delay)


def unpack(block, dst, first):
    t = swap(block)
    n = t.shape[1]
    for xm in range(2):
        dst[:, (first + xm) * n : (first + xm + 1) * n, :] = t[4 * xm : 4 * xm + 4]


def forward_kernel(ids, fields, mat, gm, tm, out, gx0, gx1, ax, bk, f_s, o_s):
    n = fields.shape[1]

    @pl.when(pl.program_id(0) == 0)
    def _():
        for e in range(2):
            unpack(mat[e, :, 0], bk, 2 * e)

    for xl in range(4):
        f_s[:, xl * n : (xl + 1) * n, :] = swap(fields[0, :, xl])
    for yl in range(2):
        b = DT * bk[yl]
        bulk = DT * bk[2 + yl]
        g0 = left(gm, f_s[yl])
        u1 = f_s[2 + yl] - b * g0
        x0 = left(tm, u1)
        p1 = f_s[4 + yl] + bulk * x0
        g1 = left(gm, p1)
        gx0[0, yl] = g0
        gx1[0, yl] = g1
        ax[0, yl] = f_s[6 + yl]
        o_s[yl] = x0
        o_s[2 + yl] = left(tm, u1 - b * g1)
    for h in range(2):
        both = [o_s[:, (2 * h + xm) * n : (2 * h + xm + 1) * n, :] for xm in range(2)]
        out[0, :, h] = swap(jnp.concatenate(both, axis=0))


def forward_call(ids, buf, mats):
    _, ns, _, _, nz = buf.shape
    nx = 4 * ns
    line = pl.BlockSpec((1, 2, nx, nz), lambda g, ids: (g, 0, 0, 0))
    full = jax.ShapeDtypeStruct((2, 2, nx, nz), F32)
    return pl.pallas_call(
        forward_kernel,
        grid_spec=pltpu.PrefetchScalarGridSpec(
            num_scalar_prefetch=1,
            grid=(2,),
            in_specs=[pl.BlockSpec((1, ns, 4, 8, nz), lambda g, ids: (g, 0, 0, 0, 0)),
                      pl.BlockSpec((2, ns, 1, 8, nz), lambda g, ids: (0, 0, 4, 0, 0))]
            + [whole((nx, nx))] * 2,
            out_specs=[pl.BlockSpec((1, ns, 2, 8, nz), lambda g, ids: (g, 0, 0, 0, 0)),
                       line, line, line, whole((4, nx, nz))],
            scratch_shapes=[pltpu.VMEM((8, nx, nz), F32), pltpu.VMEM((4, nx, nz), F32)],
        ),
        out_shape=[jax.ShapeDtypeStruct((2, ns, 2, 8, nz), F32), full, full, full,
                   jax.ShapeDtypeStruct((4, nx, nz), F32)],
        compiler_params=params(36),
        cost_estimate=cost(1600, 11),
        name="lines_forward",
    )(ids, buf, buf, *mats)


def middle_kernel(
    ids, xs, c, rho, alpha, v0, u1y, u1z, yz0, gy0, gz0, pa, uya, uza, cnt, m0, m1, e1, gm, tm,
    buf, send, keep, x_s, o_s,
):
    i = pl.program_id(0)
    xm = lax.rem(i, 2)
    ny, nz = c.shape[1], c.shape[2]
    half = ny // 2

    @pl.when(xm == 0)
    def _():
        x_s[...] = swap(xs[:, 0]).reshape(4, ny, nz)

    x0, x1 = x_s[2 * xm], x_s[2 * xm + 1]
    dens, speed = rho[0], c[0]
    b = 1.0 / dens
    dk = DT * (dens * speed * speed)
    stay = 1.0 - DT * alpha[0]
    p1 = v0[0] + dk * x0
    gy = left(gm, p1)
    gz = right(p1, tm)
    db = DT * b
    div1 = x1 + left(tm, u1y[0] - db * gy) + right(u1z[0] - db * gz, gm)
    p2 = stay * p1 + dk * div1 + e1[0]
    adj = pa[0] + (cnt[0] * p2 - m1[0])
    q = dk * adj
    ay = uya[0] + left(gm, q)
    az = uza[0] + right(q, tm)
    back = left(tm, b * ay) + right(b * az, gm)
    o_s[2 * xm] = q
    o_s[2 * xm + 1] = stay * adj - DT * back + (cnt[0] * p1 - m0[0])
    d0 = x0 + yz0[0]
    t1 = div1 * adj
    t2 = (gy + gy0[0]) * ay + (gz + gz0[0]) * az

    @pl.when(i < 2)
    def _():
        send[0, 0], send[0, 1], send[0, 2] = d0, t1, t2

    @pl.when(i >= 2)
    def _():
        keep[0, 0], keep[0, 1], keep[0, 2] = d0, t1, t2

    @pl.when(xm == 1)
    def _():
        buf[:, 0] = swap(o_s[...].reshape(8, half, nz))


def middle_call(ids, xs, fields, pa, v, maps, mats):
    ndev, _, _, nz = xs.shape
    nx, ny, _ = fields[0].shape
    pick = lambda i, ids: lax.rem(i + 2 * (1 - ids[0]), nx)
    plane = group_plane(fields[0].shape, pick)
    pair = pl.BlockSpec((ndev, 1, 8, nz), lambda i, ids: (0, pick(i, ids) // 2, 0, 0))
    three_fields = lambda f: pl.BlockSpec((1, 3, ny, nz), lambda i, ids: (f(i), 0, 0, 0))
    part = jax.ShapeDtypeStruct((2, 3, ny, nz), F32)
    return pl.pallas_call(
        middle_kernel,
        grid_spec=pltpu.PrefetchScalarGridSpec(
            num_scalar_prefetch=1,
            grid=(nx,),
            in_specs=[pair] + [plane] * len(fields) + [group_plane(pa.shape, pick)]
            + [group_plane(v.shape, pick, a) for a in (1, 2)]
            + [plane] * len(maps) + [whole((ny, ny))] * 2,
            out_specs=[pair, three_fields(lambda i: jnp.minimum(i, 1)),
                       three_fields(lambda i: jnp.maximum(i - 2, 0))],
            scratch_shapes=[pltpu.VMEM((4, ny, nz), F32)] * 2,
        ),
        out_shape=[jax.ShapeDtypeStruct(xs.shape, F32), part, part],
        compiler_params=params(36),
        cost_estimate=cost(3200, 24),
        name="slab_middle",
    )(ids, xs, *fields, pa, v, v, *maps, *mats)


def adjoint_kernel(ids, qw, ux, bk, gx0, gx1, gm, tm, out, f_s, p_s, bx_s):
    g = pl.program_id(0)
    n = qw.shape[1]
    nz = qw.shape[4]
    for h in range(2):
        unpack(qw[0, :, h], f_s, 2 * h)
    for yl in range(2):
        ax = ux[0, yl] + left(gm, f_s[yl])
        p0 = f_s[2 + yl] - DT * left(tm, bk[yl] * ax)
        p_s[2 * g + yl] = p0
        bx = gx1[0, yl] * ax + gx0[0, yl] * (ax + left(gm, (DT * bk[2 + yl]) * p0))

        @pl.when(g == 0)
        def _():
            bx_s[yl] = bx

        @pl.when(g == 1)
        def _():
            bx_s[yl] += bx

    @pl.when(g == 1)
    def _():
        lanes = [slice(z, z + nz // 2) for z in (0, nz // 2)]
        for e in range(2):
            rows = [slice((2 * e + xm) * n, (2 * e + xm + 1) * n) for xm in range(2)]
            for zh, z in enumerate(lanes):
                v = [p_s[2 * gr : 2 * gr + 2, x, z] for gr in range(2) for x in rows]
                out[e, :, 8 * zh : 8 * zh + 8, :] = swap(jnp.concatenate(v, axis=0))
            v = [bx_s[:, x, z] for z in lanes for x in rows]
            out[e, :, 16:24, :] = swap(jnp.concatenate(v, axis=0))


def adjoint_call(ids, qw, ux, bk, gx0, gx1, mats):
    _, ns, _, _, nz = qw.shape
    nx = 4 * ns
    line = pl.BlockSpec((1, 2, nx, nz), lambda g, ids: (g, 0, 0, 0))
    return pl.pallas_call(
        adjoint_kernel,
        grid_spec=pltpu.PrefetchScalarGridSpec(
            num_scalar_prefetch=1,
            grid=(2,),
            in_specs=[pl.BlockSpec((1, ns, 2, 8, nz), lambda g, ids: (g, 0, 0, 0, 0)),
                      line, whole((4, nx, nz)), line, line]
            + [whole((nx, nx))] * 2,
            out_specs=whole((2, ns, 24, nz // 2)),
            scratch_shapes=[pltpu.VMEM((4, nx, nz), F32), pltpu.VMEM((4, nx, nz), F32),
                            pltpu.VMEM((2, nx, nz), F32)],
        ),
        out_shape=jax.ShapeDtypeStruct((2, ns, 24, nz // 2), F32),
        compiler_params=params(36),
        cost_estimate=cost(1200, 9),
        name="lines_adjoint",
    )(ids, qw, ux, bk, gx0, gx1, *mats)


def last_kernel(ids, xs, c, rho, pa, pb, ta, tb, gm, tm, out, p_s, bx_s):
    i = pl.program_id(0)
    ny, nz = c.shape[1], c.shape[2]
    half = ny // 2

    @pl.when(i == 0)
    def _():
        for zh in range(2):
            z = slice(zh * (nz // 2), (zh + 1) * (nz // 2))
            p_s[:, :, z] = swap(xs[:, 8 * zh : 8 * zh + 8, :]).reshape(4, ny, nz // 2)
        t = swap(xs[:, 16:24, :]).reshape(4, ny, nz // 2)
        for zh in range(2):
            bx_s[:, :, zh * (nz // 2) : (zh + 1) * (nz // 2)] = t[2 * zh : 2 * zh + 2]

    dens, speed = rho[0], c[0]
    dk = DT * (dens * speed * speed)
    s1 = ta[0, 1] + tb[0, 1]
    s2 = ta[0, 2] + tb[0, 2] + bx_s[i]
    for group, start, t in ((ids[0], pa, ta), (1 - ids[0], pb, tb)):
        p = p_s[2 * group + i]
        q = dk * p
        s1 += t[0, 0] * p
        s2 += left(gm, start[0]) * left(gm, q) + right(start[0], tm) * right(q, tm)
    b = 1.0 / dens
    out[0, 0] = (2.0 * DT) * s1 * dens * speed
    out[1, 0] = DT * (s1 * speed * speed + s2 * b * b)


def last_call(ids, xs, c, rho, p0, p0_other, keep, other, mats):
    nx, ny, nz = c.shape
    pick = lambda i, ids: 2 * ids[0] + i
    plane = group_plane(c.shape, pick)
    three_fields = pl.BlockSpec((1, 3, ny, nz), lambda i, ids: (i, 0, 0, 0))
    return pl.pallas_call(
        last_kernel,
        grid_spec=pltpu.PrefetchScalarGridSpec(
            num_scalar_prefetch=1,
            grid=(2,),
            in_specs=[whole(xs.shape), plane, plane, group_plane(p0.shape, pick),
                      pl.BlockSpec((1, ny, nz), lambda i, ids: (i, 0, 0)), three_fields, three_fields]
            + [whole((ny, ny))] * 2,
            out_specs=pl.BlockSpec((2, 1, ny, nz), lambda i, ids: (0, i, 0, 0)),
            scratch_shapes=[pltpu.VMEM((4, ny, nz), F32), pltpu.VMEM((2, ny, nz), F32)],
        ),
        out_shape=jax.ShapeDtypeStruct((2, 2, ny, nz), F32),
        compiler_params=params(36),
        cost_estimate=cost(1100, 9),
        name="slab_last",
    )(ids, xs, c, rho, p0, p0_other, keep, other, *mats)


def change_layout(v):
    return lax.all_to_all(v, ALL, split_axis=0, concat_axis=0, tiled=True)


def swap_groups(v):
    return lax.ppermute(v, "emit", [(0, 1), (1, 0)])


def local(
    sound_speed, density, absorption, pressure_start, velocity_start, adjoint_pressure,
    adjoint_velocity, emitter_voxel, emitter_delay, drive_waveform_samples, recorded_pressures,
    sensor_flat_position,
):
    n_emit, n_slab = lax.axis_size("emit"), lax.axis_size("slab")
    ndev = n_emit * n_slab
    planes, ny, nz = sound_speed.shape
    nx = planes * n_slab
    emit = lax.axis_index("emit")
    ids = jnp.stack([emit, lax.axis_index("slab")]).astype(jnp.int32)
    mats = pair_const(deriv_matrix(ny))
    order = (4 * np.arange(n_slab)[None, :] + np.arange(4)[:, None]).reshape(-1)
    line_mats = pair_const(deriv_matrix(nx)[np.ix_(order, order)])

    p0_other = swap_groups(lax.dynamic_slice_in_dim(pressure_start[0], 2 * (1 - emit), 2, axis=0))
    buf, u1y, u1z, yz0, gy0, gz0, v0 = start_call(
        ids, sound_speed, density, absorption, pressure_start, velocity_start, adjoint_velocity,
        emitter_voxel, emitter_delay, drive_waveform_samples, mats, ndev,
    )
    maps = maps_call(
        ids, sensor_flat_position.reshape(1, -1), recorded_pressures, emitter_voxel,
        emitter_delay, drive_waveform_samples, sound_speed.shape,
    )
    lines = change_layout(buf).reshape(n_emit, n_slab, 5, 8, nz)
    xs, gx0, gx1, ux, bk = forward_call(ids, lines, line_mats)
    xs = change_layout(xs.reshape(ndev, 2, 8, nz))
    qw, send, keep = middle_call(
        ids, xs, [sound_speed, density, absorption, v0, u1y, u1z, yz0, gy0, gz0],
        adjoint_pressure, adjoint_velocity, maps, mats,
    )
    other = swap_groups(send)
    qw = change_layout(qw).reshape(n_emit, n_slab, 2, 8, nz)
    xs = adjoint_call(ids, qw, ux, bk, gx0, gx1, line_mats)
    xs = change_layout(xs.reshape(ndev, 24, nz // 2))
    own = last_call(
        ids, xs, sound_speed, density, pressure_start, p0_other, keep, other, mats
    )
    other = swap_groups(own)
    first = emit == 0
    out = jnp.concatenate(
        [jnp.where(first, own, other), jnp.where(first, other, own)], axis=1
    )
    return out[0], out[1]


def solution(mesh):
    in_specs = (
        P("slab", None, None), P("slab", None, None), P("slab", None, None),
        P("emit", "slab", None, None), P("emit", None, "slab", None, None),
        P("emit", "slab", None, None), P("emit", None, "slab", None, None),
        P("emit", None), P("emit", None), P(), P("emit", None, None), P(),
    )
    out_specs = (P("slab", None, None), P("slab", None, None))
    return jax.shard_map(local, mesh=mesh, in_specs=in_specs, out_specs=out_specs, check_vma=False)
```

time: 290 us -> 324 us (1.12)
  blocking collectives: 147 us -> 75.3 us
  starting transfers between devices: 8.62 us -> 57.3 us
  waiting for transfers between devices: 63.2 us -> 101 us
  local copies, waits for them, and re-layouts: 14.9 us -> 35.8 us
    all_to_all x3 -> x1, blocking collectives: 147 us -> 75.3 us  [change_layout(): return lax.all_to_all(v, ALL, split_axis=0, concat_axis=0, tiled=True)]
    all_to_all x1 -> x3, starting transfers between devices: 7.99 us -> 51.9 us  [change_layout(): return lax.all_to_all(v, ALL, split_axis=0, concat_axis=0, tiled=True)]
    all_to_all x1 -> x3, waiting for transfers between devices: 15.3 us -> 46.6 us  [change_layout(): return lax.all_to_all(v, ALL, split_axis=0, concat_axis=0, tiled=True)]
    unnamed x59 -> x92, local copies, waits for them, and re-layouts: 12.2 us -> 35.7 us
    ppermute x1 -> x3, waiting for transfers between devices: 48 us -> 53.9 us  [swap_groups(): return lax.ppermute(v, 'emit', [(0, 1), (1, 0)])]
    ppermute x1 -> x3, starting transfers between devices: 0.63 us -> 5.37 us  [swap_groups(): return lax.ppermute(v, 'emit', [(0, 1), (1, 0)])]
    mul x1 -> x0, other arithmetic: 3.33 us -> none  [local(): density_total = DT * (s1 * sound_speed * sound_speed + s2 * b * b)]
  transfers between devices with their start and end apart: 2 -> 6, of which waited for: 2 -> 4; matrix products, arithmetic and copies ran while one was open for 1% -> 0% of each run, Pallas kernels for 2% -> 4%
where the time goes in v2:
time: 324 us; the launch traced here: 323 us
  waiting for transfers between devices  101 us (31%)
  blocking collectives  75.3 us (23%)
  starting transfers between devices  57.3 us (18%)
  Pallas kernels  49.5 us (15%)
  local copies, waits for them, and re-layouts  35.8 us (11%)
  other arithmetic  3.51 us (1%)
    all_to_all x1, blocking collectives, change_layout(): return lax.all_to_all(v, ALL, split_axis=0, concat_axis=0, tiled=True)  75.3 us
    ppermute x3, waiting for transfers between devices, swap_groups(): return lax.ppermute(v, 'emit', [(0, 1), (1, 0)])  53.9 us
    all_to_all x3, starting transfers between devices, change_layout(): return lax.all_to_all(v, ALL, split_axis=0, concat_axis=0, tiled=True)  51.9 us
    all_to_all x3, waiting for transfers between devices, change_layout(): return lax.all_to_all(v, ALL, split_axis=0, concat_axis=0, tiled=True)  46.6 us
    unnamed x92, local copies, waits for them, and re-layouts  35.7 us
    pallas_call x1, Pallas kernels, middle_call(): pl.pallas_call(middle_kernel, grid_spec=pltpu.PrefetchScalarGridSpec(num_...  11.9 us
    pallas_call x1, Pallas kernels, start_call(): pl.pallas_call(start_kernel, grid_spec=pltpu.PrefetchScalarGridSpec(num_s...  11 us
    pallas_call x1, Pallas kernels, forward_call(): pl.pallas_call(forward_kernel, grid_spec=pltpu.PrefetchScalarGridSpec(num...  7.33 us
  transfers between devices with their start and end apart: 6, of which 4 were waited for; matrix products, arithmetic and copies ran while one was open for 0% of the time, Pallas kernels for 4%

profile of v2, /device:TPU:0, one launch (start us, length us, event | category | flops | bytes accessed | tf_op | source)
XLA Modules:
  0.0 322.8 jit_solution(12302597109351619157)
XLA Ops:
  1.2 11.0 %start.1 = (f32[128,5,8,256]{3,2,1,0:T(8,128)}, f32[4,256,256]{2,1,0:T(8,128)}, f32[4,256,256]{2,1,0:T(8,128)}, f32[4,256,256]{2,1,0:T(8,128)}, f32[4,256,256]{2...) custom-call(s32[2]{0:T(128)} %pad_add_fusion.ids, f32[64]{0:T(128)} %drive.3, f32[4,256,256]{2,1,0:T(8,128)} %c.5, ...), custom_call_target="tpu_custom_call" | custom-call | flops 2000000000 | bytes 19922944 | tf_op jit(solution)/shard_map/start/pallas_call | solution.py:162
  12.3 75.3 %all_to_all.20 = f32[128,5,8,256]{3,2,1,0:T(8,128)S(1)} all-to-all(f32[128,5,8,256]{3,2,1,0:T(8,128)} %get-tuple-element.21), channel_id=1, replica_groups=mesh['emit'=2,'slab'=64] {'emit','slab'}, dimensions={0} | all-to-all | bytes 10485760 | tf_op jit(solution)/shard_map/all_to_all | solution.py:465
  87.6 7.3 %lines_forward.1 = (f32[2,64,2,8,256]{4,3,2,1,0:T(8,128)}, f32[2,2,256,256]{3,2,1,0:T(8,128)S(1)}, f32[2,2,256,256]{3,2,1,0:T(8,128)S(1)}, f32[2,2,256,256]{3,2,1,0:T(8,128)S(1)}, f32[4,256,256]{2,1,0:T(8,128)S(1)}) custom-call(s32[2]{0:T(128)S(1)} %copy-done.39, f32[2,64,5,8,256]{4,3,2,1,0:T(8,128)S(1)} %bitcast.13, f32[2,64,5,8,256]{4,3,2,1,0:T(8,128)S(1)} %bitcast.14, ...), custom_call_target="tpu_custom_call" | custom-call | flops 1600000000 | bytes 11534336 | tf_op jit(solution)/shard_map/lines_forward/pallas_call | solution.py:263
  98.9 8.0 %all-to-all-start.1 = ((f32[128,2,8,256]{3,2,1,0:T(8,128)}), f32[128,2,8,256]{3,2,1,0:T(8,128)}, u32[]{:S(2)}, u32[]{:S(2)}) async-start(f32[128,2,8,256]{3,2,1,0:T(8,128)} %bitcast.3), calls=%async_computation.1 | async-start | bytes 4194304 | tf_op jit(solution)/shard_map/all_to_all | solution.py:465
  107.0 7.2 %maps.1 = (f32[4,256,256]{2,1,0:T(8,128)S(1)}, f32[4,256,256]{2,1,0:T(8,128)S(1)}, f32[4,256,256]{2,1,0:T(8,128)S(1)}, f32[4,256,256]{2,1,0:T(8,128)S(1)}) custom-call(s32[2]{0:T(128)S(1)} %copy-done.39, f32[64]{0:T(128)S(1)} %copy-done.42, s32[1,1024]{1,0:T(1,128)S(1)} %bitcast.16, f32[1,2,1024]{2,1,0:T(2,128)S(1)} %copy-done.44, s32[1,256]{1,0:T(1,128)S(1)} %copy-done.40, ...), custom_call_target="tpu_custom_call" | custom-call | flops 4000000000 | bytes 5242880 | tf_op jit(solution)/shard_map/maps/pallas_call | solution.py:205
  118.1 18.7 %all-to-all-done.1.xs = f32[128,2,8,256]{3,2,1,0:T(8,128)} async-done(((f32[128,2,8,256]{3,2,1,0:T(8,128)}), f32[128,2,8,256]{3,2,1,0:T(8,128)}, u32[]{:S(2)}, u32[]{:S(2)}) %all-to-all-start.1) | async-done | bytes 2097184 | tf_op jit(solution)/shard_map/all_to_all | solution.py:465
  137.8 1.2 copy-done.10
  139.0 1.2 copy-done.19
  140.2 1.2 copy-done.20
  141.5 1.2 copy-done.21
  142.7 1.2 copy-done.22
  143.9 1.2 copy-done.23
  145.2 1.2 copy-done.24
  146.4 1.2 copy-done.26
  147.6 1.2 copy-done.28
  148.8 1.2 copy-done.30
  150.1 1.2 copy-done.32
  151.3 11.9 %slab_middle.1 = (f32[128,2,8,256]{3,2,1,0:T(8,128)}, f32[2,3,256,256]{3,2,1,0:T(8,128)S(1)}, f32[2,3,256,256]{3,2,1,0:T(8,128)S(1)}) custom-call(s32[2]{0:T(128)S(1)} %copy-done.39, f32[128,2,8,256]{3,2,1,0:T(8,128)} %all-to-all-done.1.xs, f32[4,256,256]{2,1,0:T(8,128)S(1)} %copy-done, f32[4,256,256]{2,1,0:T(8,128)S(1)} %copy-done.1, ...), custom_call_target="tpu_custom_call" | custom-call | flops 3200000000 | bytes 25165824 | tf_op jit(solution)/shard_map/slab_middle/pallas_call | solution.py:339
  164.4 1.2 copy-done.43
  165.6 5.9 %all-to-all-start.2 = ((f32[128,2,8,256]{3,2,1,0:T(8,128)}), f32[128,2,8,256]{3,2,1,0:T(8,128)}, u32[]{:S(2)}, u32[]{:S(2)}) async-start(f32[128,2,8,256]{3,2,1,0:T(8,128)} %get-tuple-element.33), calls=%async_computation.2 | async-start | bytes 4194304 | tf_op jit(solution)/shard_map/all_to_all | solution.py:465
  171.6 2.5 collective-permute-start.1
  174.1 27.9 %all-to-all-done.2 = f32[128,2,8,256]{3,2,1,0:T(8,128)} async-done(((f32[128,2,8,256]{3,2,1,0:T(8,128)}), f32[128,2,8,256]{3,2,1,0:T(8,128)}, u32[]{:S(2)}, u32[]{:S(2)}) %all-to-all-start.2) | async-done | bytes 2097184 | tf_op jit(solution)/shard_map/all_to_all | solution.py:465
  202.0 1.2 copy-done.14
  207.6 6.5 %lines_adjoint.1 = f32[2,64,24,128]{3,2,1,0:T(8,128)S(1)} custom-call(s32[2]{0:T(128)S(1)} %copy-done.39, f32[2,64,2,8,256]{4,3,2,1,0:T(8,128)} %bitcast.5.qw, f32[2,2,256,256]{3,2,1,0:T(8,128)S(1)} %copy-done.16, f32[4,256,256]{2,1,0:T(8,128)S(1)} %copy-done.18, f32[2,2,256,256]{3,2,1,0:T(8,128)S(1)} %copy-done.12, f32[2,2,256,256]{3,2,1,0:T(8,128)S(1)} %copy-done.14, ...), custom_call_target="tpu_custom_call" | custom-call | flops 1200000000 | bytes 9437184 | tf_op jit(solution)/shard_map/lines_adjoint/pallas_call | solution.py:394
  215.2 38.0 %all-to-all-start.3 = ((f32[128,24,128]{2,1,0:T(8,128)}), f32[128,24,128]{2,1,0:T(8,128)}, u32[]{:S(2)}, u32[]{:S(2)}) async-start(f32[128,24,128]{2,1,0:T(8,128)} %bitcast.15), calls=%async_computation.3 | async-start | bytes 3145728 | tf_op jit(solution)/shard_map/all_to_all | solution.py:465
  253.2 2.5 collective-permute-start
  255.7 27.9 %collective-permute-done.pb = f32[2,256,256]{2,1,0:T(8,128)S(1)} collective-permute-done((f32[2,256,256]{2,1,0:T(8,128)S(1)}, f32[2,256,256]{2,1,0:T(8,128)S(1)}, u32[]{:S(2)}, u32[]{:S(2)}) %collective-permute-start) | collective-permute-done | bytes 524320 | tf_op jit(solution)/shard_map/ppermute | solution.py:469
  285.4 1.4 copy-done.9
  287.8 5.6 %slab_last.1 = f32[2,2,256,256]{3,2,1,0:T(8,128)} custom-call(s32[2]{0:T(128)S(1)} %copy-done.39, f32[128,24,128]{2,1,0:T(8,128)} %all-to-all-done.3.xs, f32[4,256,256]{2,1,0:T(8,128)S(1)} %copy-done, f32[4,256,256]{2,1,0:T(8,128)S(1)} %copy-done.1, f32[1,4,256,256]{3,2,1,0:T(8,128)S(1)} %copy-done.2, f32[2,256,256]{2,1,0:T(8,128)S(1)} %copy-done.38, ...), custom_call_target="tpu_custom_call" | custom-call | flops 1100000000 | bytes 9437184 | tf_op jit(solution)/shard_map/slab_last/pallas_call | solution.py:446
  293.8 26.1 %collective-permute-done.2 = f32[2,2,256,256]{3,2,1,0:T(8,128)S(1)} collective-permute-done((f32[2,2,256,256]{3,2,1,0:T(8,128)}, f32[2,2,256,256]{3,2,1,0:T(8,128)S(1)}, u32[]{:S(2)}, u32[]{:S(2)}) %collective-permute-start.2) | collective-permute-done | bytes 1048608 | tf_op jit(solution)/shard_map/ppermute | solution.py:469
  319.8 1.5 broadcast_select_fusion
  321.3 1.5 fusion.2
  (83 shorter events, 19.4 us)
Async XLA Ops:
  12.2 75.3 %copy-start.33 = (f32[256,256]{1,0:T(8,128)S(1)}, f32[256,256]{1,0:T(8,128)}, u32[]{:S(2)}) copy-start(f32[256,256]{1,0:T(8,128)} %constant.28.clone.gm) | copy-start | bytes 786436
  12.3 75.3 %copy-start.35 = (f32[256,256]{1,0:T(8,128)S(1)}, f32[256,256]{1,0:T(8,128)}, u32[]{:S(2)}) copy-start(f32[256,256]{1,0:T(8,128)} %constant.29.clone.tm) | copy-start | bytes 786436
  12.3 75.3 %copy-start.39 = (s32[2]{0:T(128)S(1)}, s32[2]{0:T(128)}, u32[]{:S(2)}) copy-start(s32[2]{0:T(128)} %pad_add_fusion.ids) | copy-start | bytes 28
  98.8 8.0 %copy-start.40 = (s32[1,256]{1,0:T(1,128)S(1)}, s32[1,256]{1,0:T(1,128)}, u32[]{:S(2)}) copy-start(s32[1,256]{1,0:T(1,128)} %epos.3) | copy-start | bytes 3076
  98.8 8.0 %copy-start.41 = (s32[1,256]{1,0:T(1,128)S(1)}, s32[1,256]{1,0:T(1,128)}, u32[]{:S(2)}) copy-start(s32[1,256]{1,0:T(1,128)} %delay.3) | copy-start | bytes 3076
  98.9 8.0 %copy-start.42 = (f32[64]{0:T(128)S(1)}, f32[64]{0:T(128)}, u32[]{:S(2)}) copy-start(f32[64]{0:T(128)} %drive.3) | copy-start | bytes 772
  98.9 8.0 %copy-start.44 = (f32[1,2,1024]{2,1,0:T(2,128)S(1)}, f32[1,2,1024]{2,1,0:T(2,128)}, u32[]{:S(2)}) copy-start(f32[1,2,1024]{2,1,0:T(2,128)} %rec.1) | copy-start | bytes 24580
  98.9 8.1 %copy-start.45 = (s32[1024]{0:T(1024)S(1)}, s32[1024]{0:T(1024)}, u32[]{:S(2)}) copy-start(s32[1024]{0:T(1024)} %param.27) | copy-start | bytes 12292
  98.9 38.0 %all-to-all-start.1 = ((f32[128,2,8,256]{3,2,1,0:T(8,128)}), f32[128,2,8,256]{3,2,1,0:T(8,128)}, u32[]{:S(2)}, u32[]{:S(2)}) async-start(f32[128,2,8,256]{3,2,1,0:T(8,128)} %bitcast.3), calls=%async_computation.1 | async-start | bytes 4194304 | tf_op jit(solution)/shard_map/all_to_all | solution.py:465
  106.9 29.9 %copy-start = (f32[4,256,256]{2,1,0:T(8,128)S(1)}, f32[4,256,256]{2,1,0:T(8,128)}, u32[]{:S(2)}) copy-start(f32[4,256,256]{2,1,0:T(8,128)} %c.5) | copy-start | bytes 3145732
  106.9 29.9 %copy-start.1 = (f32[4,256,256]{2,1,0:T(8,128)S(1)}, f32[4,256,256]{2,1,0:T(8,128)}, u32[]{:S(2)}) copy-start(f32[4,256,256]{2,1,0:T(8,128)} %rho.5) | copy-start | bytes 3145732
  106.9 29.9 %copy-start.4 = (f32[4,256,256]{2,1,0:T(8,128)S(1)}, f32[4,256,256]{2,1,0:T(8,128)}, u32[]{:S(2)}) copy-start(f32[4,256,256]{2,1,0:T(8,128)} %alpha.3) | copy-start | bytes 3145732
  107.0 29.9 %copy-start.5 = (f32[256,256]{1,0:T(8,128)S(1)}, f32[256,256]{1,0:T(8,128)}, u32[]{:S(2)}) copy-start(f32[256,256]{1,0:T(8,128)} %constant.26.clone.gm) | copy-start | bytes 786436
  137.8 1.2 copy-start.10
  139.0 1.2 copy-start.19
  140.2 1.2 copy-start.20
  141.5 1.2 copy-start.21
  143.9 1.2 copy-start.23
  145.1 1.2 copy-start.24
  146.4 1.2 copy-start.26
  147.6 1.2 copy-start.28
  148.8 1.2 copy-start.30
  164.4 1.2 copy-start.43
  165.6 36.4 %copy-start.12 = (f32[2,2,256,256]{3,2,1,0:T(8,128)S(1)}, f32[2,2,256,256]{3,2,1,0:T(8,128)}, u32[]{:S(2)}) copy-start(f32[2,2,256,256]{3,2,1,0:T(8,128)} %copy-done.11) | copy-start | bytes 3145732
  165.6 36.4 %all-to-all-start.2 = ((f32[128,2,8,256]{3,2,1,0:T(8,128)}), f32[128,2,8,256]{3,2,1,0:T(8,128)}, u32[]{:S(2)}, u32[]{:S(2)}) async-start(f32[128,2,8,256]{3,2,1,0:T(8,128)} %get-tuple-element.33), calls=%async_computation.2 | async-start | bytes 4194304 | tf_op jit(solution)/shard_map/all_to_all | solution.py:465
  171.6 112.8 %collective-permute-start.1 = (f32[2,3,256,256]{3,2,1,0:T(8,128)}, f32[2,3,256,256]{3,2,1,0:T(8,128)}, u32[]{:S(2)}, u32[]{:S(2)}) collective-permute-start(f32[2,3,256,256]{3,2,1,0:T(8,128)} %copy-done.43), channel_id=1, source_target_pairs={{0,64},{64,0},{1,65},{65,1},{2,66},{66,2},{3,67},{67,3},{4,68},{68... | collective-permute-start | bytes 4718600 | tf_op jit(solution)/shard_map/ppermute | solution.py:469
  202.0 1.2 copy-start.14
  215.2 38.0 %copy-start.2 = (f32[1,4,256,256]{3,2,1,0:T(8,128)S(1)}, f32[1,4,256,256]{3,2,1,0:T(8,128)}, u32[]{:S(2)}) copy-start(f32[1,4,256,256]{3,2,1,0:T(8,128)} %pa.3) | copy-start | bytes 3145732
  215.2 69.2 %all-to-all-start.3 = ((f32[128,24,128]{2,1,0:T(8,128)}), f32[128,24,128]{2,1,0:T(8,128)}, u32[]{:S(2)}, u32[]{:S(2)}) async-start(f32[128,24,128]{2,1,0:T(8,128)} %bitcast.15), calls=%async_computation.3 | async-start | bytes 3145728 | tf_op jit(solution)/shard_map/all_to_all | solution.py:465
  253.2 30.4 %collective-permute-start = (f32[2,256,256]{2,1,0:T(8,128)S(1)}, f32[2,256,256]{2,1,0:T(8,128)S(1)}, u32[]{:S(2)}, u32[]{:S(2)}) collective-permute-start(f32[2,256,256]{2,1,0:T(8,128)S(1)} %dynamic-slice_bitcast_fusion), channel_id=1, source_target_pairs={{0,64},{64,0},{1,65},{65,1},{2,66},{66,2},{3,67},{67,3},{4,68},{68... | collective-permute-start | bytes 1572872 | tf_op jit(solution)/shard_map/ppermute | solution.py:469
  285.4 1.4 copy-start.9
  293.4 26.4 %collective-permute-start.2 = (f32[2,2,256,256]{3,2,1,0:T(8,128)}, f32[2,2,256,256]{3,2,1,0:T(8,128)S(1)}, u32[]{:S(2)}, u32[]{:S(2)}) collective-permute-start(f32[2,2,256,256]{3,2,1,0:T(8,128)} %slab_last.1), channel_id=1, source_target_pairs={{0,64},{64,0},{1,65},{65,1},{2,66},{66,2},{3,67},{67,3},{4,68},{68... | collective-permute-start | bytes 3145736 | tf_op jit(solution)/shard_map/ppermute | solution.py:469
  (20 other events, 20.8 us)

commit v3 on v2

v3 whole, which is shorter than its diff:
```python
import numpy as np
import jax
import jax.numpy as jnp
from jax import lax
from jax.experimental import pallas as pl
from jax.experimental.pallas import tpu as pltpu
from jax.sharding import PartitionSpec as P

STEPS = 2
DT = 0.2
F32 = jnp.float32
BF16 = jnp.bfloat16
ALL = ("emit", "slab")
MIB = 2**20
LIMIT = {"start": 60, "prepare": 60, "forward": 60, "middle": 60, "adjoint": 60, "last": 60}


def deriv_matrix(n):
    k = np.arange(1, n // 2, dtype=np.int64)
    pts = np.arange(n, dtype=np.int64)
    shifted = (k[None, :] * (2 * pts[:, None] + 1)) % (2 * n) * (np.pi / n)
    plain = (k[None, :] * (2 * pts[:, None])) % (2 * n) * (np.pi / n)
    w = k * (2.0 * np.pi / n)
    m = (np.cos(shifted) * w) @ np.sin(plain).T - (np.sin(shifted) * w) @ np.cos(plain).T
    return m * (2.0 / n)


def pair_const(m):
    m = m.astype(np.float32)
    return [jnp.asarray(m), jnp.asarray(np.ascontiguousarray(m.T))]


def split2(v):
    hi = v.astype(BF16)
    return hi, (v - hi.astype(F32)).astype(BF16)


def split3(v):
    hi = v.astype(BF16)
    rest = v - hi.astype(F32)
    mid = rest.astype(BF16)
    return hi, mid, (rest - mid.astype(F32)).astype(BF16)


def dot(a, b):
    return jnp.dot(a, b, preferred_element_type=F32)


def left(m, v):
    mh, ml = split2(m[...])
    h, l = split2(v)
    return dot(mh, h) + (dot(mh, l) + dot(ml, h))


def right(v, m):
    mh, ml = split2(m[...])
    h, l = split2(v)
    return dot(h, mh) + (dot(l, mh) + dot(h, ml))


def params(mib, n_grid=1):
    return pltpu.CompilerParams(
        dimension_semantics=("arbitrary",) * n_grid, vmem_limit_bytes=mib * MIB
    )


def cost(mflop, mib):
    return pl.CostEstimate(flops=mflop * 10**6, bytes_accessed=mib * MIB, transcendentals=0)


def swap(v):
    return jnp.swapaxes(v, 0, 1)


def whole(shape):
    return pl.BlockSpec(shape, lambda i, ids: (0,) * len(shape))


def group_plane(shape, pick, a=0):
    block = (None,) * (len(shape) - 3) + (1,) + shape[-2:]
    return pl.BlockSpec(block, lambda i, ids: (0, a)[: len(shape) - 3] + (pick(i, ids), 0, 0))


def plane_onehot(pos, plane, ny, nz):
    local = pos - plane * (ny * nz)
    y = lax.broadcasted_iota(jnp.int32, (ny, pos.shape[1]), 0) * nz
    return jnp.where((local >= y) & (local < y + nz), 1.0, 0.0).astype(BF16)


def column_onehot(pos, nz):
    z = lax.broadcasted_iota(jnp.int32, (nz, pos.shape[1]), 0)
    return lax.rem(pos, nz) == z


def drive_at(delay, drive, step):
    amp = jnp.zeros(delay.shape, F32)
    for k in range(drive.shape[0]):
        amp = jnp.where(delay + step == k, drive[k], amp)
    return amp


def three(onehot, value):
    return jnp.concatenate(
        [jnp.where(onehot, v.astype(F32), 0.0).astype(BF16) for v in split3(value)], axis=0
    )


def spread(rows, cols):
    return lax.dot_general(rows, cols, (((1,), (1,)), ((), ())), preferred_element_type=F32)


def sum3(v):
    n = v.shape[1] // 3
    return v[:, :n] + v[:, n : 2 * n] + v[:, 2 * n :]


def first_step(c, rho, alpha, p0, uy, uz, epos, cols, plane, gm, tm):
    ny, nz = p0.shape[1], p0.shape[2]
    dens, speed, p = rho[0], c[0], p0[0]
    b = 1.0 / dens
    bulk = dens * speed * speed
    gy = left(gm, p)
    gz = right(p, tm)
    wy = uy[0] - DT * b * gy
    wz = uz[0] - DT * b * gz
    yz = left(tm, wy) + right(wz, gm)
    shot = sum3(spread(plane_onehot(epos[...], plane, ny, nz), cols[...]))
    v = (1.0 - DT * alpha[0]) * p + (DT * bulk) * yz + shot
    return gy, gz, wy, wz, yz, v, b, bulk


def start_kernel(
    ids, drive, c, rho, alpha, p0, ux, uy, uz, vx, epos, delay, gm, tm, buf, mat, cols, pack
):
    i = pl.program_id(0)
    ny, nz = p0.shape[1], p0.shape[2]
    half = ny // 2

    @pl.when(i == 0)
    def _():
        cols[...] = three(column_onehot(epos[...], nz), drive_at(delay[...], drive, 0))

    @pl.when(i < 4)
    def _():
        _, _, _, _, _, v, b, bulk = first_step(
            c, rho, alpha, p0, uy, uz, epos, cols, ids[1] * 4 + i, gm, tm
        )
        for f, field in enumerate((p0[0], ux[0], v, vx[0])):
            pack[2 * f : 2 * f + 2] = field.reshape(2, half, nz)
        buf[:, 0] = swap(pack[...])
        for xm in range(2):

            @pl.when(i == 2 * ids[0] + xm)
            def _():
                mat[4 * xm : 4 * xm + 2] = b.reshape(2, half, nz)
                mat[4 * xm + 2 : 4 * xm + 4] = bulk.reshape(2, half, nz)

    @pl.when(i == 4)
    def _():
        buf[:, 0] = swap(mat[...])


def start_call(ids, c, rho, alpha, p0, u, v, epos, delay, drive, mats, ndev):
    nx, ny, nz = c.shape
    pick = lambda i, ids: jnp.minimum(i, nx - 1)
    plane = group_plane(c.shape, pick)
    n_e = epos.shape[1]
    return pl.pallas_call(
        start_kernel,
        grid_spec=pltpu.PrefetchScalarGridSpec(
            num_scalar_prefetch=1,
            grid=(nx + 1,),
            in_specs=[pl.BlockSpec(memory_space=pltpu.SMEM)] + [plane] * 3
            + [group_plane(p0.shape, pick)]
            + [group_plane(u.shape, pick, a) for a in (0, 1, 2, 0)]
            + [whole((1, n_e))] * 2 + [whole((ny, ny))] * 2,
            out_specs=pl.BlockSpec((ndev, 1, 8, nz), lambda i, ids: (0, i, 0, 0)),
            scratch_shapes=[pltpu.VMEM((8, ndev, nz), F32), pltpu.VMEM((3 * nz, n_e), BF16),
                            pltpu.VMEM((8, ndev, nz), F32)],
        ),
        out_shape=jax.ShapeDtypeStruct((ndev, 5, 8, nz), F32),
        compiler_params=params(LIMIT["start"]),
        cost_estimate=cost(2000, 13),
        name="start",
    )(ids, drive, c, rho, alpha, p0, u, u, u, v, epos, delay, *mats)


def prepare_kernel(
    ids, drive, c, rho, alpha, p0, uy, uz, pa, spos, rec, epos, delay, gm, tm,
    v0, u1y, u1z, yz0, gy0, gz0, cnt, m0, pm, scols, ecols,
):
    i = pl.program_id(0)
    ny, nz = cnt.shape[1], cnt.shape[2]

    @pl.when(i == 0)
    def _():
        oh = column_onehot(spos[...], nz)
        scols[:nz] = jnp.where(oh, 1.0, 0.0).astype(BF16)
        scols[nz : 4 * nz] = three(oh, rec[0:1])
        scols[4 * nz :] = three(oh, rec[1:2])
        for step in range(STEPS):
            ecols[step] = three(column_onehot(epos[...], nz), drive_at(delay[...], drive, step))

    plane = ids[1] * 4 + i
    gy0[0], gz0[0], u1y[0], u1z[0], yz0[0], v0[0], _, _ = first_step(
        c, rho, alpha, p0, uy, uz, epos, ecols.at[0], plane, gm, tm
    )
    s = plane_onehot(spos[...], plane, ny, nz)
    count = spread(s, scols[:nz])
    cnt[0] = count
    m0[0] = sum3(spread(s, scols[nz : 4 * nz]))
    shot = sum3(spread(plane_onehot(epos[...], plane, ny, nz), ecols[1]))
    pm[0] = pa[0] + (count * shot - sum3(spread(s, scols[4 * nz :])))


def prepare_call(ids, c, rho, alpha, p0, u, pa, spos, rec, epos, delay, drive, mats):
    nx, ny, nz = c.shape
    n_e, n_s = epos.shape[1], spos.shape[1]
    pick = lambda i, ids: i
    plane = group_plane(c.shape, pick)
    return pl.pallas_call(
        prepare_kernel,
        grid_spec=pltpu.PrefetchScalarGridSpec(
            num_scalar_prefetch=1,
            grid=(nx,),
            in_specs=[pl.BlockSpec(memory_space=pltpu.SMEM)] + [plane] * 3
            + [group_plane(p0.shape, pick)] + [group_plane(u.shape, pick, a) for a in (1, 2)]
            + [group_plane(pa.shape, pick), whole((1, n_s)),
               pl.BlockSpec((None, STEPS, n_s), lambda i, ids: (0, 0, 0)),
               whole((1, n_e)), whole((1, n_e))] + [whole((ny, ny))] * 2,
            out_specs=[plane] * 9,
            scratch_shapes=[pltpu.VMEM((7 * nz, n_s), BF16), pltpu.VMEM((STEPS, 3 * nz, n_e), BF16)],
        ),
        out_shape=[jax.ShapeDtypeStruct(c.shape, F32)] * 9,
        compiler_params=params(LIMIT["prepare"]),
        cost_estimate=cost(6000, 17),
        name="prepare",
    )(ids, drive, c, rho, alpha, p0, u, u, pa, spos, rec, epos, delay, *mats)


def unpack(block, dst, first):
    t = swap(block)
    n, hz = t.shape[1], t.shape[2]
    for xm in range(2):
        for f in range(2):
            for yl in range(2):
                dst[f, (first + xm) * n : (first + xm + 1) * n, yl * hz : (yl + 1) * hz] = t[4 * xm + 2 * f + yl]


def line_rows(v, xl, n):
    hz = v.shape[1] // 2
    rows = v[xl * n : (xl + 1) * n]
    return jnp.stack([rows[:, :hz], rows[:, hz:]])


def forward_kernel(ids, fields, mat, gm, tm, out, gx0, gx1, ax, bk, f_s, o_s):
    n, hz = fields.shape[1], fields.shape[4]

    @pl.when(pl.program_id(1) == 0)
    def _():
        for e in range(2):
            unpack(mat[e, :, 0], bk.at[0], 2 * e)

    for xl in range(4):
        t = swap(fields[0, :, xl])
        for f in range(4):
            dst = f_s if f < 3 else ax.at[0]
            for yl in range(2):
                dst[f if f < 3 else 0, xl * n : (xl + 1) * n, yl * hz : (yl + 1) * hz] = t[2 * f + yl]
    b = DT * bk[0, 0]
    g0 = left(gm, f_s[0])
    u1 = f_s[1] - b * g0
    x0 = left(tm, u1)
    g1 = left(gm, f_s[2] + (DT * bk[0, 1]) * x0)
    gx0[0, 0] = g0
    gx1[0, 0] = g1
    o_s[0] = x0
    o_s[1] = left(tm, u1 - b * g1)
    for h in range(2):
        rows = [line_rows(o_s[f], 2 * h + xm, n) for xm in range(2) for f in range(2)]
        out[0, :, h] = swap(jnp.concatenate(rows, axis=0))


def line_specs(nx, hz):
    return (pl.BlockSpec((1, 1, nx, 2 * hz), lambda zh, g, ids: (g, zh, 0, 0)),
            pl.BlockSpec((1, 2, nx, 2 * hz), lambda zh, g, ids: (zh, 0, 0, 0)),
            pl.BlockSpec((nx, nx), lambda zh, g, ids: (0, 0)))


def forward_call(ids, buf, mats):
    _, ns, _, _, nz = buf.shape
    nx, hz = 4 * ns, nz // 2
    line, pair, mat = line_specs(nx, hz)
    full = jax.ShapeDtypeStruct((2, 2, nx, nz), F32)
    return pl.pallas_call(
        forward_kernel,
        grid_spec=pltpu.PrefetchScalarGridSpec(
            num_scalar_prefetch=1,
            grid=(2, 2),
            in_specs=[pl.BlockSpec((1, ns, 4, 8, hz), lambda zh, g, ids: (g, 0, 0, 0, zh)),
                      pl.BlockSpec((2, ns, 1, 8, hz), lambda zh, g, ids: (0, 0, 4, 0, zh)), mat, mat],
            out_specs=[pl.BlockSpec((1, ns, 2, 8, hz), lambda zh, g, ids: (g, 0, 0, 0, zh)),
                       line, line, line, pair],
            scratch_shapes=[pltpu.VMEM((3, nx, nz), F32), pltpu.VMEM((2, nx, nz), F32)],
        ),
        out_shape=[jax.ShapeDtypeStruct((2, ns, 2, 8, nz), F32), full, full, full, full],
        compiler_params=params(LIMIT["forward"], 2),
        cost_estimate=cost(1600, 11),
        name="lines_forward",
    )(ids, buf, buf, *mats)


def middle_kernel(
    ids, xs, c, rho, alpha, uya, uza, v0, u1y, u1z, yz0, gy0, gz0, cnt, m0, pm, gm, tm,
    buf, d0, t1, t2, x_s, o_s,
):
    xm = lax.rem(pl.program_id(0), 2)
    ny, nz = c.shape[1], c.shape[2]
    half = ny // 2

    @pl.when(xm == 0)
    def _():
        x_s[...] = swap(xs[:, 0]).reshape(4, ny, nz)

    x0 = x_s[2 * xm]
    dens, speed = rho[0], c[0]
    b = 1.0 / dens
    dk = DT * (dens * speed * speed)
    stay = 1.0 - DT * alpha[0]
    p1 = v0[0] + dk * x0
    d0[0] = x0 + yz0[0]
    gy = left(gm, p1)
    gz = right(p1, tm)
    db = DT * b
    div1 = x_s[2 * xm + 1] + left(tm, u1y[0] - db * gy) + right(u1z[0] - db * gz, gm)
    adj = pm[0] + cnt[0] * (stay * p1 + dk * div1)
    q = dk * adj
    ay = uya[0] + left(gm, q)
    az = uza[0] + right(q, tm)
    back = left(tm, b * ay) + right(b * az, gm)
    o_s[2 * xm] = q
    o_s[2 * xm + 1] = stay * adj - DT * back + (cnt[0] * p1 - m0[0])
    t1[0] = div1 * adj
    t2[0] = (gy + gy0[0]) * ay + (gz + gz0[0]) * az

    @pl.when(xm == 1)
    def _():
        buf[:, 0] = swap(o_s[...].reshape(8, half, nz))


def middle_call(ids, xs, c, rho, alpha, v, fields, mats):
    ndev, _, _, nz = xs.shape
    nx, ny, _ = c.shape
    pick = lambda i, ids: i
    plane = group_plane(c.shape, pick)
    pair = pl.BlockSpec((ndev, 1, 8, nz), lambda i, ids: (0, i // 2, 0, 0))
    return pl.pallas_call(
        middle_kernel,
        grid_spec=pltpu.PrefetchScalarGridSpec(
            num_scalar_prefetch=1,
            grid=(nx,),
            in_specs=[pair] + [plane] * 3 + [group_plane(v.shape, pick, a) for a in (1, 2)]
            + [plane] * len(fields) + [whole((ny, ny))] * 2,
            out_specs=[pair] + [plane] * 3,
            scratch_shapes=[pltpu.VMEM((4, ny, nz), F32)] * 2,
        ),
        out_shape=[jax.ShapeDtypeStruct(xs.shape, F32)] + [jax.ShapeDtypeStruct(c.shape, F32)] * 3,
        compiler_params=params(LIMIT["middle"]),
        cost_estimate=cost(3200, 21),
        name="slab_middle",
    )(ids, xs, c, rho, alpha, v, v, *fields, *mats)


def adjoint_kernel(ids, qw, ux, bk, gx0, gx1, gm, tm, out, f_s, bx_s):
    zh, g = pl.program_id(0), pl.program_id(1)
    n, hz = qw.shape[1], qw.shape[4]
    for h in range(2):
        unpack(qw[0, :, h], f_s, 2 * h)
    ax = ux[0, 0] + left(gm, f_s[0])
    p0 = f_s[1] - DT * left(tm, bk[0, 0] * ax)
    bx = gx1[0, 0] * ax + gx0[0, 0] * (ax + left(gm, (DT * bk[0, 1]) * p0))
    rows = swap(jnp.concatenate([line_rows(p0, xl, n) for xl in range(4)], axis=0))
    for z in range(2):

        @pl.when(zh == z)
        def _():
            out[pl.ds(g, 1), :, 8 * z : 8 * z + 8, :] = rows[None]

    @pl.when(g == 0)
    def _():
        bx_s[zh] = bx

    @pl.when(g == 1)
    def _():
        bx_s[zh] += bx

    @pl.when((g == 1) & (zh == 1))
    def _():
        for e in range(2):
            v = [line_rows(bx_s[z], 2 * e + xm, n) for z in range(2) for xm in range(2)]
            out[e, :, 16:24, :] = swap(jnp.concatenate(v, axis=0))


def adjoint_call(ids, qw, ux, bk, gx0, gx1, mats):
    _, ns, _, _, nz = qw.shape
    nx, hz = 4 * ns, nz // 2
    line, pair, mat = line_specs(nx, hz)
    return pl.pallas_call(
        adjoint_kernel,
        grid_spec=pltpu.PrefetchScalarGridSpec(
            num_scalar_prefetch=1,
            grid=(2, 2),
            in_specs=[pl.BlockSpec((1, ns, 2, 8, hz), lambda zh, g, ids: (g, 0, 0, 0, zh)),
                      line, pair, line, line, mat, mat],
            out_specs=pl.BlockSpec((2, ns, 24, hz), lambda zh, g, ids: (0, 0, 0, 0)),
            scratch_shapes=[pltpu.VMEM((2, nx, nz), F32), pltpu.VMEM((2, nx, nz), F32)],
        ),
        out_shape=jax.ShapeDtypeStruct((2, ns, 24, hz), F32),
        compiler_params=params(LIMIT["adjoint"], 2),
        cost_estimate=cost(1200, 9),
        name="lines_adjoint",
    )(ids, qw, ux, bk, gx0, gx1, *mats)


def last_bulk_kernel(ids, xs, d0, t1, out, p0):
    p = swap(xs[...]).reshape(p0.shape)
    p0[...] = p
    out[...] = t1[...] + d0[...] * p


def last_bulk_call(ids, xs, d0, t1):
    nx, ny, nz = d0.shape
    part = pl.BlockSpec((nx, ny, nz // 2), lambda zh, ids: (0, 0, zh))
    return pl.pallas_call(
        last_bulk_kernel,
        grid_spec=pltpu.PrefetchScalarGridSpec(
            num_scalar_prefetch=1,
            grid=(2,),
            in_specs=[pl.BlockSpec((xs.shape[0], 8, nz // 2), lambda zh, ids: (0, zh, 0)), part, part],
            out_specs=[part, part],
        ),
        out_shape=[jax.ShapeDtypeStruct(d0.shape, F32)] * 2,
        compiler_params=params(LIMIT["last"]),
        cost_estimate=cost(1, 5),
        name="slab_last_bulk",
    )(ids, xs, d0, t1)


def last_buoy_kernel(ids, xs, p0, c, rho, t2, gy0, gz0, gm, tm, out, bx_s):
    i = pl.program_id(0)
    ny, nz = c.shape[1], c.shape[2]

    @pl.when(i == 0)
    def _():
        t = swap(xs[...]).reshape(4, ny, nz // 2)
        for zh in range(2):
            bx_s[:, :, zh * (nz // 2) : (zh + 1) * (nz // 2)] = t[2 * zh : 2 * zh + 2]

    q = (DT * (rho[0] * c[0] * c[0])) * p0[0]
    out[0] = t2[0] + gy0[0] * left(gm, q) + gz0[0] * right(q, tm)

    @pl.when(i // 2 == ids[0])
    def _():
        out[0] += bx_s[lax.rem(i, 2)]


def last_buoy_call(ids, xs, p0, c, rho, t2, gy0, gz0, mats):
    nx, ny, nz = c.shape
    plane = group_plane(c.shape, lambda i, ids: i)
    return pl.pallas_call(
        last_buoy_kernel,
        grid_spec=pltpu.PrefetchScalarGridSpec(
            num_scalar_prefetch=1,
            grid=(nx,),
            in_specs=[pl.BlockSpec((xs.shape[0], 8, nz // 2), lambda i, ids: (0, 2, 0))]
            + [plane] * 6 + [whole((ny, ny))] * 2,
            out_specs=plane,
            scratch_shapes=[pltpu.VMEM((2, ny, nz), F32)],
        ),
        out_shape=jax.ShapeDtypeStruct(c.shape, F32),
        compiler_params=params(LIMIT["last"]),
        cost_estimate=cost(800, 8),
        name="slab_last_buoy",
    )(ids, xs, p0, c, rho, t2, gy0, gz0, *mats)


def change_layout(v):
    return lax.all_to_all(v, ALL, split_axis=0, concat_axis=0, tiled=True)


def swap_groups(v):
    return lax.ppermute(v, "emit", [(0, 1), (1, 0)])


def local(
    sound_speed, density, absorption, pressure_start, velocity_start, adjoint_pressure,
    adjoint_velocity, emitter_voxel, emitter_delay, drive_waveform_samples, recorded_pressures,
    sensor_flat_position,
):
    n_emit, n_slab = lax.axis_size("emit"), lax.axis_size("slab")
    ndev = n_emit * n_slab
    planes, ny, nz = sound_speed.shape
    nx = planes * n_slab
    emit = lax.axis_index("emit")
    ids = jnp.stack([emit, lax.axis_index("slab")]).astype(jnp.int32)
    mats = pair_const(deriv_matrix(ny))
    order = (4 * np.arange(n_slab)[None, :] + np.arange(4)[:, None]).reshape(-1)
    line_mats = pair_const(deriv_matrix(nx)[np.ix_(order, order)])

    buf = start_call(
        ids, sound_speed, density, absorption, pressure_start, velocity_start, adjoint_velocity,
        emitter_voxel, emitter_delay, drive_waveform_samples, mats, ndev,
    )
    v0, u1y, u1z, yz0, gy0, gz0, cnt, m0, pm = prepare_call(
        ids, sound_speed, density, absorption, pressure_start, velocity_start, adjoint_pressure,
        sensor_flat_position.reshape(1, -1), recorded_pressures, emitter_voxel, emitter_delay,
        drive_waveform_samples, mats,
    )
    lines = change_layout(buf).reshape(n_emit, n_slab, 5, 8, nz)
    xs, gx0, gx1, ux, bk = forward_call(ids, lines, line_mats)
    xs = change_layout(xs.reshape(ndev, 2, 8, nz))
    qw, d0, t1, t2 = middle_call(
        ids, xs, sound_speed, density, absorption, adjoint_velocity,
        [v0, u1y, u1z, yz0, gy0, gz0, cnt, m0, pm], mats,
    )
    qw = change_layout(qw).reshape(n_emit, n_slab, 2, 8, nz)
    xs = adjoint_call(ids, qw, ux, bk, gx0, gx1, line_mats)
    xs = change_layout(xs.reshape(ndev, 24, nz // 2))
    bulk_part, p0 = last_bulk_call(ids, xs, d0, t1)
    other = swap_groups(bulk_part)
    buoy_part = last_buoy_call(ids, xs, p0, sound_speed, density, t2, gy0, gz0, mats)
    s1 = bulk_part + other
    s2 = buoy_part + swap_groups(buoy_part)
    b = 1.0 / density
    speed_total = (2.0 * DT) * s1 * density * sound_speed
    density_total = DT * (s1 * sound_speed * sound_speed + s2 * b * b)
    return speed_total, density_total


def solution(mesh):
    in_specs = (
        P("slab", None, None), P("slab", None, None), P("slab", None, None),
        P("emit", "slab", None, None), P("emit", None, "slab", None, None),
        P("emit", "slab", None, None), P("emit", None, "slab", None, None),
        P("emit", None), P("emit", None), P(), P("emit", None, None), P(),
    )
    out_specs = (P("slab", None, None), P("slab", None, None))
    return jax.shard_map(local, mesh=mesh, in_specs=in_specs, out_specs=out_specs, check_vma=False)
```

time: 324 us -> 285 us (0.88)
  blocking collectives: 75.3 us -> 142 us
  starting transfers between devices: 57.3 us -> 11 us
  waiting for transfers between devices: 101 us -> 63.5 us
  local copies, waits for them, and re-layouts: 35.8 us -> 1.34 us
  Pallas kernels: 49.5 us -> 62.4 us
    all_to_all x1 -> x3, blocking collectives: 75.3 us -> 142 us  [change_layout(): return lax.all_to_all(v, ALL, split_axis=0, concat_axis=0, tiled=True)]
    all_to_all x3 -> x1, starting transfers between devices: 51.9 us -> 7.46 us  [change_layout(): return lax.all_to_all(v, ALL, split_axis=0, concat_axis=0, tiled=True)]
    unnamed x92 -> x8, local copies, waits for them, and re-layouts: 35.7 us -> 1.34 us
    all_to_all x3 -> x1, waiting for transfers between devices: 46.6 us -> 18.5 us  [change_layout(): return lax.all_to_all(v, ALL, split_axis=0, concat_axis=0, tiled=True)]
    pallas_call x2 -> x3, Pallas kernels: 12.8 us -> 22.1 us  [the longest x1 11.9 us: prepare_call(): pl.pallas_call(prepare_kernel, grid_spec=pltpu.PrefetchScalarGridSpec(num...]
    ppermute x3 -> x2, waiting for transfers between devices: 53.9 us -> 45 us  [swap_groups(): return lax.ppermute(v, 'emit', [(0, 1), (1, 0)])]
  transfers between devices with their start and end apart: 6 -> 3, of which waited for: 4 -> 3; matrix products, arithmetic and copies ran while one was open for 0% -> 0% of each run, Pallas kernels for 4% -> 4%
where the time goes in v3:
time: 285 us; the launch traced here: 284 us
  blocking collectives  142 us (50%)
  waiting for transfers between devices  63.5 us (22%)
  Pallas kernels  62.4 us (22%)
  starting transfers between devices  11 us (4%)
  other arithmetic  3.57 us (1%)
    all_to_all x3, blocking collectives, change_layout(): return lax.all_to_all(v, ALL, split_axis=0, concat_axis=0, tiled=True)  142 us
    ppermute x2, waiting for transfers between devices, swap_groups(): return lax.ppermute(v, 'emit', [(0, 1), (1, 0)])  45 us
    all_to_all x1, waiting for transfers between devices, change_layout(): return lax.all_to_all(v, ALL, split_axis=0, concat_axis=0, tiled=True)  18.5 us
    pallas_call x1, Pallas kernels, middle_call(): pl.pallas_call(middle_kernel, grid_spec=pltpu.PrefetchScalarGridSpec(num_...  13.3 us
    pallas_call x1, Pallas kernels, prepare_call(): pl.pallas_call(prepare_kernel, grid_spec=pltpu.PrefetchScalarGridSpec(num...  11.9 us
    pallas_call x1, Pallas kernels, forward_call(): pl.pallas_call(forward_kernel, grid_spec=pltpu.PrefetchScalarGridSpec(num...  9.28 us
    pallas_call x1, Pallas kernels, start_call(): pl.pallas_call(start_kernel, grid_spec=pltpu.PrefetchScalarGridSpec(num_s...  9.24 us
    pallas_call x1, Pallas kernels, adjoint_call(): pl.pallas_call(adjoint_kernel, grid_spec=pltpu.PrefetchScalarGridSpec(num...  8.43 us
  transfers between devices with their start and end apart: 3, of which 3 were waited for; matrix products, arithmetic and copies ran while one was open for 0% of the time, Pallas kernels for 4%

profile of v3, /device:TPU:0, one launch (start us, length us, event | category | flops | bytes accessed | tf_op | source)
XLA Modules:
  0.0 284.1 jit_solution(1922505933350237938)
XLA Ops:
  0.6 0.6 pad_add_fusion.ids
  1.2 9.2 %start.1 = f32[128,5,8,256]{3,2,1,0:T(8,128)} custom-call(s32[2]{0:T(128)} %pad_add_fusion.ids, f32[64]{0:T(128)} %drive.3, f32[4,256,256]{2,1,0:T(8,128)} %c.7, f32[4,256,256]{2,1,0:T(8,128)} %rho.7, f32[4,256,256]{2,1,0:T(8,128)} %alpha.5, f32[1,4,256,256]{3,2,1,0:T(8,128)} %p0.3, f32[1,3,4,256,256]{4,3,2,1,0:T(8,128)} %uz.3, f32[1,3,4,256,256]{4,3,2,1,0:T(8,128)} %uz.3, ...), custom_call_target="tpu_custom_call" | custom-call | flops 2000000000 | bytes 13631488 | tf_op jit(solution)/shard_map/start/pallas_call | solution.py:168
  10.5 75.3 %all_to_all.20 = f32[128,5,8,256]{3,2,1,0:T(8,128)} all-to-all(f32[128,5,8,256]{3,2,1,0:T(8,128)} %start.1), channel_id=1, replica_groups=mesh['emit'=2,'slab'=64] {'emit','slab'}, dimensions={0} | all-to-all | bytes 10485760 | tf_op jit(solution)/shard_map/all_to_all | solution.py:488
  85.8 9.3 %lines_forward.1 = (f32[2,64,2,8,256]{4,3,2,1,0:T(8,128)}, f32[2,2,256,256]{3,2,1,0:T(8,128)}, f32[2,2,256,256]{3,2,1,0:T(8,128)}, f32[2,2,256,256]{3,2,1,0:T(8,128)}, f32[2,2,256,256]{3,2,1,0:T(8,128)}) custom-call(s32[2]{0:T(128)} %pad_add_fusion.ids, f32[2,64,5,8,256]{4,3,2,1,0:T(8,128)} %bitcast.7, f32[2,64,5,8,256]{4,3,2,1,0:T(8,128)} %bitcast.8, ...), custom_call_target="tpu_custom_call" | custom-call | flops 1600000000 | bytes 11534336 | tf_op jit(solution)/shard_map/lines_forward/pallas_call | solution.py:295
  95.1 7.5 %all-to-all-start.1 = ((f32[128,2,8,256]{3,2,1,0:T(8,128)}), f32[128,2,8,256]{3,2,1,0:T(8,128)S(1)}, u32[]{:S(2)}, u32[]{:S(2)}) async-start(f32[128,2,8,256]{3,2,1,0:T(8,128)} %bitcast.11), calls=%async_computation.1 | async-start | bytes 4194304 | tf_op jit(solution)/shard_map/all_to_all | solution.py:488
  102.5 11.9 %prepare.1 = (f32[4,256,256]{2,1,0:T(8,128)}, f32[4,256,256]{2,1,0:T(8,128)}, f32[4,256,256]{2,1,0:T(8,128)}, f32[4,256,256]{2,1,0:T(8,128)}, f32[4,256,256]{2,1...) custom-call(s32[2]{0:T(128)} %pad_add_fusion.ids, ...), custom_call_target="tpu_custom_call" | custom-call | flops 6000000000 | bytes 17825792 | tf_op jit(solution)/shard_map/prepare/pallas_call | solution.py:221
  114.4 18.5 %all-to-all-done.1.xs = f32[128,2,8,256]{3,2,1,0:T(8,128)S(1)} async-done(((f32[128,2,8,256]{3,2,1,0:T(8,128)}), f32[128,2,8,256]{3,2,1,0:T(8,128)S(1)}, u32[]{:S(2)}, u32[]{:S(2)}) %all-to-all-start.1) | async-done | bytes 2097184 | tf_op jit(solution)/shard_map/all_to_all | solution.py:488
  132.9 0.0 copy-start.2
  132.9 1.3 copy-done.2
  134.2 13.3 %slab_middle.1 = (f32[128,2,8,256]{3,2,1,0:T(8,128)}, f32[4,256,256]{2,1,0:T(8,128)}, f32[4,256,256]{2,1,0:T(8,128)}, f32[4,256,256]{2,1,0:T(8,128)}) custom-call(s32[2]{0:T(128)} %pad_add_fusion.ids, f32[128,2,8,256]{3,2,1,0:T(8,128)} %copy-done.2, f32[4,256,256]{2,1,0:T(8,128)} %c.7, f32[4,256,256]{2,1,0:T(8,128)} %rho.7, f32[4,256,256]{2,1,0:T(8,128)} %alpha.5, ...), custom_call_target="tpu_custom_call" | custom-call | flops 3200000000 | bytes 22020096 | tf_op jit(solution)/shard_map/slab_middle/pallas_call | solution.py:357
  147.6 36.0 %all_to_all.21 = f32[128,2,8,256]{3,2,1,0:T(8,128)} all-to-all(f32[128,2,8,256]{3,2,1,0:T(8,128)} %get-tuple-element.32), channel_id=1, replica_groups=mesh['emit'=2,'slab'=64] {'emit','slab'}, dimensions={0} | all-to-all | bytes 4194304 | tf_op jit(solution)/shard_map/all_to_all | solution.py:488
  183.6 8.4 %lines_adjoint.1 = f32[2,64,24,128]{3,2,1,0:T(8,128)} custom-call(s32[2]{0:T(128)} %pad_add_fusion.ids, f32[2,64,2,8,256]{4,3,2,1,0:T(8,128)} %bitcast.9, f32[2,2,256,256]{3,2,1,0:T(8,128)} %get-tuple-element.33.ux, f32[2,2,256,256]{3,2,1,0:T(8,128)} %get-tuple-element.34.bk, f32[2,2,256,256]{3,2,1,0:T(8,128)} %get-tuple-element.35.gx0, ...), custom_call_target="tpu_custom_call" | custom-call | flops 1200000000 | bytes 9437184 | tf_op jit(solution)/shard_map/lines_adjoint/pallas_call | solution.py:408
  192.0 30.3 %all_to_all.22.xs = f32[128,24,128]{2,1,0:T(8,128)} all-to-all(f32[128,24,128]{2,1,0:T(8,128)} %bitcast.10), channel_id=1, replica_groups=mesh['emit'=2,'slab'=64] {'emit','slab'}, dimensions={0} | all-to-all | bytes 3145728 | tf_op jit(solution)/shard_map/all_to_all | solution.py:488
  222.3 3.7 %slab_last_bulk.1 = (f32[4,256,256]{2,1,0:T(8,128)}, f32[4,256,256]{2,1,0:T(8,128)}) custom-call(s32[2]{0:T(128)} %pad_add_fusion.ids, f32[128,24,128]{2,1,0:T(8,128)} %all_to_all.22.xs, f32[4,256,256]{2,1,0:T(8,128)} %get-tuple-element.37.d0, f32[4,256,256]{2,1,0:T(8,128)} %get-tuple-element.38.t1), custom_call_target="tpu_custom_call" | custom-call | flops 1000000 | bytes 5242880 | tf_op jit(solution)/shard_map/slab_last_bulk/pallas_call | solution.py:434
  226.0 0.0 copy-start.3
  226.0 0.0 copy-start
  226.0 0.0 copy-start.1
  226.0 6.6 %slab_last_buoy.1 = f32[4,256,256]{2,1,0:T(8,128)} custom-call(s32[2]{0:T(128)} %pad_add_fusion.ids, f32[128,24,128]{2,1,0:T(8,128)} %all_to_all.22.xs, f32[4,256,256]{2,1,0:T(8,128)} %get-tuple-element.40.p0, f32[4,256,256]{2,1,0:T(8,128)} %c.7, f32[4,256,256]{2,1,0:T(8,128)} %rho.7, f32[4,256,256]{2,1,0:T(8,128)} %get-tuple-element.41.t2, ...), custom_call_target="tpu_custom_call" | custom-call | flops 800000000 | bytes 8388608 | tf_op jit(solution)/shard_map/slab_last_buoy/pallas_call | solution.py:470
  232.6 0.5 collective-permute-start.1
  233.1 0.0 copy-done.3
  233.1 3.0 %collective-permute-start = (f32[4,256,256]{2,1,0:T(8,128)S(1)}, f32[4,256,256]{2,1,0:T(8,128)S(1)}, u32[]{:S(2)}, u32[]{:S(2)}) collective-permute-start(f32[4,256,256]{2,1,0:T(8,128)S(1)} %copy-done.3), channel_id=1, source_target_pairs={{0,64},{64,0},{1,65},{65,1},{2,66},{66,2},{3,67},{67,3},{4,68},{68... | collective-permute-start | bytes 3145736 | tf_op jit(solution)/shard_map/ppermute | solution.py:492
  236.1 24.3 %collective-permute-done.1 = f32[4,256,256]{2,1,0:T(8,128)S(1)} collective-permute-done((f32[4,256,256]{2,1,0:T(8,128)}, f32[4,256,256]{2,1,0:T(8,128)S(1)}, u32[]{:S(2)}, u32[]{:S(2)}) %collective-permute-start.1) | collective-permute-done | bytes 1048608 | tf_op jit(solution)/shard_map/ppermute | solution.py:492
  260.4 20.8 %collective-permute-done = f32[4,256,256]{2,1,0:T(8,128)S(1)} collective-permute-done((f32[4,256,256]{2,1,0:T(8,128)S(1)}, f32[4,256,256]{2,1,0:T(8,128)S(1)}, u32[]{:S(2)}, u32[]{:S(2)}) %collective-permute-start) | collective-permute-done | bytes 1048608 | tf_op jit(solution)/shard_map/ppermute | solution.py:492
  281.2 0.0 copy-done
  281.2 0.0 copy-done.1
  281.2 3.0 %fusion.1 = (f32[4,256,256]{2,1,0:T(8,128)}, f32[4,256,256]{2,1,0:T(8,128)}) fusion(f32[4,256,256]{2,1,0:T(8,128)S(1)} %copy-done, f32[4,256,256]{2,1,0:T(8,128)S(1)} %copy-done.1, f32[4,256,256]{2,1,0:T(8,128)} %slab_last_buoy.1, f32[4,256,256]{2,1,0:T(8,128)S(1)} %collective-permute-done.1, f32[4,256,256]{2,1,0:T(8,128)S(1)} %copy-done.3, ...), kind=kLoop, calls=%fused_computation.3 | loop fusion | flops 3145728 | bytes 8388608 | tf_op jit(solution)/shard_map/mul | solution.py:536
Async XLA Ops:
  95.1 37.8 %all-to-all-start.1 = ((f32[128,2,8,256]{3,2,1,0:T(8,128)}), f32[128,2,8,256]{3,2,1,0:T(8,128)S(1)}, u32[]{:S(2)}, u32[]{:S(2)}) async-start(f32[128,2,8,256]{3,2,1,0:T(8,128)} %bitcast.11), calls=%async_computation.1 | async-start | bytes 4194304 | tf_op jit(solution)/shard_map/all_to_all | solution.py:488
  132.9 1.3 copy-start.2
  226.0 7.1 %copy-start.3 = (f32[4,256,256]{2,1,0:T(8,128)S(1)}, f32[4,256,256]{2,1,0:T(8,128)}, u32[]{:S(2)}) copy-start(f32[4,256,256]{2,1,0:T(8,128)} %get-tuple-element.39) | copy-start | bytes 3145732
  226.0 55.2 %copy-start = (f32[4,256,256]{2,1,0:T(8,128)S(1)}, f32[4,256,256]{2,1,0:T(8,128)}, u32[]{:S(2)}) copy-start(f32[4,256,256]{2,1,0:T(8,128)} %c.7) | copy-start | bytes 3145732
  226.0 55.2 %copy-start.1 = (f32[4,256,256]{2,1,0:T(8,128)S(1)}, f32[4,256,256]{2,1,0:T(8,128)}, u32[]{:S(2)}) copy-start(f32[4,256,256]{2,1,0:T(8,128)} %rho.7) | copy-start | bytes 3145732
  232.6 27.8 %collective-permute-start.1 = (f32[4,256,256]{2,1,0:T(8,128)}, f32[4,256,256]{2,1,0:T(8,128)S(1)}, u32[]{:S(2)}, u32[]{:S(2)}) collective-permute-start(f32[4,256,256]{2,1,0:T(8,128)} %slab_last_buoy.1), channel_id=1, source_target_pairs={{0,64},{64,0},{1,65},{65,1},{2,66},{66,2},{3,67},{67,3},{4,68},{68... | collective-permute-start | bytes 3145736 | tf_op jit(solution)/shard_map/ppermute | solution.py:492
  233.1 48.1 %collective-permute-start = (f32[4,256,256]{2,1,0:T(8,128)S(1)}, f32[4,256,256]{2,1,0:T(8,128)S(1)}, u32[]{:S(2)}, u32[]{:S(2)}) collective-permute-start(f32[4,256,256]{2,1,0:T(8,128)S(1)} %copy-done.3), channel_id=1, source_target_pairs={{0,64},{64,0},{1,65},{65,1},{2,66},{66,2},{3,67},{67,3},{4,68},{68... | collective-permute-start | bytes 3145736 | tf_op jit(solution)/shard_map/ppermute | solution.py:492

commit v4 on v3

v4 whole, which is shorter than its diff:
```python
import numpy as np
import jax
import jax.numpy as jnp
from jax import lax
from jax.experimental import pallas as pl
from jax.experimental.pallas import tpu as pltpu
from jax.sharding import PartitionSpec as P

STEPS = 2
DT = 0.2
F32 = jnp.float32
BF16 = jnp.bfloat16
ALL = ("emit", "slab")
MIB = 2**20
LIMIT = {"start": 60, "prepare": 60, "forward": 16, "middle": 14, "adjoint": 14, "last": 12}


def deriv_matrix(n):
    k = np.arange(1, n // 2, dtype=np.int64)
    pts = np.arange(n, dtype=np.int64)
    shifted = (k[None, :] * (2 * pts[:, None] + 1)) % (2 * n) * (np.pi / n)
    plain = (k[None, :] * (2 * pts[:, None])) % (2 * n) * (np.pi / n)
    w = k * (2.0 * np.pi / n)
    m = (np.cos(shifted) * w) @ np.sin(plain).T - (np.sin(shifted) * w) @ np.cos(plain).T
    return m * (2.0 / n)


def pair_const(m):
    m = m.astype(np.float32)
    return [jnp.asarray(m), jnp.asarray(np.ascontiguousarray(m.T))]


def split2(v):
    hi = v.astype(BF16)
    return hi, (v - hi.astype(F32)).astype(BF16)


def split3(v):
    hi = v.astype(BF16)
    rest = v - hi.astype(F32)
    mid = rest.astype(BF16)
    return hi, mid, (rest - mid.astype(F32)).astype(BF16)


def dot(a, b):
    return jnp.dot(a, b, preferred_element_type=F32)


def split_mats(gm, tm, ms):
    for k, m in enumerate((gm, tm)):
        ms[2 * k], ms[2 * k + 1] = split2(m[...])


G, T = 0, 2


def left(ms, k, v):
    h, l = split2(v)
    return dot(ms[k], h) + (dot(ms[k], l) + dot(ms[k + 1], h))


def right(v, ms, k):
    h, l = split2(v)
    return dot(h, ms[k]) + (dot(l, ms[k]) + dot(h, ms[k + 1]))


def mats_scratch(mats):
    return pltpu.VMEM((4,) + mats[0].shape, BF16)


def params(mib, n_grid=1):
    return pltpu.CompilerParams(
        dimension_semantics=("arbitrary",) * n_grid, vmem_limit_bytes=mib * MIB
    )


def cost(mflop, mib):
    return pl.CostEstimate(flops=mflop * 10**6, bytes_accessed=mib * MIB, transcendentals=0)


def swap(v):
    return jnp.swapaxes(v, 0, 1)


def whole(shape):
    return pl.BlockSpec(shape, lambda i, ids: (0,) * len(shape))


def group_plane(shape, pick, a=0):
    block = (None,) * (len(shape) - 3) + (1,) + shape[-2:]
    return pl.BlockSpec(block, lambda i, ids: (0, a)[: len(shape) - 3] + (pick(i, ids), 0, 0))


def plane_onehot(pos, plane, ny, nz):
    local = pos - plane * (ny * nz)
    y = lax.broadcasted_iota(jnp.int32, (ny, pos.shape[1]), 0) * nz
    return jnp.where((local >= y) & (local < y + nz), 1.0, 0.0).astype(BF16)


def column_onehot(pos, nz):
    z = lax.broadcasted_iota(jnp.int32, (nz, pos.shape[1]), 0)
    return lax.rem(pos, nz) == z


def drive_at(delay, drive, step):
    amp = jnp.zeros(delay.shape, F32)
    for k in range(drive.shape[0]):
        amp = jnp.where(delay + step == k, drive[k], amp)
    return amp


def three(onehot, value):
    return jnp.concatenate(
        [jnp.where(onehot, v.astype(F32), 0.0).astype(BF16) for v in split3(value)], axis=0
    )


def spread(rows, cols):
    return lax.dot_general(rows, cols, (((1,), (1,)), ((), ())), preferred_element_type=F32)


def sum3(v):
    n = v.shape[1] // 3
    return v[:, :n] + v[:, n : 2 * n] + v[:, 2 * n :]


def first_step(c, rho, alpha, p0, uy, uz, epos, cols, plane, ms):
    ny, nz = p0.shape[1], p0.shape[2]
    dens, speed, p = rho[0], c[0], p0[0]
    b = 1.0 / dens
    bulk = dens * speed * speed
    gy = left(ms, G, p)
    gz = right(p, ms, T)
    wy = uy[0] - DT * b * gy
    wz = uz[0] - DT * b * gz
    yz = left(ms, T, wy) + right(wz, ms, G)
    shot = sum3(spread(plane_onehot(epos[...], plane, ny, nz), cols[...]))
    v = (1.0 - DT * alpha[0]) * p + (DT * bulk) * yz + shot
    return gy, gz, wy, wz, yz, v, b, bulk


def start_kernel(
    ids, drive, c, rho, alpha, p0, ux, uy, uz, vx, epos, delay, gm, tm, buf, mat, cols, pack, ms
):
    i = pl.program_id(0)
    ny, nz = p0.shape[1], p0.shape[2]
    half = ny // 2

    @pl.when(i == 0)
    def _():
        split_mats(gm, tm, ms)
        cols[...] = three(column_onehot(epos[...], nz), drive_at(delay[...], drive, 0))

    @pl.when(i < 4)
    def _():
        _, _, _, _, _, v, b, bulk = first_step(
            c, rho, alpha, p0, uy, uz, epos, cols, ids[1] * 4 + i, ms
        )
        for f, field in enumerate((p0[0], ux[0], v, vx[0])):
            pack[2 * f : 2 * f + 2] = field.reshape(2, half, nz)
        buf[:, 0] = swap(pack[...])
        for xm in range(2):

            @pl.when(i == 2 * ids[0] + xm)
            def _():
                mat[4 * xm : 4 * xm + 2] = b.reshape(2, half, nz)
                mat[4 * xm + 2 : 4 * xm + 4] = bulk.reshape(2, half, nz)

    @pl.when(i == 4)
    def _():
        buf[:, 0] = swap(mat[...])


def start_call(ids, c, rho, alpha, p0, u, v, epos, delay, drive, mats, ndev):
    nx, ny, nz = c.shape
    pick = lambda i, ids: jnp.minimum(i, nx - 1)
    plane = group_plane(c.shape, pick)
    n_e = epos.shape[1]
    return pl.pallas_call(
        start_kernel,
        grid_spec=pltpu.PrefetchScalarGridSpec(
            num_scalar_prefetch=1,
            grid=(nx + 1,),
            in_specs=[pl.BlockSpec(memory_space=pltpu.SMEM)] + [plane] * 3
            + [group_plane(p0.shape, pick)]
            + [group_plane(u.shape, pick, a) for a in (0, 1, 2, 0)]
            + [whole((1, n_e))] * 2 + [whole((ny, ny))] * 2,
            out_specs=pl.BlockSpec((ndev, 1, 8, nz), lambda i, ids: (0, i, 0, 0)),
            scratch_shapes=[pltpu.VMEM((8, ndev, nz), F32), pltpu.VMEM((3 * nz, n_e), BF16),
                            pltpu.VMEM((8, ndev, nz), F32), mats_scratch(mats)],
        ),
        out_shape=jax.ShapeDtypeStruct((ndev, 5, 8, nz), F32),
        compiler_params=params(LIMIT["start"]),
        cost_estimate=cost(2000, 13),
        name="start",
    )(ids, drive, c, rho, alpha, p0, u, u, u, v, epos, delay, *mats)


def prepare_kernel(
    ids, drive, c, rho, alpha, p0, uy, uz, pa, ay, az, spos, rec, epos, delay, gm, tm,
    dk, stay, b, pm, cdk, wb, yz1, yz0, gsy, gsz, gy0, gz0, scols, ecols, ms,
):
    i = pl.program_id(0)
    ny, nz = c.shape[1], c.shape[2]

    @pl.when(i == 0)
    def _():
        split_mats(gm, tm, ms)
        oh = column_onehot(spos[...], nz)
        scols[:nz] = jnp.where(oh, 1.0, 0.0).astype(BF16)
        scols[nz : 4 * nz] = three(oh, rec[0:1])
        scols[4 * nz :] = three(oh, rec[1:2])
        for step in range(STEPS):
            ecols[step] = three(column_onehot(epos[...], nz), drive_at(delay[...], drive, step))

    plane = ids[1] * 4 + i
    gy, gz, u1y, u1z, yz0[0], v0, buoy, bulk = first_step(
        c, rho, alpha, p0, uy, uz, epos, ecols.at[0], plane, ms
    )
    keep = 1.0 - DT * alpha[0]
    s = plane_onehot(spos[...], plane, ny, nz)
    count = spread(s, scols[:nz])
    m0 = sum3(spread(s, scols[nz : 4 * nz]))
    m1 = sum3(spread(s, scols[4 * nz :]))
    shot = sum3(spread(plane_onehot(epos[...], plane, ny, nz), ecols[1]))
    gyv = left(ms, G, v0)
    gzv = right(v0, ms, T)
    db = DT * buoy
    yz = left(ms, T, u1y - db * gyv) + right(u1z - db * gzv, ms, G)
    back = left(ms, T, buoy * ay[0]) + right(buoy * az[0], ms, G)
    dk[0] = DT * bulk
    stay[0] = keep
    b[0] = buoy
    cdk[0] = count * (DT * bulk)
    pm[0] = pa[0] + (count * (keep * v0 + (DT * bulk) * yz + shot) - m1)
    wb[0] = (count * v0 - m0) - DT * back
    yz1[0] = yz
    gsy[0] = gy + gyv
    gsz[0] = gz + gzv
    gy0[0] = gy
    gz0[0] = gz


def prepare_call(ids, c, rho, alpha, p0, u, pa, v, spos, rec, epos, delay, drive, mats):
    nx, ny, nz = c.shape
    n_e, n_s = epos.shape[1], spos.shape[1]
    pick = lambda i, ids: i
    plane = group_plane(c.shape, pick)
    return pl.pallas_call(
        prepare_kernel,
        grid_spec=pltpu.PrefetchScalarGridSpec(
            num_scalar_prefetch=1,
            grid=(nx,),
            in_specs=[pl.BlockSpec(memory_space=pltpu.SMEM)] + [plane] * 3
            + [group_plane(p0.shape, pick)] + [group_plane(u.shape, pick, a) for a in (1, 2)]
            + [group_plane(pa.shape, pick)] + [group_plane(v.shape, pick, a) for a in (1, 2)]
            + [whole((1, n_s)), pl.BlockSpec((None, STEPS, n_s), lambda i, ids: (0, 0, 0)),
               whole((1, n_e)), whole((1, n_e))] + [whole((ny, ny))] * 2,
            out_specs=[plane] * 12,
            scratch_shapes=[pltpu.VMEM((7 * nz, n_s), BF16), pltpu.VMEM((STEPS, 3 * nz, n_e), BF16),
                            mats_scratch(mats)],
        ),
        out_shape=[jax.ShapeDtypeStruct(c.shape, F32)] * 12,
        compiler_params=params(LIMIT["prepare"]),
        cost_estimate=cost(8000, 22),
        name="prepare",
    )(ids, drive, c, rho, alpha, p0, u, u, pa, v, v, spos, rec, epos, delay, *mats)


def on_chip(kernel, args, shapes, scratch, limit, estimate, name, away=0):
    vmem = pl.BlockSpec(memory_space=pltpu.VMEM)
    return pl.pallas_call(
        kernel,
        in_specs=[pl.BlockSpec(memory_space=pl.ANY)] * away + [vmem] * (len(args) - away),
        out_specs=[vmem] * len(shapes),
        out_shape=[jax.ShapeDtypeStruct(v, F32) for v in shapes],
        scratch_shapes=[pltpu.VMEM(v, F32) for v in scratch] + [mats_scratch(args[-2:])],
        compiler_params=pltpu.CompilerParams(vmem_limit_bytes=limit * MIB),
        cost_estimate=estimate,
        name=name,
    )(*args)


def unpack(block, dst, first):
    t = swap(block)
    n = t.shape[1]
    for xm in range(2):
        dst[:, (first + xm) * n : (first + xm + 1) * n, :] = t[4 * xm : 4 * xm + 4]


def forward_kernel(ready, lines, gm, tm, out, gx0, gx1, ax, bk, f_s, o_s, ms):
    n = lines.shape[1]
    split_mats(gm, tm, ms)
    for e in range(2):
        unpack(lines[e, :, 4], bk, 2 * e)

    @pl.loop(0, 2)
    def _(g):
        for xl in range(4):
            rows = slice(xl * n, (xl + 1) * n)
            t = swap(lines[g, :, xl])
            f_s[g, :, rows, :] = t[:6]
            ax[pl.ds(2 * g, 2), rows, :] = t[6:]

    @pl.loop(0, 4)
    def _(j):
        g, yl = j // 2, lax.rem(j, 2)
        b = DT * bk[yl]
        g0 = left(ms, G, f_s[g, yl])
        u1 = f_s[g, 2 + yl] - b * g0
        x0 = left(ms, T, u1)
        g1 = left(ms, G, f_s[g, 4 + yl] + (DT * bk[2 + yl]) * x0)
        gx0[j] = g0
        gx1[j] = g1
        o_s[g, yl] = x0
        o_s[g, 2 + yl] = left(ms, T, u1 - b * g1)

    @pl.loop(0, 2)
    def _(g):
        for h in range(2):
            both = [o_s[g, :, (2 * h + xm) * n : (2 * h + xm + 1) * n, :] for xm in range(2)]
            out[g, :, h] = swap(jnp.concatenate(both, axis=0))


def forward_call(ready, lines, mats):
    _, ns, _, _, nz = lines.shape
    nx = 4 * ns
    full = (4, nx, nz)
    return on_chip(
        forward_kernel, (ready, lines, *mats), [(2, ns, 2, 8, nz), full, full, full, full],
        [(2, 6, nx, nz), (2, 4, nx, nz)], LIMIT["forward"], cost(1600, 11), "lines_forward", 1,
    )


def middle_kernel(
    xs, dk, stay, b, pm, cdk, wb, yz1, yz0, gsy, gsz, v, gm, tm, buf, d0, t1, t2, x_s, o_s, ms
):
    nx, ny, nz = dk.shape
    split_mats(gm, tm, ms)
    for h in range(2):
        x_s[4 * h : 4 * h + 4] = swap(xs[:, h]).reshape(4, ny, nz)

    @pl.loop(0, nx)
    def _(i):
        x0 = x_s[2 * i]
        add = dk[i] * x0
        ey = left(ms, G, add)
        ez = right(add, ms, T)
        db = DT * b[i]
        rest = x_s[2 * i + 1] - (left(ms, T, db * ey) + right(db * ez, ms, G))
        adj = pm[i] + cdk[i] * (stay[i] * x0 + rest)
        q = dk[i] * adj
        fy = left(ms, G, q)
        fz = right(q, ms, T)
        back = left(ms, T, b[i] * fy) + right(b[i] * fz, ms, G)
        o_s[2 * i] = q
        o_s[2 * i + 1] = stay[i] * adj + (cdk[i] * x0 + wb[i]) - DT * back
        d0[i] = x0 + yz0[i]
        t1[i] = (yz1[i] + rest) * adj
        t2[i] = (gsy[i] + ey) * (v[0, 1, i] + fy) + (gsz[i] + ez) * (v[0, 2, i] + fz)

    for h in range(2):
        buf[:, h] = swap(o_s[4 * h : 4 * h + 4].reshape(8, ny // 2, nz))


def middle_call(xs, fields, v, mats):
    nat = fields[0].shape
    saved = (8,) + nat[1:]
    return on_chip(
        middle_kernel, (xs, *fields, v, *mats), [xs.shape, nat, nat, nat], [saved, saved],
        LIMIT["middle"], cost(3200, 18), "slab_middle",
    )


def adjoint_kernel(qw, ux, bk, gx0, gx1, gm, tm, out, f_s, p_s, bx_s, ms):
    split_mats(gm, tm, ms)
    n, nz = qw.shape[1], qw.shape[4]
    lanes = [slice(0, nz // 2), slice(nz // 2, nz)]

    @pl.loop(0, 2)
    def _(g):
        for h in range(2):
            unpack(qw[g, :, h], f_s.at[g], 2 * h)

    bx_s[...] = jnp.zeros_like(bx_s)

    @pl.loop(0, 4)
    def _(j):
        g, yl = j // 2, lax.rem(j, 2)
        ax = ux[j] + left(ms, G, f_s[g, yl])
        p0 = f_s[g, 2 + yl] - DT * left(ms, T, bk[yl] * ax)
        p_s[j] = p0
        bx_s[yl] += gx1[j] * ax + gx0[j] * (ax + left(ms, G, (DT * bk[2 + yl]) * p0))

    @pl.loop(0, 2)
    def _(g):
        for zh, z in enumerate(lanes):
            v = [p_s[pl.ds(2 * g, 2), xl * n : (xl + 1) * n, z] for xl in range(4)]
            out[g, :, 8 * zh : 8 * zh + 8, :] = swap(jnp.concatenate(v, axis=0))

    for e in range(2):
        v = [bx_s[:, (2 * e + xm) * n : (2 * e + xm + 1) * n, z] for z in lanes for xm in range(2)]
        out[e, :, 16:24, :] = swap(jnp.concatenate(v, axis=0))


def adjoint_call(qw, ux, bk, gx0, gx1, mats):
    _, ns, _, _, nz = qw.shape
    nx = 4 * ns
    return on_chip(
        adjoint_kernel, (qw, ux, bk, gx0, gx1, *mats), [(2, ns, 24, nz // 2)],
        [(2, 4, nx, nz), (4, nx, nz), (2, nx, nz)], LIMIT["adjoint"], cost(1200, 9), "lines_adjoint",
    )[0]


def last_kernel(ids, xs, d0, t1, t2, gy0, gz0, dk, gm, tm, out, p_s, bx_s, ms):
    split_mats(gm, tm, ms)
    nx, ny, nz = d0.shape
    half = nz // 2
    t = swap(xs[:, 16:24, :]).reshape(4, ny, half)
    for zh in range(2):
        z = slice(zh * half, (zh + 1) * half)
        p_s[:, :, z] = swap(xs[:, 8 * zh : 8 * zh + 8, :]).reshape(nx, ny, half)
        bx_s[:, :, z] = t[2 * zh : 2 * zh + 2]

    @pl.loop(0, nx)
    def _(i):
        p = p_s[i]
        q = dk[i] * p
        out[0, i] = t1[i] + d0[i] * p
        out[1, i] = t2[i] + gy0[i] * left(ms, G, q) + gz0[i] * right(q, ms, T)

    for xm in range(2):
        out[1, 2 * ids[0] + xm] += bx_s[xm]


def last_call(ids, xs, fields, mats):
    nat = fields[0].shape
    vmem = pl.BlockSpec(memory_space=pltpu.VMEM)
    args = (xs, *fields, *mats)
    return pl.pallas_call(
        last_kernel,
        in_specs=[pl.BlockSpec(memory_space=pltpu.SMEM)] + [vmem] * len(args),
        out_specs=vmem,
        out_shape=jax.ShapeDtypeStruct((2,) + nat, F32),
        scratch_shapes=[pltpu.VMEM(nat, F32), pltpu.VMEM((2,) + nat[1:], F32), mats_scratch(mats)],
        compiler_params=pltpu.CompilerParams(vmem_limit_bytes=LIMIT["last"] * MIB),
        cost_estimate=cost(800, 9),
        name="slab_last",
    )(ids, *args)


def change_layout(v):
    return lax.all_to_all(v, ALL, split_axis=0, concat_axis=0, tiled=True)


def swap_groups(v):
    return lax.ppermute(v, "emit", [(0, 1), (1, 0)])


def local(
    sound_speed, density, absorption, pressure_start, velocity_start, adjoint_pressure,
    adjoint_velocity, emitter_voxel, emitter_delay, drive_waveform_samples, recorded_pressures,
    sensor_flat_position,
):
    n_emit, n_slab = lax.axis_size("emit"), lax.axis_size("slab")
    ndev = n_emit * n_slab
    planes, ny, nz = sound_speed.shape
    nx = planes * n_slab
    emit = lax.axis_index("emit")
    ids = jnp.stack([emit, lax.axis_index("slab")]).astype(jnp.int32)
    mats = pair_const(deriv_matrix(ny))
    order = (4 * np.arange(n_slab)[None, :] + np.arange(4)[:, None]).reshape(-1)
    line_mats = pair_const(deriv_matrix(nx)[np.ix_(order, order)])

    buf = start_call(
        ids, sound_speed, density, absorption, pressure_start, velocity_start, adjoint_velocity,
        emitter_voxel, emitter_delay, drive_waveform_samples, mats, ndev,
    )
    fields = prepare_call(
        ids, sound_speed, density, absorption, pressure_start, velocity_start, adjoint_pressure,
        adjoint_velocity, sensor_flat_position.reshape(1, -1), recorded_pressures, emitter_voxel,
        emitter_delay, drive_waveform_samples, mats,
    )
    gy0, gz0, dk = fields[10], fields[11], fields[0]
    lines = change_layout(buf).reshape(n_emit, n_slab, 5, 8, nz)
    xs, gx0, gx1, ux, bk = forward_call(dk, lines, line_mats)
    xs = change_layout(xs.reshape(ndev, 2, 8, nz))
    qw, d0, t1, t2 = middle_call(xs, fields[:10], adjoint_velocity, mats)
    qw = change_layout(qw).reshape(n_emit, n_slab, 2, 8, nz)
    xs = adjoint_call(qw, ux, bk, gx0, gx1, line_mats)
    xs = change_layout(xs.reshape(ndev, 24, nz // 2))
    t = last_call(ids, xs, [d0, t1, t2, gy0, gz0, dk], mats)
    other = swap_groups(t)
    s1, s2 = t[0] + other[0], t[1] + other[1]
    b = 1.0 / density
    speed_total = (2.0 * DT) * s1 * density * sound_speed
    density_total = DT * (s1 * sound_speed * sound_speed + s2 * b * b)
    return speed_total, density_total


def solution(mesh):
    in_specs = (
        P("slab", None, None), P("slab", None, None), P("slab", None, None),
        P("emit", "slab", None, None), P("emit", None, "slab", None, None),
        P("emit", "slab", None, None), P("emit", None, "slab", None, None),
        P("emit", None), P("emit", None), P(), P("emit", None, None), P(),
    )
    out_specs = (P("slab", None, None), P("slab", None, None))
    return jax.shard_map(local, mesh=mesh, in_specs=in_specs, out_specs=out_specs, check_vma=False)
```

time: 285 us -> 271 us (0.951)
  blocking collectives: 142 us -> 104 us
  waiting for transfers between devices: 63.5 us -> 95.8 us
  Pallas kernels: 62.4 us -> 49.9 us
  local copies, waits for them, and re-layouts: 1.34 us -> 4.98 us
    all_to_all x3, blocking collectives: 142 us -> 104 us  [change_layout(): return lax.all_to_all(v, ALL, split_axis=0, concat_axis=0, tiled=True)]
    all_to_all x1, waiting for transfers between devices: 18.5 us -> 47.9 us  [change_layout(): return lax.all_to_all(v, ALL, split_axis=0, concat_axis=0, tiled=True)]
    pallas_call x5 -> x4, Pallas kernels: 41.3 us -> 24.5 us  [the longest x3 22 us: on_chip(): pl.pallas_call(kernel, in_specs=[pl.BlockSpec(memory_space=pl.ANY)] * awa...]
    all_to_all x1, starting transfers between devices: 7.46 us -> 11.6 us  [change_layout(): return lax.all_to_all(v, ALL, split_axis=0, concat_axis=0, tiled=True)]
    pallas_call x1, Pallas kernels: 11.9 us -> 16 us  [prepare_call(): pl.pallas_call(prepare_kernel, grid_spec=pltpu.PrefetchScalarGridSpec(num...]
    unnamed x8 -> x42, local copies, waits for them, and re-layouts: 1.34 us -> 4.98 us
    ppermute x2 -> x1, starting transfers between devices: 3.54 us -> 0.61 us  [swap_groups(): return lax.ppermute(v, 'emit', [(0, 1), (1, 0)])]
    ppermute x2 -> x1, waiting for transfers between devices: 45 us -> 47.9 us  [swap_groups(): return lax.ppermute(v, 'emit', [(0, 1), (1, 0)])]
  transfers between devices with their start and end apart: 3 -> 2, of which waited for: 3 -> 2; matrix products, arithmetic and copies ran while one was open for 0% -> 0% of each run, Pallas kernels for 4% -> 6%
where the time goes in v4:
time: 271 us; the launch traced here: 270 us
  blocking collectives  104 us (38%)
  waiting for transfers between devices  95.8 us (35%)
  Pallas kernels  49.9 us (18%)
  starting transfers between devices  12.2 us (5%)
  local copies, waits for them, and re-layouts  4.98 us (2%)
    all_to_all x3, blocking collectives, change_layout(): return lax.all_to_all(v, ALL, split_axis=0, concat_axis=0, tiled=True)  104 us
    all_to_all x1, waiting for transfers between devices, change_layout(): return lax.all_to_all(v, ALL, split_axis=0, concat_axis=0, tiled=True)  47.9 us
    ppermute x1, waiting for transfers between devices, swap_groups(): return lax.ppermute(v, 'emit', [(0, 1), (1, 0)])  47.9 us
    pallas_call x3, Pallas kernels, on_chip(): pl.pallas_call(kernel, in_specs=[pl.BlockSpec(memory_space=pl.ANY)] * awa...  22 us
    pallas_call x1, Pallas kernels, prepare_call(): pl.pallas_call(prepare_kernel, grid_spec=pltpu.PrefetchScalarGridSpec(num...  16 us
    all_to_all x1, starting transfers between devices, change_layout(): return lax.all_to_all(v, ALL, split_axis=0, concat_axis=0, tiled=True)  11.6 us
    pallas_call x1, Pallas kernels, start_call(): pl.pallas_call(start_kernel, grid_spec=pltpu.PrefetchScalarGridSpec(num_s...  9.39 us
  transfers between devices with their start and end apart: 2, of which 2 were waited for; matrix products, arithmetic and copies ran while one was open for 0% of the time, Pallas kernels for 6%

profile of v4, /device:TPU:0, one launch (start us, length us, event | category | flops | bytes accessed | tf_op | source)
XLA Modules:
  0.0 270.1 jit_solution(9409763691135122099)
XLA Ops:
  0.6 0.6 pad_add_fusion.ids
  1.2 9.4 %start.1 = f32[128,5,8,256]{3,2,1,0:T(8,128)} custom-call(s32[2]{0:T(128)} %pad_add_fusion.ids, f32[64]{0:T(128)} %drive.3, f32[4,256,256]{2,1,0:T(8,128)} %c.3, f32[4,256,256]{2,1,0:T(8,128)} %rho.3, f32[4,256,256]{2,1,0:T(8,128)} %alpha.3, f32[1,4,256,256]{3,2,1,0:T(8,128)} %p0.3, f32[1,3,4,256,256]{4,3,2,1,0:T(8,128)} %uz.3, f32[1,3,4,256,256]{4,3,2,1,0:T(8,128)} %uz.3, ...), custom_call_target="tpu_custom_call" | custom-call | flops 2000000000 | bytes 13631488 | tf_op jit(solution)/shard_map/start/pallas_call | solution.py:179
  10.6 11.6 %all-to-all-start = ((f32[128,5,8,256]{3,2,1,0:T(8,128)}), f32[128,5,8,256]{3,2,1,0:T(8,128)}, u32[]{:S(2)}, u32[]{:S(2)}) async-start(f32[128,5,8,256]{3,2,1,0:T(8,128)} %start.1), calls=%async_computation | async-start | bytes 10485760 | tf_op jit(solution)/shard_map/all_to_all | solution.py:453
  22.2 0.0 copy-start.16
  22.2 0.0 copy-start.17
  22.3 16.0 %prepare.1 = (f32[4,256,256]{2,1,0:T(8,128)}, f32[4,256,256]{2,1,0:T(8,128)}, f32[4,256,256]{2,1,0:T(8,128)}, f32[4,256,256]{2,1,0:T(8,128)}, f32[4,256,256]{2,1...) custom-call(s32[2]{0:T(128)} %pad_add_fusion.ids, ...), custom_call_target="tpu_custom_call" | custom-call | flops 8000000000 | bytes 23068672 | tf_op jit(solution)/shard_map/prepare/pallas_call | solution.py:249
  38.3 47.9 %all-to-all-done = f32[128,5,8,256]{3,2,1,0:T(8,128)} async-done(((f32[128,5,8,256]{3,2,1,0:T(8,128)}), f32[128,5,8,256]{3,2,1,0:T(8,128)}, u32[]{:S(2)}, u32[]{:S(2)}) %all-to-all-start) | async-done | bytes 5242912 | tf_op jit(solution)/shard_map/all_to_all | solution.py:453
  86.2 0.0 copy-done.16
  86.2 0.0 copy-done.17
  86.2 1.2 copy-done.1
  87.4 0.0 copy-start.7
  87.4 0.0 copy-start.8
  87.5 0.0 copy-start.9
  87.5 9.5 %lines_forward.1 = (f32[2,64,2,8,256]{4,3,2,1,0:T(8,128)S(1)}, f32[4,256,256]{2,1,0:T(8,128)S(1)}, f32[4,256,256]{2,1,0:T(8,128)S(1)}, f32[4,256,256]{2,1,0:T(8,128)S(1)}, f32[4,256,256]{2,1,0:T(8,128)S(1)}) custom-call(f32[4,256,256]{2,1,0:T(8,128)S(1)} %copy-done.1, f32[2,64,5,8,256]{4,3,2,1,0:T(8,128)} %bitcast.3.lines, f32[256,256]{1,0:T(8,128)S(1)} %copy-done.17, ...), custom_call_target="tpu_custom_call" | custom-call | flops 1600000000 | bytes 11534336 | tf_op jit(solution)/shard_map/lines_forward/pallas_call | solution.py:272
  97.0 0.0 copy-start
  97.0 0.0 copy-start.2
  97.0 39.7 %all_to_all.20.xs = f32[128,2,8,256]{3,2,1,0:T(8,128)S(1)} all-to-all(f32[128,2,8,256]{3,2,1,0:T(8,128)S(1)} %bitcast.19), channel_id=1, replica_groups=mesh['emit'=2,'slab'=64] {'emit','slab'}, dimensions={0} | all-to-all | bytes 4194304 | tf_op jit(solution)/shard_map/all_to_all | solution.py:453
  136.7 0.0 copy-done.3
  136.8 1.2 copy-done.11
  138.0 1.2 copy-done.12
  139.2 1.2 copy-done.13
  140.4 8.0 %slab_middle.1 = (f32[128,2,8,256]{3,2,1,0:T(8,128)S(1)}, f32[4,256,256]{2,1,0:T(8,128)S(1)}, f32[4,256,256]{2,1,0:T(8,128)S(1)}, f32[4,256,256]{2,1,0:T(8,128)S(1)}) custom-call(f32[128,2,8,256]{3,2,1,0:T(8,128)S(1)} %all_to_all.20.xs, f32[4,256,256]{2,1,0:T(8,128)S(1)} %copy-done.2, f32[4,256,256]{2,1,0:T(8,128)S(1)} %copy-done.5, ...), custom_call_target="tpu_custom_call" | custom-call | flops 3200000000 | bytes 18874368 | tf_op jit(solution)/shard_map/slab_middle/pallas_call | solution.py:272
  148.4 35.0 %all_to_all.21 = f32[128,2,8,256]{3,2,1,0:T(8,128)S(1)} all-to-all(f32[128,2,8,256]{3,2,1,0:T(8,128)S(1)} %get-tuple-element.34), channel_id=1, replica_groups=mesh['emit'=2,'slab'=64] {'emit','slab'}, dimensions={0} | all-to-all | bytes 4194304 | tf_op jit(solution)/shard_map/all_to_all | solution.py:453
  183.4 4.5 %lines_adjoint.1 = f32[2,64,24,128]{3,2,1,0:T(8,128)S(1)} custom-call(f32[2,64,2,8,256]{4,3,2,1,0:T(8,128)S(1)} %bitcast.17, f32[4,256,256]{2,1,0:T(8,128)S(1)} %get-tuple-element.35.ux, f32[4,256,256]{2,1,0:T(8,128)S(1)} %get-tuple-element.36.bk, f32[4,256,256]{2,1,0:T(8,128)S(1)} %get-tuple-element.37.gx0, f32[4,256,256]{2,1,0:T(8,128)S(1)} %get-tuple-element.38.gx1, ...), custom_call_target="tpu_custom_call" | custom-call | flops 1200000000 | bytes 9437184 | tf_op jit(solution)/shard_map/lines_adjoint/pallas_call | solution.py:272
  188.0 29.4 %all_to_all.22.xs = f32[128,24,128]{2,1,0:T(8,128)S(1)} all-to-all(f32[128,24,128]{2,1,0:T(8,128)S(1)} %bitcast.18), channel_id=1, replica_groups=mesh['emit'=2,'slab'=64] {'emit','slab'}, dimensions={0} | all-to-all | bytes 3145728 | tf_op jit(solution)/shard_map/all_to_all | solution.py:453
  217.4 0.0 copy-start.19
  217.4 0.0 copy-start.20
  217.4 2.5 slab_last.1
  219.9 0.6 collective-permute-start
  220.5 47.9 %collective-permute-done = f32[2,4,256,256]{3,2,1,0:T(8,128)S(1)} collective-permute-done((f32[2,4,256,256]{3,2,1,0:T(8,128)S(1)}, f32[2,4,256,256]{3,2,1,0:T(8,128)S(1)}, u32[]{:S(2)}, u32[]{:S(2)}) %collective-permute-start) | collective-permute-done | bytes 2097184 | tf_op jit(solution)/shard_map/ppermute | solution.py:457
  268.4 0.0 copy-done.20
  268.4 1.8 fusion.1
  (25 shorter events, 0.0 us)
Async XLA Ops:
  10.6 75.6 %all-to-all-start = ((f32[128,5,8,256]{3,2,1,0:T(8,128)}), f32[128,5,8,256]{3,2,1,0:T(8,128)}, u32[]{:S(2)}, u32[]{:S(2)}) async-start(f32[128,5,8,256]{3,2,1,0:T(8,128)} %start.1), calls=%async_computation | async-start | bytes 10485760 | tf_op jit(solution)/shard_map/all_to_all | solution.py:453
  22.2 64.0 %copy-start.16 = (f32[256,256]{1,0:T(8,128)S(1)}, f32[256,256]{1,0:T(8,128)}, u32[]{:S(2)}) copy-start(f32[256,256]{1,0:T(8,128)} %constant.26.clone.tm) | copy-start | bytes 786436
  22.2 64.0 %copy-start.17 = (f32[256,256]{1,0:T(8,128)S(1)}, f32[256,256]{1,0:T(8,128)}, u32[]{:S(2)}) copy-start(f32[256,256]{1,0:T(8,128)} %constant.25.clone.gm) | copy-start | bytes 786436
  86.2 1.2 copy-start.1
  87.4 49.3 %copy-start.3 = (f32[256,256]{1,0:T(8,128)S(1)}, f32[256,256]{1,0:T(8,128)}, u32[]{:S(2)}) copy-start(f32[256,256]{1,0:T(8,128)} %constant.24.clone.tm) | copy-start | bytes 786436
  87.4 49.3 %copy-start.4 = (f32[256,256]{1,0:T(8,128)S(1)}, f32[256,256]{1,0:T(8,128)}, u32[]{:S(2)}) copy-start(f32[256,256]{1,0:T(8,128)} %constant.23.clone.gm) | copy-start | bytes 786436
  87.4 49.3 %copy-start.5 = (f32[4,256,256]{2,1,0:T(8,128)S(1)}, f32[4,256,256]{2,1,0:T(8,128)}, u32[]{:S(2)}) copy-start(f32[4,256,256]{2,1,0:T(8,128)} %get-tuple-element.25.stay) | copy-start | bytes 3145732
  87.4 49.3 %copy-start.6 = (f32[4,256,256]{2,1,0:T(8,128)S(1)}, f32[4,256,256]{2,1,0:T(8,128)}, u32[]{:S(2)}) copy-start(f32[4,256,256]{2,1,0:T(8,128)} %get-tuple-element.26.b) | copy-start | bytes 3145732
  87.4 49.3 %copy-start.7 = (f32[4,256,256]{2,1,0:T(8,128)S(1)}, f32[4,256,256]{2,1,0:T(8,128)}, u32[]{:S(2)}) copy-start(f32[4,256,256]{2,1,0:T(8,128)} %get-tuple-element.27.pm) | copy-start | bytes 3145732
  87.4 49.3 %copy-start.8 = (f32[4,256,256]{2,1,0:T(8,128)S(1)}, f32[4,256,256]{2,1,0:T(8,128)}, u32[]{:S(2)}) copy-start(f32[4,256,256]{2,1,0:T(8,128)} %get-tuple-element.28.cdk) | copy-start | bytes 3145732
  87.5 49.3 %copy-start.9 = (f32[4,256,256]{2,1,0:T(8,128)S(1)}, f32[4,256,256]{2,1,0:T(8,128)}, u32[]{:S(2)}) copy-start(f32[4,256,256]{2,1,0:T(8,128)} %get-tuple-element.29.wb) | copy-start | bytes 3145732
  87.5 49.3 %copy-start.10 = (f32[4,256,256]{2,1,0:T(8,128)S(1)}, f32[4,256,256]{2,1,0:T(8,128)}, u32[]{:S(2)}) copy-start(f32[4,256,256]{2,1,0:T(8,128)} %get-tuple-element.30.yz1) | copy-start | bytes 3145732
  97.0 39.8 %copy-start = (f32[1,3,4,256,256]{4,3,2,1,0:T(8,128)S(1)}, f32[1,3,4,256,256]{4,3,2,1,0:T(8,128)}, u32[]{:S(2)}) copy-start(f32[1,3,4,256,256]{4,3,2,1,0:T(8,128)} %v.1) | copy-start | bytes 9437188
  97.0 39.8 %copy-start.2 = (f32[4,256,256]{2,1,0:T(8,128)S(1)}, f32[4,256,256]{2,1,0:T(8,128)}, u32[]{:S(2)}) copy-start(f32[4,256,256]{2,1,0:T(8,128)} %get-tuple-element.23.ready.dk) | copy-start | bytes 3145732
  136.8 1.2 copy-start.11
  138.0 1.2 copy-start.12
  139.2 1.2 copy-start.13
  188.0 29.4 %copy-start.14 = (f32[4,256,256]{2,1,0:T(8,128)S(1)}, f32[4,256,256]{2,1,0:T(8,128)}, u32[]{:S(2)}) copy-start(f32[4,256,256]{2,1,0:T(8,128)} %get-tuple-element.42.gy0) | copy-start | bytes 3145732
  188.0 29.4 %copy-start.15 = (f32[4,256,256]{2,1,0:T(8,128)S(1)}, f32[4,256,256]{2,1,0:T(8,128)}, u32[]{:S(2)}) copy-start(f32[4,256,256]{2,1,0:T(8,128)} %get-tuple-element.43.gz0) | copy-start | bytes 3145732
  188.0 29.4 %copy-start.18 = (s32[2]{0:T(128)S(1)}, s32[2]{0:T(128)}, u32[]{:S(2)}) copy-start(s32[2]{0:T(128)} %pad_add_fusion.ids) | copy-start | bytes 28
  217.4 51.0 %copy-start.19 = (f32[4,256,256]{2,1,0:T(8,128)S(1)}, f32[4,256,256]{2,1,0:T(8,128)}, u32[]{:S(2)}) copy-start(f32[4,256,256]{2,1,0:T(8,128)} %c.3) | copy-start | bytes 3145732
  217.4 51.0 %copy-start.20 = (f32[4,256,256]{2,1,0:T(8,128)S(1)}, f32[4,256,256]{2,1,0:T(8,128)}, u32[]{:S(2)}) copy-start(f32[4,256,256]{2,1,0:T(8,128)} %rho.3) | copy-start | bytes 3145732
  219.9 48.5 %collective-permute-start = (f32[2,4,256,256]{3,2,1,0:T(8,128)S(1)}, f32[2,4,256,256]{3,2,1,0:T(8,128)S(1)}, u32[]{:S(2)}, u32[]{:S(2)}) collective-permute-start(f32[2,4,256,256]{3,2,1,0:T(8,128)S(1)} %slab_last.1), channel_id=1, source_target_pairs={{0,64},{64,0},{1,65},{65,1},{2,66},{66,2},{3,67},{67,3},{4,68},{68... | collective-permute-start | bytes 6291464 | tf_op jit(solution)/shard_map/ppermute | solution.py:457

commit v5 on v4

v5 whole, which is shorter than its diff:
```python
import numpy as np
import jax
import jax.numpy as jnp
from jax import lax
from jax.experimental import pallas as pl
from jax.experimental.pallas import tpu as pltpu
from jax.sharding import PartitionSpec as P

STEPS = 2
DT = 0.2
F32 = jnp.float32
BF16 = jnp.bfloat16
ALL = ("emit", "slab")
MIB = 2**20
LIMIT = {"start": 60, "prepare": 60, "forward": 24, "middle": 40, "adjoint": 20, "last": 20}


def deriv_matrix(n):
    k = np.arange(1, n // 2, dtype=np.int64)
    pts = np.arange(n, dtype=np.int64)
    shifted = (k[None, :] * (2 * pts[:, None] + 1)) % (2 * n) * (np.pi / n)
    plain = (k[None, :] * (2 * pts[:, None])) % (2 * n) * (np.pi / n)
    w = k * (2.0 * np.pi / n)
    m = (np.cos(shifted) * w) @ np.sin(plain).T - (np.sin(shifted) * w) @ np.cos(plain).T
    return m * (2.0 / n)


def pair_const(m):
    m = m.astype(np.float32)
    return [jnp.asarray(m), jnp.asarray(np.ascontiguousarray(m.T))]


def split2(v):
    hi = v.astype(BF16)
    return hi, (v - hi.astype(F32)).astype(BF16)


def split3(v):
    hi = v.astype(BF16)
    rest = v - hi.astype(F32)
    mid = rest.astype(BF16)
    return hi, mid, (rest - mid.astype(F32)).astype(BF16)


def dot(a, b):
    return jnp.dot(a, b, preferred_element_type=F32)


def split_mats(gm, tm, ms):
    for k, m in enumerate((gm, tm)):
        ms[2 * k], ms[2 * k + 1] = split2(m[...])


G, T = 0, 2


def left(ms, k, v):
    h, l = split2(v)
    return dot(ms[k], h) + (dot(ms[k], l) + dot(ms[k + 1], h))


def right(v, ms, k):
    h, l = split2(v)
    return dot(h, ms[k]) + (dot(l, ms[k]) + dot(h, ms[k + 1]))


def mats_scratch(mats):
    return pltpu.VMEM((4,) + mats[0].shape, BF16)


def params(mib, n_grid=1):
    return pltpu.CompilerParams(
        dimension_semantics=("arbitrary",) * n_grid, vmem_limit_bytes=mib * MIB
    )


def cost(mflop, mib):
    return pl.CostEstimate(flops=mflop * 10**6, bytes_accessed=mib * MIB, transcendentals=0)


def swap(v):
    return jnp.swapaxes(v, 0, 1)


def whole(shape):
    return pl.BlockSpec(shape, lambda i, ids: (0,) * len(shape))


def group_plane(shape, pick, a=0):
    block = (None,) * (len(shape) - 3) + (1,) + shape[-2:]
    return pl.BlockSpec(block, lambda i, ids: (0, a)[: len(shape) - 3] + (pick(i, ids), 0, 0))


def plane_onehot(pos, plane, ny, nz):
    local = pos - plane * (ny * nz)
    y = lax.broadcasted_iota(jnp.int32, (ny, pos.shape[1]), 0) * nz
    return jnp.where((local >= y) & (local < y + nz), 1.0, 0.0).astype(BF16)


def column_onehot(pos, nz):
    z = lax.broadcasted_iota(jnp.int32, (nz, pos.shape[1]), 0)
    return lax.rem(pos, nz) == z


def drive_at(delay, drive, step):
    amp = jnp.zeros(delay.shape, F32)
    for k in range(drive.shape[0]):
        amp = jnp.where(delay + step == k, drive[k], amp)
    return amp


def three(onehot, value):
    parts = [jnp.where(onehot, v.astype(F32), 0.0) for v in split3(value)]
    return jnp.concatenate(parts, axis=1).T.astype(BF16)


def spread(rows, cols):
    return dot(jnp.concatenate([rows] * 3, axis=1), cols)


def first_step(planes, cols, epos, numbers, ms):
    ny, nz = planes[0][0].shape
    c, rho, alpha, p, uy, uz = zip(*planes)
    at = range(len(planes))
    gy = [left(ms, G, v) for v in p]
    gz = [right(v, ms, T) for v in p]
    b = [1.0 / v for v in rho]
    bulk = [rho[k] * c[k] * c[k] for k in at]
    wy = [uy[k] - DT * b[k] * gy[k] for k in at]
    wz = [uz[k] - DT * b[k] * gz[k] for k in at]
    yz = [left(ms, T, v) for v in wy]
    zz = [right(v, ms, G) for v in wz]
    shot = [spread(plane_onehot(epos[...], n, ny, nz), cols[...]) for n in numbers]
    yz = [yz[k] + zz[k] for k in at]
    v0 = [(1.0 - DT * alpha[k]) * p[k] + (DT * bulk[k]) * yz[k] + shot[k] for k in at]
    return list(zip(gy, gz, wy, wz, yz, v0, b, bulk))


def plane_copies(srcs, dst, sems, i):
    return [
        pltpu.make_async_copy(src.at[pl.ds(i, 1)], dst.at[i, pl.ds(k, 1)], sems.at[i, k])
        for k, src in enumerate(srcs)
    ]


def start_kernel(
    drive, c, rho, alpha, p0, u, v, epos, delay, gm, tm, buf, ins, sems, outs, out_sems, mat, cols,
    pack, ms
):
    emit, slab = lax.axis_index("emit"), lax.axis_index("slab")
    nx, ny, nz = c.shape
    half = ny // 2

    def send(i):
        return pltpu.make_async_copy(outs.at[i], buf.at[:, i], out_sems.at[i])

    srcs = (p0.at[0], c, rho, alpha, u.at[0, 1], u.at[0, 2], u.at[0, 0], v.at[0, 0])
    for i in range(nx):
        for copy in plane_copies(srcs, ins, sems, i):
            copy.start()
    split_mats(gm, tm, ms)
    cols[...] = three(column_onehot(epos[...], nz), drive_at(delay[...], drive, 0))

    @pl.loop(0, nx // 2)
    def _(k):
        pair = (2 * k, 2 * k + 1)
        for i in pair:
            for copy in plane_copies(srcs, ins, sems, i):
                copy.wait()
        steps = first_step(
            [tuple(ins[i, f] for f in (1, 2, 3, 0, 4, 5)) for i in pair],
            cols, epos, [slab * nx + i for i in pair], ms,
        )
        for xm, i in enumerate(pair):
            v0, b, bulk = steps[xm][5:]
            for f, field in enumerate((ins[i, 0], ins[i, 6], v0, ins[i, 7])):
                pack[xm, 2 * f : 2 * f + 2] = field.reshape(2, half, nz)
            outs[i] = swap(pack[xm])
            send(i).start()

            @pl.when(k == emit)
            def _():
                mat[4 * xm : 4 * xm + 2] = b.reshape(2, half, nz)
                mat[4 * xm + 2 : 4 * xm + 4] = bulk.reshape(2, half, nz)

    outs[nx] = swap(mat[...])
    send(nx).start()
    for i in range(nx + 1):
        send(i).wait()


def start_call(c, rho, alpha, p0, u, v, epos, delay, drive, mats, ndev):
    nx, ny, nz = c.shape
    n_e = epos.shape[1]
    hbm, vmem, smem = (pl.BlockSpec(memory_space=m) for m in (pltpu.HBM, pltpu.VMEM, pltpu.SMEM))
    return pl.pallas_call(
        start_kernel,
        in_specs=[smem] + [hbm] * 6 + [vmem] * 4,
        out_specs=hbm,
        out_shape=jax.ShapeDtypeStruct((ndev, nx + 1, 8, nz), F32),
        scratch_shapes=[pltpu.VMEM((nx, 8, ny, nz), F32), pltpu.SemaphoreType.DMA((nx, 8)),
                        pltpu.VMEM((nx + 1, ndev, 8, nz), F32), pltpu.SemaphoreType.DMA((nx + 1,)),
                        pltpu.VMEM((8, ndev, nz), F32), pltpu.VMEM((3 * n_e, nz), BF16),
                        pltpu.VMEM((2, 8, ndev, nz), F32), mats_scratch(mats)],
        compiler_params=pltpu.CompilerParams(vmem_limit_bytes=LIMIT["start"] * MIB),
        cost_estimate=cost(2000, 13),
        name="start",
    )(drive, c, rho, alpha, p0, u, v, epos, delay, *mats)


def prepare_kernel(
    ids, drive, c, rho, alpha, p0, uy, uz, pa, ay, az, spos, rec, epos, delay, gm, tm,
    dk, stay, b, pm, cdk, wb, yz1, late, gy0, gz0, ones, scols, ecols, ms,
):
    i = pl.program_id(0)
    ny, nz = c.shape[1], c.shape[2]

    @pl.when(i == 0)
    def _():
        split_mats(gm, tm, ms)
        oh = column_onehot(spos[...], nz)
        ones[...] = jnp.where(oh, 1.0, 0.0).T.astype(BF16)
        for step in range(STEPS):
            scols[step] = three(oh, rec[step : step + 1])
        for step in range(STEPS):
            ecols[step] = three(column_onehot(epos[...], nz), drive_at(delay[...], drive, step))

    plane = ids[1] * 4 + i
    gy, gz, u1y, u1z, yz0, v0, buoy, bulk = first_step(
        [(c[0], rho[0], alpha[0], p0[0], uy[0], uz[0])], ecols.at[0], epos, [plane], ms
    )[0]
    keep = 1.0 - DT * alpha[0]
    s = plane_onehot(spos[...], plane, ny, nz)
    count = dot(s, ones[...])
    m0 = spread(s, scols[0])
    m1 = spread(s, scols[1])
    shot = spread(plane_onehot(epos[...], plane, ny, nz), ecols[1])
    gyv = left(ms, G, v0)
    gzv = right(v0, ms, T)
    db = DT * buoy
    yz = left(ms, T, u1y - db * gyv) + right(u1z - db * gzv, ms, G)
    back = left(ms, T, buoy * ay[0]) + right(buoy * az[0], ms, G)
    dk[0] = DT * bulk
    stay[0] = keep
    b[0] = buoy
    cdk[0] = count * (DT * bulk)
    pm[0] = pa[0] + (count * (keep * v0 + (DT * bulk) * yz + shot) - m1)
    wb[0] = (count * v0 - m0) - DT * back
    yz1[0] = yz
    for k, field in enumerate((yz0, gy + gyv, gz + gzv, ay[0], az[0])):
        late[0, k] = field
    gy0[0] = gy
    gz0[0] = gz


def prepare_call(
    ids, c, rho, alpha, p0, u, pa, v, spos, rec, epos, delay, drive, mats
):
    nx, ny, nz = c.shape
    n_e, n_s = epos.shape[1], spos.shape[1]
    pick = lambda i, ids: i
    plane = group_plane(c.shape, pick)
    return pl.pallas_call(
        prepare_kernel,
        grid_spec=pltpu.PrefetchScalarGridSpec(
            num_scalar_prefetch=1,
            grid=(nx,),
            in_specs=[pl.BlockSpec(memory_space=pltpu.SMEM)] + [plane] * 3
            + [group_plane(p0.shape, pick)] + [group_plane(u.shape, pick, a) for a in (1, 2)]
            + [group_plane(pa.shape, pick)] + [group_plane(v.shape, pick, a) for a in (1, 2)]
            + [whole((1, n_s)), pl.BlockSpec((None, STEPS, n_s), lambda i, ids: (0, 0, 0)),
               whole((1, n_e)), whole((1, n_e))]
            + [whole((ny, ny))] * 2,
            out_specs=[plane] * 7 + [pl.BlockSpec((1, 5, ny, nz), lambda i, ids: (i, 0, 0, 0))]
            + [plane] * 2,
            scratch_shapes=[pltpu.VMEM((n_s, nz), BF16), pltpu.VMEM((STEPS, 3 * n_s, nz), BF16),
                            pltpu.VMEM((STEPS, 3 * n_e, nz), BF16), mats_scratch(mats)],
        ),
        out_shape=[jax.ShapeDtypeStruct(c.shape, F32)] * 7
        + [jax.ShapeDtypeStruct((nx, 5, ny, nz), F32)] + [jax.ShapeDtypeStruct(c.shape, F32)] * 2,
        compiler_params=params(LIMIT["prepare"]),
        cost_estimate=cost(8000, 22),
        name="prepare",
    )(ids, drive, c, rho, alpha, p0, u, u, pa, v, v, spos, rec, epos, delay, *mats)


def on_chip(kernel, away, args, shapes, scratch, limit, estimate, name):
    vmem = pl.BlockSpec(memory_space=pltpu.VMEM)
    return pl.pallas_call(
        kernel,
        in_specs=[pl.BlockSpec(memory_space=pltpu.HBM)] * len(away) + [vmem] * len(args),
        out_specs=[vmem] * len(shapes),
        out_shape=[jax.ShapeDtypeStruct(v, F32) for v in shapes],
        scratch_shapes=[pltpu.VMEM(v, F32) if isinstance(v, tuple) else v for v in scratch]
        + [mats_scratch(args[-2:])],
        compiler_params=pltpu.CompilerParams(vmem_limit_bytes=limit * MIB),
        cost_estimate=estimate,
        name=name,
    )(*away, *args)


def unpack(block, dst, first):
    t = swap(block)
    n = t.shape[1]
    for xm in range(2):
        dst[:, (first + xm) * n : (first + xm + 1) * n, :] = t[4 * xm : 4 * xm + 4]


def forward_kernel(lines, gm, tm, out, gx0, gx1, ax, bk, in_s, mat_s, sems, f_s, o_s, ms):
    n = lines.shape[1]
    copies = [pltpu.make_async_copy(lines.at[:, :, 4], mat_s, sems.at[0])] + [
        pltpu.make_async_copy(lines.at[g, :, pl.ds(0, 4)], in_s.at[g], sems.at[1 + g]) for g in range(2)
    ]
    for copy in copies:
        copy.start()
    split_mats(gm, tm, ms)
    copies[0].wait()
    for e in range(2):
        unpack(mat_s[e], bk, 2 * e)

    @pl.loop(0, 2)
    def _(g):
        pltpu.make_async_copy(lines.at[g, :, pl.ds(0, 4)], in_s.at[g], sems.at[1 + g]).wait()
        for xl in range(4):
            rows = slice(xl * n, (xl + 1) * n)
            t = swap(in_s[g, :, xl])
            f_s[:, rows, :] = t[:6]
            ax[pl.ds(2 * g, 2), rows, :] = t[6:]
        rows = range(2)
        g0 = [left(ms, G, f_s[yl]) for yl in rows]
        u1 = [f_s[2 + yl] - (DT * bk[yl]) * g0[yl] for yl in rows]
        x0 = [left(ms, T, u1[yl]) for yl in rows]
        p1 = [f_s[4 + yl] + (DT * bk[2 + yl]) * x0[yl] for yl in rows]
        g1 = [left(ms, G, p1[yl]) for yl in rows]
        x1 = [left(ms, T, u1[yl] - (DT * bk[yl]) * g1[yl]) for yl in rows]
        for yl in rows:
            gx0[2 * g + yl] = g0[yl]
            gx1[2 * g + yl] = g1[yl]
            o_s[yl] = x0[yl]
            o_s[2 + yl] = x1[yl]
        for h in range(2):
            both = [o_s[:, (2 * h + xm) * n : (2 * h + xm + 1) * n, :] for xm in range(2)]
            out[g, :, h] = swap(jnp.concatenate(both, axis=0))


def forward_call(lines, mats):
    _, ns, _, _, nz = lines.shape
    nx = 4 * ns
    full = (4, nx, nz)
    return on_chip(
        forward_kernel, (lines,), mats, [(2, ns, 2, 8, nz), full, full, full, full],
        [(2, ns, 4, 8, nz), (2, ns, 8, nz), pltpu.SemaphoreType.DMA((3,)), (6, nx, nz), (4, nx, nz)],
        LIMIT["forward"], cost(1600, 11), "lines_forward",
    )


def middle_kernel(
    late, xs, dk, stay, b, pm, cdk, wb, yz1, gm, tm,
    buf, d0, t1, t2, x_s, o_s, ins, sems, ms,
):
    nx, ny, nz = dk.shape
    fetch = lambda i: pltpu.make_async_copy(late.at[i], ins.at[i], sems.at[i])
    for i in range(nx):
        fetch(i).start()
    split_mats(gm, tm, ms)
    for h in range(2):
        x_s[4 * h : 4 * h + 4] = swap(xs[:, h]).reshape(4, ny, nz)

    def some(planes):
        add = [dk[i] * x_s[2 * i] for i in planes]
        ey = [left(ms, G, a) for a in add]
        ez = [right(a, ms, T) for a in add]
        gy = [left(ms, T, (DT * b[i]) * e) for i, e in zip(planes, ey)]
        gz = [right((DT * b[i]) * e, ms, G) for i, e in zip(planes, ez)]
        rest = [x_s[2 * i + 1] - (e + f) for i, e, f in zip(planes, gy, gz)]
        adj = [pm[i] + cdk[i] * (stay[i] * x_s[2 * i] + r) for i, r in zip(planes, rest)]
        q = [dk[i] * a for i, a in zip(planes, adj)]
        fy = [left(ms, G, a) for a in q]
        fz = [right(a, ms, T) for a in q]
        for k, i in enumerate(planes):
            o_s[2 * i] = q[k]
            t1[i] = (yz1[i] + rest[k]) * adj[k]
        gy = [left(ms, T, b[i] * e) for i, e in zip(planes, fy)]
        gz = [right(b[i] * e, ms, G) for i, e in zip(planes, fz)]
        for k, i in enumerate(planes):
            o_s[2 * i + 1] = stay[i] * adj[k] + (cdk[i] * x_s[2 * i] + wb[i]) - DT * (gy[k] + gz[k])
            fetch(i).wait()
            d0[i] = x_s[2 * i] + ins[i, 0]
            t2[i] = (ins[i, 1] + ey[k]) * (ins[i, 3] + fy[k]) + (ins[i, 2] + ez[k]) * (ins[i, 4] + fz[k])

    some(range(nx))

    for h in range(2):
        buf[:, h] = swap(o_s[4 * h : 4 * h + 4].reshape(8, ny // 2, nz))


def middle_call(xs, fields, mats):
    nat = fields[0].shape
    saved = (8,) + nat[1:]
    return on_chip(
        middle_kernel, (fields[7],), (xs, *fields[:7], *mats), [xs.shape, nat, nat, nat],
        [saved, saved, (nat[0], 5) + nat[1:], pltpu.SemaphoreType.DMA((nat[0],))],
        LIMIT["middle"], cost(3200, 18), "slab_middle",
    )


def adjoint_kernel(qw, ux, bk, gx0, gx1, gm, tm, out, f_s, p_s, bx_s, ms):
    split_mats(gm, tm, ms)
    n, nz = qw.shape[1], qw.shape[4]
    lanes = [slice(0, nz // 2), slice(nz // 2, nz)]

    @pl.loop(0, 2)
    def _(g):
        for h in range(2):
            unpack(qw[g, :, h], f_s.at[g], 2 * h)

    at = [(g, yl) for g in range(2) for yl in range(2)]
    ax = [left(ms, G, f_s[g, yl]) for g, yl in at]
    ax = [ux[j] + v for j, v in enumerate(ax)]
    back = [left(ms, T, bk[yl] * v) for (g, yl), v in zip(at, ax)]
    p0 = [f_s[g, 2 + yl] - DT * v for (g, yl), v in zip(at, back)]
    gq = [left(ms, G, (DT * bk[2 + yl]) * v) for (g, yl), v in zip(at, p0)]
    bx = [gx1[j] * ax[j] + gx0[j] * (ax[j] + gq[j]) for j in range(4)]
    for j in range(4):
        p_s[j] = p0[j]
    for yl in range(2):
        bx_s[yl] = bx[yl] + bx[2 + yl]

    @pl.loop(0, 2)
    def _(g):
        for zh, z in enumerate(lanes):
            v = [p_s[pl.ds(2 * g, 2), xl * n : (xl + 1) * n, z] for xl in range(4)]
            out[g, :, 8 * zh : 8 * zh + 8, :] = swap(jnp.concatenate(v, axis=0))

    for e in range(2):
        v = [bx_s[:, (2 * e + xm) * n : (2 * e + xm + 1) * n, z] for z in lanes for xm in range(2)]
        out[e, :, 16:24, :] = swap(jnp.concatenate(v, axis=0))


def adjoint_call(qw, ux, bk, gx0, gx1, mats):
    _, ns, _, _, nz = qw.shape
    nx = 4 * ns
    return on_chip(
        adjoint_kernel, (), (qw, ux, bk, gx0, gx1, *mats), [(2, ns, 24, nz // 2)],
        [(2, 4, nx, nz), (4, nx, nz), (2, nx, nz)], LIMIT["adjoint"], cost(1200, 9), "lines_adjoint",
    )[0]


def last_kernel(ids, xs, d0, t1, t2, gy0, gz0, dk, gm, tm, out, p_s, bx_s, ms):
    split_mats(gm, tm, ms)
    nx, ny, nz = d0.shape
    half = nz // 2
    t = swap(xs[:, 16:24, :]).reshape(4, ny, half)
    for zh in range(2):
        z = slice(zh * half, (zh + 1) * half)
        p_s[:, :, z] = swap(xs[:, 8 * zh : 8 * zh + 8, :]).reshape(nx, ny, half)
        bx_s[:, :, z] = t[2 * zh : 2 * zh + 2]

    q = [dk[i] * p_s[i] for i in range(nx)]
    gy = [left(ms, G, v) for v in q]
    gz = [right(v, ms, T) for v in q]
    for i in range(nx):
        out[0, i] = t1[i] + d0[i] * p_s[i]
        out[1, i] = t2[i] + gy0[i] * gy[i] + gz0[i] * gz[i]

    for xm in range(2):
        out[1, 2 * ids[0] + xm] += bx_s[xm]


def last_call(ids, xs, fields, mats):
    nat = fields[0].shape
    vmem = pl.BlockSpec(memory_space=pltpu.VMEM)
    args = (xs, *fields, *mats)
    return pl.pallas_call(
        last_kernel,
        in_specs=[pl.BlockSpec(memory_space=pltpu.SMEM)] + [vmem] * len(args),
        out_specs=vmem,
        out_shape=jax.ShapeDtypeStruct((2,) + nat, F32),
        scratch_shapes=[pltpu.VMEM(nat, F32), pltpu.VMEM((2,) + nat[1:], F32), mats_scratch(mats)],
        compiler_params=pltpu.CompilerParams(vmem_limit_bytes=LIMIT["last"] * MIB),
        cost_estimate=cost(800, 9),
        name="slab_last",
    )(ids, *args)


def change_layout(v):
    return lax.all_to_all(v, ALL, split_axis=0, concat_axis=0, tiled=True)


def swap_groups(v):
    return lax.ppermute(v, "emit", [(0, 1), (1, 0)])


def local(
    sound_speed, density, absorption, pressure_start, velocity_start, adjoint_pressure,
    adjoint_velocity, emitter_voxel, emitter_delay, drive_waveform_samples, recorded_pressures,
    sensor_flat_position,
):
    n_emit, n_slab = lax.axis_size("emit"), lax.axis_size("slab")
    ndev = n_emit * n_slab
    planes, ny, nz = sound_speed.shape
    nx = planes * n_slab
    emit = lax.axis_index("emit")
    ids = jnp.stack([emit, lax.axis_index("slab")]).astype(jnp.int32)
    mats = pair_const(deriv_matrix(ny))
    order = (4 * np.arange(n_slab)[None, :] + np.arange(4)[:, None]).reshape(-1)
    line_mats = pair_const(deriv_matrix(nx)[np.ix_(order, order)])

    buf = start_call(
        sound_speed, density, absorption, pressure_start, velocity_start, adjoint_velocity,
        emitter_voxel, emitter_delay, drive_waveform_samples, mats, ndev,
    )
    fields = prepare_call(
        ids, sound_speed, density, absorption, pressure_start, velocity_start, adjoint_pressure,
        adjoint_velocity, sensor_flat_position.reshape(1, -1), recorded_pressures, emitter_voxel,
        emitter_delay, drive_waveform_samples, mats,
    )
    lines, fields = lax.optimization_barrier((change_layout(buf), fields))
    lines = lines.reshape(n_emit, n_slab, 5, 8, nz)
    xs, gx0, gx1, ux, bk = forward_call(lines, line_mats)
    xs = change_layout(xs.reshape(ndev, 2, 8, nz))
    qw, d0, t1, t2 = middle_call(xs, fields, mats)
    qw = change_layout(qw).reshape(n_emit, n_slab, 2, 8, nz)
    xs = adjoint_call(qw, ux, bk, gx0, gx1, line_mats)
    xs = change_layout(xs.reshape(ndev, 24, nz // 2))
    t = last_call(ids, xs, [d0, t1, t2, fields[8], fields[9], fields[0]], mats)
    other = swap_groups(t)
    s1, s2 = t[0] + other[0], t[1] + other[1]
    b = 1.0 / density
    speed_total = (2.0 * DT) * s1 * density * sound_speed
    density_total = DT * (s1 * sound_speed * sound_speed + s2 * b * b)
    return speed_total, density_total


def solution(mesh):
    in_specs = (
        P("slab", None, None), P("slab", None, None), P("slab", None, None),
        P("emit", "slab", None, None), P("emit", None, "slab", None, None),
        P("emit", "slab", None, None), P("emit", None, "slab", None, None),
        P("emit", None), P("emit", None), P(), P("emit", None, None), P(),
    )
    out_specs = (P("slab", None, None), P("slab", None, None))
    return jax.shard_map(local, mesh=mesh, in_specs=in_specs, out_specs=out_specs, check_vma=False)
```

time: 271 us -> 257 us (0.948)
  Pallas kernels: 49.9 us -> 43.2 us
  local copies, waits for them, and re-layouts: 4.98 us -> 0.08 us
    pallas_call x4, Pallas kernels: 31.4 us -> 24.4 us  [the longest x3 15.9 us: on_chip(): pl.pallas_call(kernel, in_specs=[pl.BlockSpec(memory_space=pltpu.HBM)] *...]
    unnamed x42 -> x32, local copies, waits for them, and re-layouts: 4.98 us -> 0.08 us
  transfers between devices with their start and end apart: 2 -> 2, of which waited for: 2 -> 2; matrix products, arithmetic and copies ran while one was open for 0% -> 0% of each run, Pallas kernels for 6% -> 7%
where the time goes in v5:
time: 257 us
  blocking collectives  104 us (40%)
  waiting for transfers between devices  94.3 us (37%)
  Pallas kernels  43.2 us (17%)
  starting transfers between devices  12.2 us (5%)
    all_to_all x3, blocking collectives, change_layout(): return lax.all_to_all(v, ALL, split_axis=0, concat_axis=0, tiled=True)  104 us
    ppermute x1, waiting for transfers between devices, swap_groups(): return lax.ppermute(v, 'emit', [(0, 1), (1, 0)])  47.8 us
    all_to_all x1, waiting for transfers between devices, change_layout(): return lax.all_to_all(v, ALL, split_axis=0, concat_axis=0, tiled=True)  46.4 us
    pallas_call x1, Pallas kernels, prepare_call(): pl.pallas_call(prepare_kernel, grid_spec=pltpu.PrefetchScalarGridSpec(num...  16.9 us
    pallas_call x3, Pallas kernels, on_chip(): pl.pallas_call(kernel, in_specs=[pl.BlockSpec(memory_space=pltpu.HBM)] *...  15.9 us
    all_to_all x1, starting transfers between devices, change_layout(): return lax.all_to_all(v, ALL, split_axis=0, concat_axis=0, tiled=True)  11.6 us
    pallas_call x1, Pallas kernels, start_call(): pl.pallas_call(start_kernel, in_specs=[smem] + [hbm] * 6 + [vmem] * 4, ou...  8.5 us
  transfers between devices with their start and end apart: 2, of which 2 were waited for; matrix products, arithmetic and copies ran while one was open for 0% of the time, Pallas kernels for 7%

profile of v5, /device:TPU:0, one launch (start us, length us, event | category | flops | bytes accessed | tf_op | source)
XLA Modules:
  0.0 257.1 jit_solution(2022115637923472948)
XLA Ops:
  0.6 8.5 %start.1 = f32[128,5,8,256]{3,2,1,0:T(8,128)} custom-call(f32[64]{0:T(128)} %drive.3, f32[4,256,256]{2,1,0:T(8,128)} %c.3, f32[4,256,256]{2,1,0:T(8,128)} %rho.3, f32[4,256,256]{2,1,0:T(8,128)} %alpha.3, f32[1,4,256,256]{3,2,1,0:T(8,128)} %p0.3, f32[1,3,4,256,256]{4,3,2,1,0:T(8,128)} %uz.1, f32[1,3,4,256,256]{4,3,2,1,0:T(8,128)} %az.1, s32[1,256]{1,0:T(1,128)} %epos.3, ...), custom_call_target="tpu_custom_call" | custom-call | flops 2000000000 | bytes 13631488 | tf_op jit(solution)/shard_map/start/pallas_call | solution.py:196
  9.1 11.6 %all-to-all-start = ((f32[128,5,8,256]{3,2,1,0:T(8,128)}), f32[128,5,8,256]{3,2,1,0:T(8,128)}, u32[]{:S(2)}, u32[]{:S(2)}) async-start(f32[128,5,8,256]{3,2,1,0:T(8,128)} %start.1), calls=%async_computation | async-start | bytes 10485760 | tf_op jit(solution)/shard_map/all_to_all | solution.py:487
  20.7 0.6 pad_add_fusion.ids
  21.3 16.9 %prepare.1 = (f32[4,256,256]{2,1,0:T(8,128)}, f32[4,256,256]{2,1,0:T(8,128)}, f32[4,256,256]{2,1,0:T(8,128)}, f32[4,256,256]{2,1,0:T(8,128)}, f32[4,256,256]{2,1...) custom-call(s32[2]{0:T(128)} %pad_add_fusion.ids, ...), custom_call_target="tpu_custom_call" | custom-call | flops 8000000000 | bytes 23068672 | tf_op jit(solution)/shard_map/prepare/pallas_call | solution.py:263
  38.2 46.4 %all-to-all-done = f32[128,5,8,256]{3,2,1,0:T(8,128)} async-done(((f32[128,5,8,256]{3,2,1,0:T(8,128)}), f32[128,5,8,256]{3,2,1,0:T(8,128)}, u32[]{:S(2)}, u32[]{:S(2)}) %all-to-all-start) | async-done | bytes 5242912 | tf_op jit(solution)/shard_map/all_to_all | solution.py:487
  84.7 0.0 copy-done.11
  84.7 0.0 copy-done.12
  84.7 0.0 copy-start.9
  84.7 0.0 copy-start.10
  84.7 5.9 %lines_forward.1 = (f32[2,64,2,8,256]{4,3,2,1,0:T(8,128)S(1)}, f32[4,256,256]{2,1,0:T(8,128)S(1)}, f32[4,256,256]{2,1,0:T(8,128)S(1)}, f32[4,256,256]{2,1,0:T(8,128)S(1)}, f32[4,256,256]{2,1,0:T(8,128)S(1)}) custom-call(f32[2,64,5,8,256]{4,3,2,1,0:T(8,128)} %bitcast.3.lines, f32[256,256]{1,0:T(8,128)S(1)} %copy-done.12, f32[256,256]{1,0:T(8,128)S(1)} %copy-done.11), custom_call_target="tpu_custom_call" | custom-call | flops 1600000000 | bytes 11534336 | tf_op jit(solution)/shard_map/lines_forward/pallas_call | solution.py:289
  90.6 0.0 copy-start
  90.6 0.0 copy-start.1
  90.7 0.0 copy-start.2
  90.7 0.0 copy-start.5
  90.7 0.0 copy-start.6
  90.7 39.8 %all_to_all.20.xs = f32[128,2,8,256]{3,2,1,0:T(8,128)} all-to-all(f32[128,2,8,256]{3,2,1,0:T(8,128)S(1)} %bitcast.19), channel_id=1, replica_groups=mesh['emit'=2,'slab'=64] {'emit','slab'}, dimensions={0} | all-to-all | bytes 4194304 | tf_op jit(solution)/shard_map/all_to_all | solution.py:487
  130.5 0.0 copy-done.7
  130.5 0.0 copy-done.8
  130.5 0.0 copy-done.9
  130.5 0.0 copy-done.10
  130.5 0.0 copy-done
  130.5 7.5 %slab_middle.1 = (f32[128,2,8,256]{3,2,1,0:T(8,128)S(1)}, f32[4,256,256]{2,1,0:T(8,128)S(1)}, f32[4,256,256]{2,1,0:T(8,128)S(1)}, f32[4,256,256]{2,1,0:T(8,128)S(1)}) custom-call(f32[4,5,256,256]{3,2,1,0:T(8,128)} %get-tuple-element.42.late, f32[128,2,8,256]{3,2,1,0:T(8,128)} %all_to_all.20.xs, f32[4,256,256]{2,1,0:T(8,128)S(1)} %copy-done, ...), custom_call_target="tpu_custom_call" | custom-call | flops 3200000000 | bytes 18874368 | tf_op jit(solution)/shard_map/slab_middle/pallas_call | solution.py:289
  138.0 35.0 %all_to_all.21 = f32[128,2,8,256]{3,2,1,0:T(8,128)S(1)} all-to-all(f32[128,2,8,256]{3,2,1,0:T(8,128)S(1)} %get-tuple-element.52), channel_id=1, replica_groups=mesh['emit'=2,'slab'=64] {'emit','slab'}, dimensions={0} | all-to-all | bytes 4194304 | tf_op jit(solution)/shard_map/all_to_all | solution.py:487
  173.0 2.5 lines_adjoint.1
  175.5 29.4 %all_to_all.22.xs = f32[128,24,128]{2,1,0:T(8,128)S(1)} all-to-all(f32[128,24,128]{2,1,0:T(8,128)S(1)} %bitcast.18), channel_id=1, replica_groups=mesh['emit'=2,'slab'=64] {'emit','slab'}, dimensions={0} | all-to-all | bytes 3145728 | tf_op jit(solution)/shard_map/all_to_all | solution.py:487
  204.8 0.0 copy-done.4
  204.9 0.0 copy-start.14
  204.9 0.0 copy-start.15
  204.9 1.9 slab_last.1
  206.8 0.6 collective-permute-start
  207.4 47.8 %collective-permute-done = f32[2,4,256,256]{3,2,1,0:T(8,128)S(1)} collective-permute-done((f32[2,4,256,256]{3,2,1,0:T(8,128)S(1)}, f32[2,4,256,256]{3,2,1,0:T(8,128)S(1)}, u32[]{:S(2)}, u32[]{:S(2)}) %collective-permute-start) | collective-permute-done | bytes 2097184 | tf_op jit(solution)/shard_map/ppermute | solution.py:491
  255.3 1.8 fusion.1
  (15 shorter events, 0.0 us)
Async XLA Ops:
  9.1 75.5 %all-to-all-start = ((f32[128,5,8,256]{3,2,1,0:T(8,128)}), f32[128,5,8,256]{3,2,1,0:T(8,128)}, u32[]{:S(2)}, u32[]{:S(2)}) async-start(f32[128,5,8,256]{3,2,1,0:T(8,128)} %start.1), calls=%async_computation | async-start | bytes 10485760 | tf_op jit(solution)/shard_map/all_to_all | solution.py:487
  21.3 63.4 %copy-start.11 = (f32[256,256]{1,0:T(8,128)S(1)}, f32[256,256]{1,0:T(8,128)}, u32[]{:S(2)}) copy-start(f32[256,256]{1,0:T(8,128)} %constant.26.clone.tm) | copy-start | bytes 786436
  21.3 63.4 %copy-start.12 = (f32[256,256]{1,0:T(8,128)S(1)}, f32[256,256]{1,0:T(8,128)}, u32[]{:S(2)}) copy-start(f32[256,256]{1,0:T(8,128)} %constant.25.clone.gm) | copy-start | bytes 786436
  84.7 45.8 %copy-start.7 = (f32[4,256,256]{2,1,0:T(8,128)S(1)}, f32[4,256,256]{2,1,0:T(8,128)}, u32[]{:S(2)}) copy-start(f32[4,256,256]{2,1,0:T(8,128)} %get-tuple-element.48.pm) | copy-start | bytes 3145732
  84.7 45.8 %copy-start.8 = (f32[4,256,256]{2,1,0:T(8,128)S(1)}, f32[4,256,256]{2,1,0:T(8,128)}, u32[]{:S(2)}) copy-start(f32[4,256,256]{2,1,0:T(8,128)} %get-tuple-element.49.cdk) | copy-start | bytes 3145732
  84.7 45.8 %copy-start.9 = (f32[4,256,256]{2,1,0:T(8,128)S(1)}, f32[4,256,256]{2,1,0:T(8,128)}, u32[]{:S(2)}) copy-start(f32[4,256,256]{2,1,0:T(8,128)} %get-tuple-element.50.wb) | copy-start | bytes 3145732
  84.7 45.8 %copy-start.10 = (f32[4,256,256]{2,1,0:T(8,128)S(1)}, f32[4,256,256]{2,1,0:T(8,128)}, u32[]{:S(2)}) copy-start(f32[4,256,256]{2,1,0:T(8,128)} %get-tuple-element.51.yz1) | copy-start | bytes 3145732
  90.6 39.9 %copy-start = (f32[4,256,256]{2,1,0:T(8,128)S(1)}, f32[4,256,256]{2,1,0:T(8,128)}, u32[]{:S(2)}) copy-start(f32[4,256,256]{2,1,0:T(8,128)} %get-tuple-element.45.dk) | copy-start | bytes 3145732
  90.6 39.9 %copy-start.1 = (f32[256,256]{1,0:T(8,128)S(1)}, f32[256,256]{1,0:T(8,128)}, u32[]{:S(2)}) copy-start(f32[256,256]{1,0:T(8,128)} %constant.24.clone.tm) | copy-start | bytes 786436
  90.7 39.9 %copy-start.2 = (f32[256,256]{1,0:T(8,128)S(1)}, f32[256,256]{1,0:T(8,128)}, u32[]{:S(2)}) copy-start(f32[256,256]{1,0:T(8,128)} %constant.23.clone.gm) | copy-start | bytes 786436
  90.7 39.9 %copy-start.5 = (f32[4,256,256]{2,1,0:T(8,128)S(1)}, f32[4,256,256]{2,1,0:T(8,128)}, u32[]{:S(2)}) copy-start(f32[4,256,256]{2,1,0:T(8,128)} %get-tuple-element.46.stay) | copy-start | bytes 3145732
  90.7 39.9 %copy-start.6 = (f32[4,256,256]{2,1,0:T(8,128)S(1)}, f32[4,256,256]{2,1,0:T(8,128)}, u32[]{:S(2)}) copy-start(f32[4,256,256]{2,1,0:T(8,128)} %get-tuple-element.47.b) | copy-start | bytes 3145732
  175.5 29.4 %copy-start.3 = (f32[4,256,256]{2,1,0:T(8,128)S(1)}, f32[4,256,256]{2,1,0:T(8,128)}, u32[]{:S(2)}) copy-start(f32[4,256,256]{2,1,0:T(8,128)} %get-tuple-element.60.gy0) | copy-start | bytes 3145732
  175.5 29.4 %copy-start.4 = (f32[4,256,256]{2,1,0:T(8,128)S(1)}, f32[4,256,256]{2,1,0:T(8,128)}, u32[]{:S(2)}) copy-start(f32[4,256,256]{2,1,0:T(8,128)} %get-tuple-element.61.gz0) | copy-start | bytes 3145732
  175.5 29.4 %copy-start.13 = (s32[2]{0:T(128)S(1)}, s32[2]{0:T(128)}, u32[]{:S(2)}) copy-start(s32[2]{0:T(128)} %pad_add_fusion.ids) | copy-start | bytes 28
  204.9 50.4 %copy-start.14 = (f32[4,256,256]{2,1,0:T(8,128)S(1)}, f32[4,256,256]{2,1,0:T(8,128)}, u32[]{:S(2)}) copy-start(f32[4,256,256]{2,1,0:T(8,128)} %c.3) | copy-start | bytes 3145732
  204.9 50.4 %copy-start.15 = (f32[4,256,256]{2,1,0:T(8,128)S(1)}, f32[4,256,256]{2,1,0:T(8,128)}, u32[]{:S(2)}) copy-start(f32[4,256,256]{2,1,0:T(8,128)} %rho.3) | copy-start | bytes 3145732
  206.8 48.5 %collective-permute-start = (f32[2,4,256,256]{3,2,1,0:T(8,128)S(1)}, f32[2,4,256,256]{3,2,1,0:T(8,128)S(1)}, u32[]{:S(2)}, u32[]{:S(2)}) collective-permute-start(f32[2,4,256,256]{3,2,1,0:T(8,128)S(1)} %slab_last.1), channel_id=1, source_target_pairs={{0,64},{64,0},{1,65},{65,1},{2,66},{66,2},{3,67},{67,3},{4,68},{68... | collective-permute-start | bytes 6291464 | tf_op jit(solution)/shard_map/ppermute | solution.py:491

commit v6 on v5

--- a/solution.py
+++ b/solution.py
@@ -10,7 +10,7 @@
 DT = 0.2
 F32 = jnp.float32
 BF16 = jnp.bfloat16
-ALL = ("emit", "slab")
+ALL = ("slab", "emit")
 MIB = 2**20
 LIMIT = {"start": 60, "prepare": 60, "forward": 24, "middle": 40, "adjoint": 20, "last": 20}
 
@@ -155,9 +155,10 @@
         return pltpu.make_async_copy(outs.at[i], buf.at[:, i], out_sems.at[i])
 
     srcs = (p0.at[0], c, rho, alpha, u.at[0, 1], u.at[0, 2], u.at[0, 0], v.at[0, 0])
-    for i in range(nx):
-        for copy in plane_copies(srcs, ins, sems, i):
-            copy.start()
+    for fields in (slice(0, 6), slice(6, 8)):
+        for i in range(nx):
+            for copy in plane_copies(srcs, ins, sems, i)[fields]:
+                copy.start()
     split_mats(gm, tm, ms)
     cols[...] = three(column_onehot(epos[...], nz), drive_at(delay[...], drive, 0))
 
@@ -165,7 +166,7 @@
     def _(k):
         pair = (2 * k, 2 * k + 1)
         for i in pair:
-            for copy in plane_copies(srcs, ins, sems, i):
+            for copy in plane_copies(srcs, ins, sems, i)[:6]:
                 copy.wait()
         steps = first_step(
             [tuple(ins[i, f] for f in (1, 2, 3, 0, 4, 5)) for i in pair],
@@ -173,6 +174,8 @@
         )
         for xm, i in enumerate(pair):
             v0, b, bulk = steps[xm][5:]
+            for copy in plane_copies(srcs, ins, sems, i)[6:]:
+                copy.wait()
             for f, field in enumerate((ins[i, 0], ins[i, 6], v0, ins[i, 7])):
                 pack[xm, 2 * f : 2 * f + 2] = field.reshape(2, half, nz)
             outs[i] = swap(pack[xm])
@@ -307,20 +310,19 @@
 
 
 def forward_kernel(lines, gm, tm, out, gx0, gx1, ax, bk, in_s, mat_s, sems, f_s, o_s, ms):
-    n = lines.shape[1]
-    copies = [pltpu.make_async_copy(lines.at[:, :, 4], mat_s, sems.at[0])] + [
-        pltpu.make_async_copy(lines.at[g, :, pl.ds(0, 4)], in_s.at[g], sems.at[1 + g]) for g in range(2)
-    ]
+    n = lines.shape[0]
+    fetch = lambda g: pltpu.make_async_copy(lines.at[:, g, pl.ds(0, 4)], in_s.at[g], sems.at[1 + g])
+    copies = [pltpu.make_async_copy(lines.at[:, :, 4], mat_s, sems.at[0]), fetch(0), fetch(1)]
     for copy in copies:
         copy.start()
     split_mats(gm, tm, ms)
     copies[0].wait()
     for e in range(2):
-        unpack(mat_s[e], bk, 2 * e)
+        unpack(mat_s[:, e], bk, 2 * e)
 
     @pl.loop(0, 2)
     def _(g):
-        pltpu.make_async_copy(lines.at[g, :, pl.ds(0, 4)], in_s.at[g], sems.at[1 + g]).wait()
+        fetch(g).wait()
         for xl in range(4):
             rows = slice(xl * n, (xl + 1) * n)
             t = swap(in_s[g, :, xl])
@@ -340,16 +342,16 @@
             o_s[2 + yl] = x1[yl]
         for h in range(2):
             both = [o_s[:, (2 * h + xm) * n : (2 * h + xm + 1) * n, :] for xm in range(2)]
-            out[g, :, h] = swap(jnp.concatenate(both, axis=0))
+            out[:, pl.ds(g, 1), h] = swap(jnp.concatenate(both, axis=0))[:, None]
 
 
 def forward_call(lines, mats):
-    _, ns, _, _, nz = lines.shape
+    ns, _, _, _, nz = lines.shape
     nx = 4 * ns
     full = (4, nx, nz)
     return on_chip(
-        forward_kernel, (lines,), mats, [(2, ns, 2, 8, nz), full, full, full, full],
-        [(2, ns, 4, 8, nz), (2, ns, 8, nz), pltpu.SemaphoreType.DMA((3,)), (6, nx, nz), (4, nx, nz)],
+        forward_kernel, (lines,), mats, [(ns, 2, 2, 8, nz), full, full, full, full],
+        [(2, ns, 4, 8, nz), (ns, 2, 8, nz), pltpu.SemaphoreType.DMA((3,)), (6, nx, nz), (4, nx, nz)],
         LIMIT["forward"], cost(1600, 11), "lines_forward",
     )
 
@@ -406,13 +408,12 @@
 
 def adjoint_kernel(qw, ux, bk, gx0, gx1, gm, tm, out, f_s, p_s, bx_s, ms):
     split_mats(gm, tm, ms)
-    n, nz = qw.shape[1], qw.shape[4]
+    n, nz = qw.shape[0], qw.shape[4]
     lanes = [slice(0, nz // 2), slice(nz // 2, nz)]
 
-    @pl.loop(0, 2)
-    def _(g):
+    for g in range(2):
         for h in range(2):
-            unpack(qw[g, :, h], f_s.at[g], 2 * h)
+            unpack(qw[:, g, h], f_s.at[g], 2 * h)
 
     at = [(g, yl) for g in range(2) for yl in range(2)]
     ax = [left(ms, G, f_s[g, yl]) for g, yl in at]
@@ -426,22 +427,21 @@
     for yl in range(2):
         bx_s[yl] = bx[yl] + bx[2 + yl]
 
-    @pl.loop(0, 2)
-    def _(g):
+    for g in range(2):
         for zh, z in enumerate(lanes):
-            v = [p_s[pl.ds(2 * g, 2), xl * n : (xl + 1) * n, z] for xl in range(4)]
-            out[g, :, 8 * zh : 8 * zh + 8, :] = swap(jnp.concatenate(v, axis=0))
+            v = [p_s[2 * g : 2 * g + 2, xl * n : (xl + 1) * n, z] for xl in range(4)]
+            out[:, g, 8 * zh : 8 * zh + 8, :] = swap(jnp.concatenate(v, axis=0))
 
     for e in range(2):
         v = [bx_s[:, (2 * e + xm) * n : (2 * e + xm + 1) * n, z] for z in lanes for xm in range(2)]
-        out[e, :, 16:24, :] = swap(jnp.concatenate(v, axis=0))
+        out[:, e, 16:24, :] = swap(jnp.concatenate(v, axis=0))
 
 
 def adjoint_call(qw, ux, bk, gx0, gx1, mats):
-    _, ns, _, _, nz = qw.shape
+    ns, _, _, _, nz = qw.shape
     nx = 4 * ns
     return on_chip(
-        adjoint_kernel, (), (qw, ux, bk, gx0, gx1, *mats), [(2, ns, 24, nz // 2)],
+        adjoint_kernel, (), (qw, ux, bk, gx0, gx1, *mats), [(ns, 2, 24, nz // 2)],
         [(2, 4, nx, nz), (4, nx, nz), (2, nx, nz)], LIMIT["adjoint"], cost(1200, 9), "lines_adjoint",
     )[0]
 
@@ -516,11 +516,11 @@
         emitter_delay, drive_waveform_samples, mats,
     )
     lines, fields = lax.optimization_barrier((change_layout(buf), fields))
-    lines = lines.reshape(n_emit, n_slab, 5, 8, nz)
+    lines = lines.reshape(n_slab, n_emit, 5, 8, nz)
     xs, gx0, gx1, ux, bk = forward_call(lines, line_mats)
     xs = change_layout(xs.reshape(ndev, 2, 8, nz))
     qw, d0, t1, t2 = middle_call(xs, fields, mats)
-    qw = change_layout(qw).reshape(n_emit, n_slab, 2, 8, nz)
+    qw = change_layout(qw).reshape(n_slab, n_emit, 2, 8, nz)
     xs = adjoint_call(qw, ux, bk, gx0, gx1, line_mats)
     xs = change_layout(xs.reshape(ndev, 24, nz // 2))
     t = last_call(ids, xs, [d0, t1, t2, fields[8], fields[9], fields[0]], mats)

time: 257 us -> 250 us (0.973)
  blocking collectives: 104 us -> 97.2 us
    all_to_all x3, blocking collectives: 104 us -> 97.2 us  [change_layout(): return lax.all_to_all(v, ALL, split_axis=0, concat_axis=0, tiled=True)]
where the time goes in v6:
time: 250 us
  blocking collectives  97.2 us (39%)
  waiting for transfers between devices  92.9 us (37%)
  Pallas kernels  42.8 us (17%)
  starting transfers between devices  13.4 us (5%)
    all_to_all x3, blocking collectives, change_layout(): return lax.all_to_all(v, ALL, split_axis=0, concat_axis=0, tiled=True)  97.2 us
    ppermute x1, waiting for transfers between devices, swap_groups(): return lax.ppermute(v, 'emit', [(0, 1), (1, 0)])  46.9 us
    all_to_all x1, waiting for transfers between devices, change_layout(): return lax.all_to_all(v, ALL, split_axis=0, concat_axis=0, tiled=True)  46 us
    pallas_call x1, Pallas kernels, prepare_call(): pl.pallas_call(prepare_kernel, grid_spec=pltpu.PrefetchScalarGridSpec(num...  16.9 us
    pallas_call x3, Pallas kernels, on_chip(): pl.pallas_call(kernel, in_specs=[pl.BlockSpec(memory_space=pltpu.HBM)] *...  15.6 us
    all_to_all x1, starting transfers between devices, change_layout(): return lax.all_to_all(v, ALL, split_axis=0, concat_axis=0, tiled=True)  11.6 us
    pallas_call x1, Pallas kernels, start_call(): pl.pallas_call(start_kernel, in_specs=[smem] + [hbm] * 6 + [vmem] * 4, ou...  8.34 us
  transfers between devices with their start and end apart: 2, of which 2 were waited for; matrix products, arithmetic and copies ran while one was open for 0% of the time, Pallas kernels for 7%

profile of v6, /device:TPU:0, one launch (start us, length us, event | category | flops | bytes accessed | tf_op | source)
XLA Modules:
  0.0 249.7 jit_solution(11521729262184672796)
XLA Ops:
  0.6 8.3 %start.1 = f32[128,5,8,256]{3,2,1,0:T(8,128)} custom-call(f32[64]{0:T(128)} %drive.3, f32[4,256,256]{2,1,0:T(8,128)} %c.3, f32[4,256,256]{2,1,0:T(8,128)} %rho.3, f32[4,256,256]{2,1,0:T(8,128)} %alpha.3, f32[1,4,256,256]{3,2,1,0:T(8,128)} %p0.3, f32[1,3,4,256,256]{4,3,2,1,0:T(8,128)} %uz.1, f32[1,3,4,256,256]{4,3,2,1,0:T(8,128)} %az.1, s32[1,256]{1,0:T(1,128)} %epos.3, ...), custom_call_target="tpu_custom_call" | custom-call | flops 2000000000 | bytes 13631488 | tf_op jit(solution)/shard_map/start/pallas_call | solution.py:199
  9.0 11.6 %all-to-all-start = ((f32[128,5,8,256]{3,2,1,0:T(8,128)}), f32[128,5,8,256]{3,2,1,0:T(8,128)}, u32[]{:S(2)}, u32[]{:S(2)}) async-start(f32[128,5,8,256]{3,2,1,0:T(8,128)} %start.1), calls=%async_computation | async-start | bytes 10485760 | tf_op jit(solution)/shard_map/all_to_all | solution.py:487
  20.5 0.6 pad_add_fusion.ids
  21.1 16.9 %prepare.1 = (f32[4,256,256]{2,1,0:T(8,128)}, f32[4,256,256]{2,1,0:T(8,128)}, f32[4,256,256]{2,1,0:T(8,128)}, f32[4,256,256]{2,1,0:T(8,128)}, f32[4,256,256]{2,1...) custom-call(s32[2]{0:T(128)} %pad_add_fusion.ids, ...), custom_call_target="tpu_custom_call" | custom-call | flops 8000000000 | bytes 23068672 | tf_op jit(solution)/shard_map/prepare/pallas_call | solution.py:266
  38.1 46.0 %all-to-all-done = f32[128,5,8,256]{3,2,1,0:T(8,128)} async-done(((f32[128,5,8,256]{3,2,1,0:T(8,128)}), f32[128,5,8,256]{3,2,1,0:T(8,128)}, u32[]{:S(2)}, u32[]{:S(2)}) %all-to-all-start) | async-done | bytes 5242912 | tf_op jit(solution)/shard_map/all_to_all | solution.py:487
  84.1 0.0 copy-done.11
  84.1 0.0 copy-done.12
  84.1 0.0 copy-start.9
  84.1 0.0 copy-start.10
  84.1 5.9 %lines_forward.1 = (f32[64,2,2,8,256]{4,3,2,1,0:T(8,128)S(1)}, f32[4,256,256]{2,1,0:T(8,128)S(1)}, f32[4,256,256]{2,1,0:T(8,128)S(1)}, f32[4,256,256]{2,1,0:T(8,128)S(1)}, f32[4,256,256]{2,1,0:T(8,128)S(1)}) custom-call(f32[64,2,5,8,256]{4,3,2,1,0:T(8,128)} %bitcast.3.lines, f32[256,256]{1,0:T(8,128)S(1)} %copy-done.12, f32[256,256]{1,0:T(8,128)S(1)} %copy-done.11), custom_call_target="tpu_custom_call" | custom-call | flops 1600000000 | bytes 11534336 | tf_op jit(solution)/shard_map/lines_forward/pallas_call | solution.py:292
  90.1 0.0 copy-start
  90.1 0.0 copy-start.1
  90.1 0.0 copy-start.2
  90.1 0.0 copy-start.5
  90.1 0.0 copy-start.6
  90.1 34.8 %all_to_all.20.xs = f32[128,2,8,256]{3,2,1,0:T(8,128)} all-to-all(f32[128,2,8,256]{3,2,1,0:T(8,128)S(1)} %bitcast.19), channel_id=1, replica_groups=mesh['emit'=2,'slab'=64] {'slab','emit'}, dimensions={0} | all-to-all | bytes 4194304 | tf_op jit(solution)/shard_map/all_to_all | solution.py:487
  124.9 0.0 copy-done.7
  124.9 0.0 copy-done.8
  124.9 0.0 copy-done.9
  125.0 0.0 copy-done.10
  125.0 7.5 %slab_middle.1 = (f32[128,2,8,256]{3,2,1,0:T(8,128)S(1)}, f32[4,256,256]{2,1,0:T(8,128)S(1)}, f32[4,256,256]{2,1,0:T(8,128)S(1)}, f32[4,256,256]{2,1,0:T(8,128)S(1)}) custom-call(f32[4,5,256,256]{3,2,1,0:T(8,128)} %get-tuple-element.42.late, f32[128,2,8,256]{3,2,1,0:T(8,128)} %all_to_all.20.xs, f32[4,256,256]{2,1,0:T(8,128)S(1)} %copy-done, ...), custom_call_target="tpu_custom_call" | custom-call | flops 3200000000 | bytes 18874368 | tf_op jit(solution)/shard_map/slab_middle/pallas_call | solution.py:292
  132.5 34.0 %all_to_all.21 = f32[128,2,8,256]{3,2,1,0:T(8,128)S(1)} all-to-all(f32[128,2,8,256]{3,2,1,0:T(8,128)S(1)} %get-tuple-element.52), channel_id=1, replica_groups=mesh['emit'=2,'slab'=64] {'slab','emit'}, dimensions={0} | all-to-all | bytes 4194304 | tf_op jit(solution)/shard_map/all_to_all | solution.py:487
  166.5 2.2 lines_adjoint.1
  168.7 28.4 %all_to_all.22.xs = f32[128,24,128]{2,1,0:T(8,128)S(1)} all-to-all(f32[128,24,128]{2,1,0:T(8,128)S(1)} %bitcast.18), channel_id=1, replica_groups=mesh['emit'=2,'slab'=64] {'slab','emit'}, dimensions={0} | all-to-all | bytes 3145728 | tf_op jit(solution)/shard_map/all_to_all | solution.py:487
  197.1 0.0 copy-done.3
  197.2 0.0 copy-start.14
  197.2 0.0 copy-start.15
  197.2 1.9 slab_last.1
  199.1 1.9 collective-permute-start
  201.0 46.9 %collective-permute-done = f32[2,4,256,256]{3,2,1,0:T(8,128)S(1)} collective-permute-done((f32[2,4,256,256]{3,2,1,0:T(8,128)S(1)}, f32[2,4,256,256]{3,2,1,0:T(8,128)S(1)}, u32[]{:S(2)}, u32[]{:S(2)}) %collective-permute-start) | collective-permute-done | bytes 2097184 | tf_op jit(solution)/shard_map/ppermute | solution.py:491
  247.9 0.0 copy-done.15
  247.9 1.8 fusion.1
  (15 shorter events, 0.0 us)
Async XLA Ops:
  9.0 75.1 %all-to-all-start = ((f32[128,5,8,256]{3,2,1,0:T(8,128)}), f32[128,5,8,256]{3,2,1,0:T(8,128)}, u32[]{:S(2)}, u32[]{:S(2)}) async-start(f32[128,5,8,256]{3,2,1,0:T(8,128)} %start.1), calls=%async_computation | async-start | bytes 10485760 | tf_op jit(solution)/shard_map/all_to_all | solution.py:487
  21.1 63.0 %copy-start.11 = (f32[256,256]{1,0:T(8,128)S(1)}, f32[256,256]{1,0:T(8,128)}, u32[]{:S(2)}) copy-start(f32[256,256]{1,0:T(8,128)} %constant.26.clone.tm) | copy-start | bytes 786436
  21.1 63.0 %copy-start.12 = (f32[256,256]{1,0:T(8,128)S(1)}, f32[256,256]{1,0:T(8,128)}, u32[]{:S(2)}) copy-start(f32[256,256]{1,0:T(8,128)} %constant.25.clone.gm) | copy-start | bytes 786436
  84.1 40.8 %copy-start.7 = (f32[4,256,256]{2,1,0:T(8,128)S(1)}, f32[4,256,256]{2,1,0:T(8,128)}, u32[]{:S(2)}) copy-start(f32[4,256,256]{2,1,0:T(8,128)} %get-tuple-element.48.pm) | copy-start | bytes 3145732
  84.1 40.8 %copy-start.8 = (f32[4,256,256]{2,1,0:T(8,128)S(1)}, f32[4,256,256]{2,1,0:T(8,128)}, u32[]{:S(2)}) copy-start(f32[4,256,256]{2,1,0:T(8,128)} %get-tuple-element.49.cdk) | copy-start | bytes 3145732
  84.1 40.8 %copy-start.9 = (f32[4,256,256]{2,1,0:T(8,128)S(1)}, f32[4,256,256]{2,1,0:T(8,128)}, u32[]{:S(2)}) copy-start(f32[4,256,256]{2,1,0:T(8,128)} %get-tuple-element.50.wb) | copy-start | bytes 3145732
  84.1 40.8 %copy-start.10 = (f32[4,256,256]{2,1,0:T(8,128)S(1)}, f32[4,256,256]{2,1,0:T(8,128)}, u32[]{:S(2)}) copy-start(f32[4,256,256]{2,1,0:T(8,128)} %get-tuple-element.51.yz1) | copy-start | bytes 3145732
  90.1 34.9 %copy-start = (f32[4,256,256]{2,1,0:T(8,128)S(1)}, f32[4,256,256]{2,1,0:T(8,128)}, u32[]{:S(2)}) copy-start(f32[4,256,256]{2,1,0:T(8,128)} %get-tuple-element.45.dk) | copy-start | bytes 3145732
  90.1 34.9 %copy-start.1 = (f32[256,256]{1,0:T(8,128)S(1)}, f32[256,256]{1,0:T(8,128)}, u32[]{:S(2)}) copy-start(f32[256,256]{1,0:T(8,128)} %constant.24.clone.tm) | copy-start | bytes 786436
  90.1 34.9 %copy-start.2 = (f32[256,256]{1,0:T(8,128)S(1)}, f32[256,256]{1,0:T(8,128)}, u32[]{:S(2)}) copy-start(f32[256,256]{1,0:T(8,128)} %constant.23.clone.gm) | copy-start | bytes 786436
  90.1 34.9 %copy-start.5 = (f32[4,256,256]{2,1,0:T(8,128)S(1)}, f32[4,256,256]{2,1,0:T(8,128)}, u32[]{:S(2)}) copy-start(f32[4,256,256]{2,1,0:T(8,128)} %get-tuple-element.46.stay) | copy-start | bytes 3145732
  90.1 34.9 %copy-start.6 = (f32[4,256,256]{2,1,0:T(8,128)S(1)}, f32[4,256,256]{2,1,0:T(8,128)}, u32[]{:S(2)}) copy-start(f32[4,256,256]{2,1,0:T(8,128)} %get-tuple-element.47.b) | copy-start | bytes 3145732
  168.7 28.5 %copy-start.3 = (f32[4,256,256]{2,1,0:T(8,128)S(1)}, f32[4,256,256]{2,1,0:T(8,128)}, u32[]{:S(2)}) copy-start(f32[4,256,256]{2,1,0:T(8,128)} %get-tuple-element.60.gy0) | copy-start | bytes 3145732
  168.7 28.5 %copy-start.4 = (f32[4,256,256]{2,1,0:T(8,128)S(1)}, f32[4,256,256]{2,1,0:T(8,128)}, u32[]{:S(2)}) copy-start(f32[4,256,256]{2,1,0:T(8,128)} %get-tuple-element.61.gz0) | copy-start | bytes 3145732
  168.7 28.5 %copy-start.13 = (s32[2]{0:T(128)S(1)}, s32[2]{0:T(128)}, u32[]{:S(2)}) copy-start(s32[2]{0:T(128)} %pad_add_fusion.ids) | copy-start | bytes 28
  197.2 50.8 %copy-start.14 = (f32[4,256,256]{2,1,0:T(8,128)S(1)}, f32[4,256,256]{2,1,0:T(8,128)}, u32[]{:S(2)}) copy-start(f32[4,256,256]{2,1,0:T(8,128)} %c.3) | copy-start | bytes 3145732
  197.2 50.7 %copy-start.15 = (f32[4,256,256]{2,1,0:T(8,128)S(1)}, f32[4,256,256]{2,1,0:T(8,128)}, u32[]{:S(2)}) copy-start(f32[4,256,256]{2,1,0:T(8,128)} %rho.3) | copy-start | bytes 3145732
  199.1 48.8 %collective-permute-start = (f32[2,4,256,256]{3,2,1,0:T(8,128)S(1)}, f32[2,4,256,256]{3,2,1,0:T(8,128)S(1)}, u32[]{:S(2)}, u32[]{:S(2)}) collective-permute-start(f32[2,4,256,256]{3,2,1,0:T(8,128)S(1)} %slab_last.1), channel_id=1, source_target_pairs={{0,64},{64,0},{1,65},{65,1},{2,66},{66,2},{3,67},{67,3},{4,68},{68... | collective-permute-start | bytes 6291464 | tf_op jit(solution)/shard_map/ppermute | solution.py:491

commit v7 on v6

--- a/solution.py
+++ b/solution.py
@@ -144,8 +144,7 @@
 
 
 def start_kernel(
-    drive, c, rho, alpha, p0, u, v, epos, delay, gm, tm, buf, ins, sems, outs, out_sems, mat, cols,
-    pack, ms
+    drive, c, rho, alpha, p0, u, epos, delay, gm, tm, buf, ins, sems, outs, out_sems, cols, pack, ms
 ):
     emit, slab = lax.axis_index("emit"), lax.axis_index("slab")
     nx, ny, nz = c.shape
@@ -154,8 +153,8 @@
     def send(i):
         return pltpu.make_async_copy(outs.at[i], buf.at[:, i], out_sems.at[i])
 
-    srcs = (p0.at[0], c, rho, alpha, u.at[0, 1], u.at[0, 2], u.at[0, 0], v.at[0, 0])
-    for fields in (slice(0, 6), slice(6, 8)):
+    srcs = (p0.at[0], c, rho, alpha, u.at[0, 1], u.at[0, 2], u.at[0, 0])
+    for fields in (slice(0, 6), slice(6, 7)):
         for i in range(nx):
             for copy in plane_copies(srcs, ins, sems, i)[fields]:
                 copy.start()
@@ -176,44 +175,37 @@
             v0, b, bulk = steps[xm][5:]
             for copy in plane_copies(srcs, ins, sems, i)[6:]:
                 copy.wait()
-            for f, field in enumerate((ins[i, 0], ins[i, 6], v0, ins[i, 7])):
+            for f, field in enumerate((ins[i, 0], ins[i, 6], v0, jnp.where(emit == 0, b, bulk))):
                 pack[xm, 2 * f : 2 * f + 2] = field.reshape(2, half, nz)
             outs[i] = swap(pack[xm])
             send(i).start()
 
-            @pl.when(k == emit)
-            def _():
-                mat[4 * xm : 4 * xm + 2] = b.reshape(2, half, nz)
-                mat[4 * xm + 2 : 4 * xm + 4] = bulk.reshape(2, half, nz)
-
-    outs[nx] = swap(mat[...])
-    send(nx).start()
-    for i in range(nx + 1):
+    for i in range(nx):
         send(i).wait()
 
 
-def start_call(c, rho, alpha, p0, u, v, epos, delay, drive, mats, ndev):
+def start_call(c, rho, alpha, p0, u, epos, delay, drive, mats, ndev):
     nx, ny, nz = c.shape
     n_e = epos.shape[1]
     hbm, vmem, smem = (pl.BlockSpec(memory_space=m) for m in (pltpu.HBM, pltpu.VMEM, pltpu.SMEM))
     return pl.pallas_call(
         start_kernel,
-        in_specs=[smem] + [hbm] * 6 + [vmem] * 4,
+        in_specs=[smem] + [hbm] * 5 + [vmem] * 4,
         out_specs=hbm,
-        out_shape=jax.ShapeDtypeStruct((ndev, nx + 1, 8, nz), F32),
-        scratch_shapes=[pltpu.VMEM((nx, 8, ny, nz), F32), pltpu.SemaphoreType.DMA((nx, 8)),
-                        pltpu.VMEM((nx + 1, ndev, 8, nz), F32), pltpu.SemaphoreType.DMA((nx + 1,)),
-                        pltpu.VMEM((8, ndev, nz), F32), pltpu.VMEM((3 * n_e, nz), BF16),
+        out_shape=jax.ShapeDtypeStruct((ndev, nx, 8, nz), F32),
+        scratch_shapes=[pltpu.VMEM((nx, 7, ny, nz), F32), pltpu.SemaphoreType.DMA((nx, 7)),
+                        pltpu.VMEM((nx, ndev, 8, nz), F32), pltpu.SemaphoreType.DMA((nx,)),
+                        pltpu.VMEM((3 * n_e, nz), BF16),
                         pltpu.VMEM((2, 8, ndev, nz), F32), mats_scratch(mats)],
         compiler_params=pltpu.CompilerParams(vmem_limit_bytes=LIMIT["start"] * MIB),
         cost_estimate=cost(2000, 13),
         name="start",
-    )(drive, c, rho, alpha, p0, u, v, epos, delay, *mats)
+    )(drive, c, rho, alpha, p0, u, epos, delay, *mats)
 
 
 def prepare_kernel(
-    ids, drive, c, rho, alpha, p0, uy, uz, pa, ay, az, spos, rec, epos, delay, gm, tm,
-    dk, stay, b, pm, cdk, wb, yz1, late, gy0, gz0, ones, scols, ecols, ms,
+    ids, drive, c, rho, alpha, p0, uy, uz, pa, ax, ay, az, spos, rec, epos, delay, gm, tm,
+    dk, stay, b, pm, cdk, wb, yz1, late, gy0, gz0, axs, ones, scols, ecols, pack, ms,
 ):
     i = pl.program_id(0)
     ny, nz = c.shape[1], c.shape[2]
@@ -254,6 +246,11 @@
         late[0, k] = field
     gy0[0] = gy
     gz0[0] = gz
+    pack[pl.ds(2 * i, 2)] = ax[0].reshape(2, ny // 2, nz)
+
+    @pl.when(i == pl.num_programs(0) - 1)
+    def _():
+        axs[...] = swap(pack[...])
 
 
 def prepare_call(
@@ -270,21 +267,23 @@
             grid=(nx,),
             in_specs=[pl.BlockSpec(memory_space=pltpu.SMEM)] + [plane] * 3
             + [group_plane(p0.shape, pick)] + [group_plane(u.shape, pick, a) for a in (1, 2)]
-            + [group_plane(pa.shape, pick)] + [group_plane(v.shape, pick, a) for a in (1, 2)]
+            + [group_plane(pa.shape, pick)] + [group_plane(v.shape, pick, a) for a in range(3)]
             + [whole((1, n_s)), pl.BlockSpec((None, STEPS, n_s), lambda i, ids: (0, 0, 0)),
                whole((1, n_e)), whole((1, n_e))]
             + [whole((ny, ny))] * 2,
             out_specs=[plane] * 7 + [pl.BlockSpec((1, 5, ny, nz), lambda i, ids: (i, 0, 0, 0))]
-            + [plane] * 2,
+            + [plane] * 2 + [whole((ny // 2, 2 * nx, nz))],
             scratch_shapes=[pltpu.VMEM((n_s, nz), BF16), pltpu.VMEM((STEPS, 3 * n_s, nz), BF16),
-                            pltpu.VMEM((STEPS, 3 * n_e, nz), BF16), mats_scratch(mats)],
+                            pltpu.VMEM((STEPS, 3 * n_e, nz), BF16),
+                            pltpu.VMEM((2 * nx, ny // 2, nz), F32), mats_scratch(mats)],
         ),
         out_shape=[jax.ShapeDtypeStruct(c.shape, F32)] * 7
-        + [jax.ShapeDtypeStruct((nx, 5, ny, nz), F32)] + [jax.ShapeDtypeStruct(c.shape, F32)] * 2,
+        + [jax.ShapeDtypeStruct((nx, 5, ny, nz), F32)] + [jax.ShapeDtypeStruct(c.shape, F32)] * 2
+        + [jax.ShapeDtypeStruct((ny // 2, 2 * nx, nz), F32)],
         compiler_params=params(LIMIT["prepare"]),
         cost_estimate=cost(8000, 22),
         name="prepare",
-    )(ids, drive, c, rho, alpha, p0, u, u, pa, v, v, spos, rec, epos, delay, *mats)
+    )(ids, drive, c, rho, alpha, p0, u, u, pa, v, v, v, spos, rec, epos, delay, *mats)
 
 
 def on_chip(kernel, away, args, shapes, scratch, limit, estimate, name):
@@ -309,40 +308,36 @@
         dst[:, (first + xm) * n : (first + xm + 1) * n, :] = t[4 * xm : 4 * xm + 4]
 
 
-def forward_kernel(lines, gm, tm, out, gx0, gx1, ax, bk, in_s, mat_s, sems, f_s, o_s, ms):
+def forward_kernel(lines, gm, tm, out, gx0, gx1, bk, in_s, sems, f_s, o_s, ms):
     n = lines.shape[0]
-    fetch = lambda g: pltpu.make_async_copy(lines.at[:, g, pl.ds(0, 4)], in_s.at[g], sems.at[1 + g])
-    copies = [pltpu.make_async_copy(lines.at[:, :, 4], mat_s, sems.at[0]), fetch(0), fetch(1)]
-    for copy in copies:
-        copy.start()
+    fetch = lambda g: pltpu.make_async_copy(lines.at[:, g], in_s.at[g], sems.at[g])
+    groups, at = range(2), range(4)
+    for g in groups:
+        fetch(g).start()
     split_mats(gm, tm, ms)
-    copies[0].wait()
-    for e in range(2):
-        unpack(mat_s[:, e], bk, 2 * e)
-
-    @pl.loop(0, 2)
-    def _(g):
+    g0, u1, x0 = [], [], []
+    for g in groups:
         fetch(g).wait()
         for xl in range(4):
             rows = slice(xl * n, (xl + 1) * n)
             t = swap(in_s[g, :, xl])
-            f_s[:, rows, :] = t[:6]
-            ax[pl.ds(2 * g, 2), rows, :] = t[6:]
-        rows = range(2)
-        g0 = [left(ms, G, f_s[yl]) for yl in rows]
-        u1 = [f_s[2 + yl] - (DT * bk[yl]) * g0[yl] for yl in rows]
-        x0 = [left(ms, T, u1[yl]) for yl in rows]
-        p1 = [f_s[4 + yl] + (DT * bk[2 + yl]) * x0[yl] for yl in rows]
-        g1 = [left(ms, G, p1[yl]) for yl in rows]
-        x1 = [left(ms, T, u1[yl] - (DT * bk[yl]) * g1[yl]) for yl in rows]
-        for yl in rows:
-            gx0[2 * g + yl] = g0[yl]
-            gx1[2 * g + yl] = g1[yl]
-            o_s[yl] = x0[yl]
-            o_s[2 + yl] = x1[yl]
+            f_s[g, :, rows, :] = t[:6]
+            bk[2 * g : 2 * g + 2, rows, :] = t[6:]
+        g0 += [left(ms, G, f_s[g, yl]) for yl in range(2)]
+        u1 += [f_s[g, 2 + yl] - (DT * bk[yl]) * g0[2 * g + yl] for yl in range(2)]
+        x0 += [left(ms, T, u1[2 * g + yl]) for yl in range(2)]
+    p1 = [f_s[j // 2, 4 + j % 2] + (DT * bk[2 + j % 2]) * x0[j] for j in at]
+    g1 = [left(ms, G, p1[j]) for j in at]
+    x1 = [left(ms, T, u1[j] - (DT * bk[j % 2]) * g1[j]) for j in at]
+    for j in at:
+        gx0[j] = g0[j]
+        gx1[j] = g1[j]
+        o_s[j // 2, j % 2] = x0[j]
+        o_s[j // 2, 2 + j % 2] = x1[j]
+    for g in groups:
         for h in range(2):
-            both = [o_s[:, (2 * h + xm) * n : (2 * h + xm + 1) * n, :] for xm in range(2)]
-            out[:, pl.ds(g, 1), h] = swap(jnp.concatenate(both, axis=0))[:, None]
+            both = [o_s[g, :, (2 * h + xm) * n : (2 * h + xm + 1) * n, :] for xm in range(2)]
+            out[:, g, h] = swap(jnp.concatenate(both, axis=0))
 
 
 def forward_call(lines, mats):
@@ -350,20 +345,22 @@
     nx = 4 * ns
     full = (4, nx, nz)
     return on_chip(
-        forward_kernel, (lines,), mats, [(ns, 2, 2, 8, nz), full, full, full, full],
-        [(2, ns, 4, 8, nz), (ns, 2, 8, nz), pltpu.SemaphoreType.DMA((3,)), (6, nx, nz), (4, nx, nz)],
-        LIMIT["forward"], cost(1600, 11), "lines_forward",
+        forward_kernel, (lines,), mats, [(ns, 2, 2, 8, nz), full, full, full],
+        [(2, ns, 4, 8, nz), pltpu.SemaphoreType.DMA((2,)), (2, 6, nx, nz), (2, 4, nx, nz)],
+        LIMIT["forward"], cost(1600, 9), "lines_forward",
     )
 
 
 def middle_kernel(
-    late, xs, dk, stay, b, pm, cdk, wb, yz1, gm, tm,
+    late, axs, xs, dk, stay, b, pm, cdk, wb, yz1, gm, tm,
     buf, d0, t1, t2, x_s, o_s, ins, sems, ms,
 ):
     nx, ny, nz = dk.shape
     fetch = lambda i: pltpu.make_async_copy(late.at[i], ins.at[i], sems.at[i])
     for i in range(nx):
         fetch(i).start()
+    fetch_ax = pltpu.make_async_copy(axs, buf.at[:, 2], sems.at[nx])
+    fetch_ax.start()
     split_mats(gm, tm, ms)
     for h in range(2):
         x_s[4 * h : 4 * h + 4] = swap(xs[:, h]).reshape(4, ny, nz)
@@ -394,19 +391,21 @@
 
     for h in range(2):
         buf[:, h] = swap(o_s[4 * h : 4 * h + 4].reshape(8, ny // 2, nz))
+    fetch_ax.wait()
 
 
 def middle_call(xs, fields, mats):
     nat = fields[0].shape
     saved = (8,) + nat[1:]
     return on_chip(
-        middle_kernel, (fields[7],), (xs, *fields[:7], *mats), [xs.shape, nat, nat, nat],
-        [saved, saved, (nat[0], 5) + nat[1:], pltpu.SemaphoreType.DMA((nat[0],))],
+        middle_kernel, (fields[7], fields[10]), (xs, *fields[:7], *mats),
+        [(xs.shape[0], 3) + xs.shape[2:], nat, nat, nat],
+        [saved, saved, (nat[0], 5) + nat[1:], pltpu.SemaphoreType.DMA((nat[0] + 1,))],
         LIMIT["middle"], cost(3200, 18), "slab_middle",
     )
 
 
-def adjoint_kernel(qw, ux, bk, gx0, gx1, gm, tm, out, f_s, p_s, bx_s, ms):
+def adjoint_kernel(qw, bk, gx0, gx1, gm, tm, out, f_s, ux, p_s, bx_s, ms):
     split_mats(gm, tm, ms)
     n, nz = qw.shape[0], qw.shape[4]
     lanes = [slice(0, nz // 2), slice(nz // 2, nz)]
@@ -414,6 +413,9 @@
     for g in range(2):
         for h in range(2):
             unpack(qw[:, g, h], f_s.at[g], 2 * h)
+        t = swap(qw[:, g, 2])
+        for xl in range(4):
+            ux[2 * g : 2 * g + 2, xl * n : (xl + 1) * n, :] = t[2 * xl : 2 * xl + 2]
 
     at = [(g, yl) for g in range(2) for yl in range(2)]
     ax = [left(ms, G, f_s[g, yl]) for g, yl in at]
@@ -437,12 +439,12 @@
         out[:, e, 16:24, :] = swap(jnp.concatenate(v, axis=0))
 
 
-def adjoint_call(qw, ux, bk, gx0, gx1, mats):
+def adjoint_call(qw, bk, gx0, gx1, mats):
     ns, _, _, _, nz = qw.shape
     nx = 4 * ns
     return on_chip(
-        adjoint_kernel, (), (qw, ux, bk, gx0, gx1, *mats), [(ns, 2, 24, nz // 2)],
-        [(2, 4, nx, nz), (4, nx, nz), (2, nx, nz)], LIMIT["adjoint"], cost(1200, 9), "lines_adjoint",
+        adjoint_kernel, (), (qw, bk, gx0, gx1, *mats), [(ns, 2, 24, nz // 2)],
+        [(2, 4, nx, nz), (4, nx, nz), (4, nx, nz), (2, nx, nz)], LIMIT["adjoint"], cost(1200, 9), "lines_adjoint",
     )[0]
 
 
@@ -507,8 +509,8 @@
     line_mats = pair_const(deriv_matrix(nx)[np.ix_(order, order)])
 
     buf = start_call(
-        sound_speed, density, absorption, pressure_start, velocity_start, adjoint_velocity,
-        emitter_voxel, emitter_delay, drive_waveform_samples, mats, ndev,
+        sound_speed, density, absorption, pressure_start, velocity_start, emitter_voxel,
+        emitter_delay, drive_waveform_samples, mats, ndev,
     )
     fields = prepare_call(
         ids, sound_speed, density, absorption, pressure_start, velocity_start, adjoint_pressure,
@@ -516,12 +518,12 @@
         emitter_delay, drive_waveform_samples, mats,
     )
     lines, fields = lax.optimization_barrier((change_layout(buf), fields))
-    lines = lines.reshape(n_slab, n_emit, 5, 8, nz)
-    xs, gx0, gx1, ux, bk = forward_call(lines, line_mats)
+    lines = lines.reshape(n_slab, n_emit, 4, 8, nz)
+    xs, gx0, gx1, bk = forward_call(lines, line_mats)
     xs = change_layout(xs.reshape(ndev, 2, 8, nz))
     qw, d0, t1, t2 = middle_call(xs, fields, mats)
-    qw = change_layout(qw).reshape(n_slab, n_emit, 2, 8, nz)
-    xs = adjoint_call(qw, ux, bk, gx0, gx1, line_mats)
+    qw = change_layout(qw).reshape(n_slab, n_emit, 3, 8, nz)
+    xs = adjoint_call(qw, bk, gx0, gx1, line_mats)
     xs = change_layout(xs.reshape(ndev, 24, nz // 2))
     t = last_call(ids, xs, [d0, t1, t2, fields[8], fields[9], fields[0]], mats)
     other = swap_groups(t)

time: 250 us -> 248 us (level)
  waiting for transfers between devices: 92.9 us -> 80.2 us
  blocking collectives: 97.2 us -> 108 us
    all_to_all x1, waiting for transfers between devices: 46 us -> 33.3 us  [change_layout(): return lax.all_to_all(v, ALL, split_axis=0, concat_axis=0, tiled=True)]
    all_to_all x3, blocking collectives: 97.2 us -> 108 us  [change_layout(): return lax.all_to_all(v, ALL, split_axis=0, concat_axis=0, tiled=True)]
where the time goes in v7:
time: 248 us
  blocking collectives  108 us (44%)
  waiting for transfers between devices  80.2 us (32%)
  Pallas kernels  42.2 us (17%)
  starting transfers between devices  13.5 us (5%)
    all_to_all x3, blocking collectives, change_layout(): return lax.all_to_all(v, ALL, split_axis=0, concat_axis=0, tiled=True)  108 us
    ppermute x1, waiting for transfers between devices, swap_groups(): return lax.ppermute(v, 'emit', [(0, 1), (1, 0)])  46.9 us
    all_to_all x1, waiting for transfers between devices, change_layout(): return lax.all_to_all(v, ALL, split_axis=0, concat_axis=0, tiled=True)  33.3 us
    pallas_call x1, Pallas kernels, prepare_call(): pl.pallas_call(prepare_kernel, grid_spec=pltpu.PrefetchScalarGridSpec(num...  18 us
    pallas_call x3, Pallas kernels, on_chip(): pl.pallas_call(kernel, in_specs=[pl.BlockSpec(memory_space=pltpu.HBM)] *...  14.5 us
    all_to_all x1, starting transfers between devices, change_layout(): return lax.all_to_all(v, ALL, split_axis=0, concat_axis=0, tiled=True)  11.7 us
    pallas_call x1, Pallas kernels, start_call(): pl.pallas_call(start_kernel, in_specs=[smem] + [hbm] * 5 + [vmem] * 4, ou...  7.78 us
  transfers between devices with their start and end apart: 2, of which 2 were waited for; matrix products, arithmetic and copies ran while one was open for 0% of the time, Pallas kernels for 7%

profile of v7, /device:TPU:0, one launch (start us, length us, event | category | flops | bytes accessed | tf_op | source)
XLA Modules:
  0.0 247.6 jit_solution(2420394838186406148)
XLA Ops:
  0.6 7.8 %start.1 = f32[128,4,8,256]{3,2,1,0:T(8,128)} custom-call(f32[64]{0:T(128)} %drive.3, f32[4,256,256]{2,1,0:T(8,128)} %c.3, f32[4,256,256]{2,1,0:T(8,128)} %rho.3, f32[4,256,256]{2,1,0:T(8,128)} %alpha.3, f32[1,4,256,256]{3,2,1,0:T(8,128)} %p0.3, f32[1,3,4,256,256]{4,3,2,1,0:T(8,128)} %uz.1, s32[1,256]{1,0:T(1,128)} %epos.3, s32[1,256]{1,0:T(1,128)} %delay.3, ...), custom_call_target="tpu_custom_call" | custom-call | flops 2000000000 | bytes 13631488 | tf_op jit(solution)/shard_map/start/pallas_call | solution.py:191
  8.4 11.7 %all-to-all-start = ((f32[128,4,8,256]{3,2,1,0:T(8,128)}), f32[128,4,8,256]{3,2,1,0:T(8,128)}, u32[]{:S(2)}, u32[]{:S(2)}) async-start(f32[128,4,8,256]{3,2,1,0:T(8,128)} %start.1), calls=%async_computation | async-start | bytes 8388608 | tf_op jit(solution)/shard_map/all_to_all | solution.py:489
  20.1 0.6 pad_add_fusion.ids
  20.7 18.0 %prepare.1 = (f32[4,256,256]{2,1,0:T(8,128)}, f32[4,256,256]{2,1,0:T(8,128)}, f32[4,256,256]{2,1,0:T(8,128)}, f32[4,256,256]{2,1,0:T(8,128)}, f32[4,256,256]{2,1...) custom-call(s32[2]{0:T(128)} %pad_add_fusion.ids, ...), custom_call_target="tpu_custom_call" | custom-call | flops 8000000000 | bytes 23068672 | tf_op jit(solution)/shard_map/prepare/pallas_call | solution.py:263
  38.7 33.3 %all-to-all-done = f32[128,4,8,256]{3,2,1,0:T(8,128)} async-done(((f32[128,4,8,256]{3,2,1,0:T(8,128)}), f32[128,4,8,256]{3,2,1,0:T(8,128)}, u32[]{:S(2)}, u32[]{:S(2)}) %all-to-all-start) | async-done | bytes 4194336 | tf_op jit(solution)/shard_map/all_to_all | solution.py:489
  72.0 0.0 copy-done.12
  72.0 0.0 copy-done.13
  72.0 0.0 copy-start.7
  72.0 0.0 copy-start.8
  72.0 0.0 copy-start.9
  72.1 5.0 %lines_forward.1 = (f32[64,2,2,8,256]{4,3,2,1,0:T(8,128)S(1)}, f32[4,256,256]{2,1,0:T(8,128)S(1)}, f32[4,256,256]{2,1,0:T(8,128)S(1)}, f32[4,256,256]{2,1,0:T(8,128)S(1)}) custom-call(f32[64,2,4,8,256]{4,3,2,1,0:T(8,128)} %bitcast.3.lines, f32[256,256]{1,0:T(8,128)S(1)} %copy-done.13, f32[256,256]{1,0:T(8,128)S(1)} %copy-done.12), custom_call_target="tpu_custom_call" | custom-call | flops 1600000000 | bytes 9437184 | tf_op jit(solution)/shard_map/lines_forward/pallas_call | solution.py:291
  77.1 0.0 copy-start
  77.1 0.0 copy-start.1
  77.1 0.0 copy-start.2
  77.1 0.0 copy-start.3
  77.2 0.0 copy-start.4
  77.2 34.1 %all_to_all.20.xs = f32[128,2,8,256]{3,2,1,0:T(8,128)S(1)} all-to-all(f32[128,2,8,256]{3,2,1,0:T(8,128)S(1)} %bitcast.19), channel_id=1, replica_groups=mesh['emit'=2,'slab'=64] {'slab','emit'}, dimensions={0} | all-to-all | bytes 4194304 | tf_op jit(solution)/shard_map/all_to_all | solution.py:489
  111.2 0.0 copy-done.5
  111.2 0.0 copy-done.6
  111.3 0.0 copy-done.7
  111.3 7.2 %slab_middle.1 = (f32[128,3,8,256]{3,2,1,0:T(8,128)}, f32[4,256,256]{2,1,0:T(8,128)S(1)}, f32[4,256,256]{2,1,0:T(8,128)S(1)}, f32[4,256,256]{2,1,0:T(8,128)S(1)}) custom-call(f32[4,5,256,256]{3,2,1,0:T(8,128)} %get-tuple-element.44.late, f32[128,8,256]{2,1,0:T(8,128)S(1)} %copy-done.9, f32[128,2,8,256]{3,2,1,0:T(8,128)S(1)} %all_to_all.20.xs, ...), custom_call_target="tpu_custom_call" | custom-call | flops 3200000000 | bytes 18874368 | tf_op jit(solution)/shard_map/slab_middle/pallas_call | solution.py:291
  118.5 45.7 %all_to_all.21 = f32[128,3,8,256]{3,2,1,0:T(8,128)S(1)} all-to-all(f32[128,3,8,256]{3,2,1,0:T(8,128)} %get-tuple-element.55), channel_id=1, replica_groups=mesh['emit'=2,'slab'=64] {'slab','emit'}, dimensions={0} | all-to-all | bytes 6291456 | tf_op jit(solution)/shard_map/all_to_all | solution.py:489
  164.3 2.3 lines_adjoint.1
  166.6 28.5 %all_to_all.22.xs = f32[128,24,128]{2,1,0:T(8,128)S(1)} all-to-all(f32[128,24,128]{2,1,0:T(8,128)S(1)} %bitcast.18), channel_id=1, replica_groups=mesh['emit'=2,'slab'=64] {'slab','emit'}, dimensions={0} | all-to-all | bytes 3145728 | tf_op jit(solution)/shard_map/all_to_all | solution.py:489
  195.1 0.0 copy-done.10
  195.1 0.0 copy-start.15
  195.1 0.0 copy-start.16
  195.1 1.9 slab_last.1
  197.0 1.9 collective-permute-start
  198.9 46.9 %collective-permute-done = f32[2,4,256,256]{3,2,1,0:T(8,128)S(1)} collective-permute-done((f32[2,4,256,256]{3,2,1,0:T(8,128)S(1)}, f32[2,4,256,256]{3,2,1,0:T(8,128)S(1)}, u32[]{:S(2)}, u32[]{:S(2)}) %collective-permute-start) | collective-permute-done | bytes 2097184 | tf_op jit(solution)/shard_map/ppermute | solution.py:493
  245.8 0.0 copy-done.16
  245.8 1.8 fusion.1
  (17 shorter events, 0.0 us)
Async XLA Ops:
  8.4 63.6 %all-to-all-start = ((f32[128,4,8,256]{3,2,1,0:T(8,128)}), f32[128,4,8,256]{3,2,1,0:T(8,128)}, u32[]{:S(2)}, u32[]{:S(2)}) async-start(f32[128,4,8,256]{3,2,1,0:T(8,128)} %start.1), calls=%async_computation | async-start | bytes 8388608 | tf_op jit(solution)/shard_map/all_to_all | solution.py:489
  20.7 51.3 %copy-start.12 = (f32[256,256]{1,0:T(8,128)S(1)}, f32[256,256]{1,0:T(8,128)}, u32[]{:S(2)}) copy-start(f32[256,256]{1,0:T(8,128)} %constant.26.clone.tm) | copy-start | bytes 786436
  20.7 51.3 %copy-start.13 = (f32[256,256]{1,0:T(8,128)S(1)}, f32[256,256]{1,0:T(8,128)}, u32[]{:S(2)}) copy-start(f32[256,256]{1,0:T(8,128)} %constant.25.clone.gm) | copy-start | bytes 786436
  72.0 39.2 %copy-start.5 = (f32[4,256,256]{2,1,0:T(8,128)S(1)}, f32[4,256,256]{2,1,0:T(8,128)}, u32[]{:S(2)}) copy-start(f32[4,256,256]{2,1,0:T(8,128)} %get-tuple-element.51.pm) | copy-start | bytes 3145732
  72.0 39.2 %copy-start.6 = (f32[4,256,256]{2,1,0:T(8,128)S(1)}, f32[4,256,256]{2,1,0:T(8,128)}, u32[]{:S(2)}) copy-start(f32[4,256,256]{2,1,0:T(8,128)} %get-tuple-element.52.cdk) | copy-start | bytes 3145732
  72.0 39.2 %copy-start.7 = (f32[4,256,256]{2,1,0:T(8,128)S(1)}, f32[4,256,256]{2,1,0:T(8,128)}, u32[]{:S(2)}) copy-start(f32[4,256,256]{2,1,0:T(8,128)} %get-tuple-element.53.wb) | copy-start | bytes 3145732
  72.0 39.2 %copy-start.8 = (f32[4,256,256]{2,1,0:T(8,128)S(1)}, f32[4,256,256]{2,1,0:T(8,128)}, u32[]{:S(2)}) copy-start(f32[4,256,256]{2,1,0:T(8,128)} %get-tuple-element.54.yz1) | copy-start | bytes 3145732
  72.0 39.2 %copy-start.9 = (f32[128,8,256]{2,1,0:T(8,128)S(1)}, f32[128,8,256]{2,1,0:T(8,128)}, u32[]{:S(2)}) copy-start(f32[128,8,256]{2,1,0:T(8,128)} %get-tuple-element.45.axs) | copy-start | bytes 3145732
  77.1 34.2 %copy-start = (f32[4,256,256]{2,1,0:T(8,128)S(1)}, f32[4,256,256]{2,1,0:T(8,128)}, u32[]{:S(2)}) copy-start(f32[4,256,256]{2,1,0:T(8,128)} %get-tuple-element.48.dk) | copy-start | bytes 3145732
  77.1 34.2 %copy-start.1 = (f32[256,256]{1,0:T(8,128)S(1)}, f32[256,256]{1,0:T(8,128)}, u32[]{:S(2)}) copy-start(f32[256,256]{1,0:T(8,128)} %constant.24.clone.tm) | copy-start | bytes 786436
  77.1 34.2 %copy-start.2 = (f32[256,256]{1,0:T(8,128)S(1)}, f32[256,256]{1,0:T(8,128)}, u32[]{:S(2)}) copy-start(f32[256,256]{1,0:T(8,128)} %constant.23.clone.gm) | copy-start | bytes 786436
  77.1 34.2 %copy-start.3 = (f32[4,256,256]{2,1,0:T(8,128)S(1)}, f32[4,256,256]{2,1,0:T(8,128)}, u32[]{:S(2)}) copy-start(f32[4,256,256]{2,1,0:T(8,128)} %get-tuple-element.49.stay) | copy-start | bytes 3145732
  77.2 34.2 %copy-start.4 = (f32[4,256,256]{2,1,0:T(8,128)S(1)}, f32[4,256,256]{2,1,0:T(8,128)}, u32[]{:S(2)}) copy-start(f32[4,256,256]{2,1,0:T(8,128)} %get-tuple-element.50.b) | copy-start | bytes 3145732
  166.6 28.5 %copy-start.10 = (f32[4,256,256]{2,1,0:T(8,128)S(1)}, f32[4,256,256]{2,1,0:T(8,128)}, u32[]{:S(2)}) copy-start(f32[4,256,256]{2,1,0:T(8,128)} %get-tuple-element.62.gy0) | copy-start | bytes 3145732
  166.6 28.5 %copy-start.11 = (f32[4,256,256]{2,1,0:T(8,128)S(1)}, f32[4,256,256]{2,1,0:T(8,128)}, u32[]{:S(2)}) copy-start(f32[4,256,256]{2,1,0:T(8,128)} %get-tuple-element.63.gz0) | copy-start | bytes 3145732
  166.6 28.5 %copy-start.14 = (s32[2]{0:T(128)S(1)}, s32[2]{0:T(128)}, u32[]{:S(2)}) copy-start(s32[2]{0:T(128)} %pad_add_fusion.ids) | copy-start | bytes 28
  195.1 50.7 %copy-start.15 = (f32[4,256,256]{2,1,0:T(8,128)S(1)}, f32[4,256,256]{2,1,0:T(8,128)}, u32[]{:S(2)}) copy-start(f32[4,256,256]{2,1,0:T(8,128)} %c.3) | copy-start | bytes 3145732
  195.1 50.7 %copy-start.16 = (f32[4,256,256]{2,1,0:T(8,128)S(1)}, f32[4,256,256]{2,1,0:T(8,128)}, u32[]{:S(2)}) copy-start(f32[4,256,256]{2,1,0:T(8,128)} %rho.3) | copy-start | bytes 3145732
  197.0 48.8 %collective-permute-start = (f32[2,4,256,256]{3,2,1,0:T(8,128)S(1)}, f32[2,4,256,256]{3,2,1,0:T(8,128)S(1)}, u32[]{:S(2)}, u32[]{:S(2)}) collective-permute-start(f32[2,4,256,256]{3,2,1,0:T(8,128)S(1)} %slab_last.1), channel_id=1, source_target_pairs={{0,64},{64,0},{1,65},{65,1},{2,66},{66,2},{3,67},{67,3},{4,68},{68... | collective-permute-start | bytes 6291464 | tf_op jit(solution)/shard_map/ppermute | solution.py:493

commit v8 on v7

--- a/solution.py
+++ b/solution.py
@@ -448,41 +448,76 @@
     )[0]
 
 
-def last_kernel(ids, xs, d0, t1, t2, gy0, gz0, dk, gm, tm, out, p_s, bx_s, ms):
+def last_bulk_kernel(xs, d0, t1, out, p_s):
+    nx, ny, nz = d0.shape
+    half = nz // 2
+    for zh in range(2):
+        z = slice(zh * half, (zh + 1) * half)
+        p = swap(xs[:, 8 * zh : 8 * zh + 8, :]).reshape(nx, ny, half)
+        p_s[:, :, z] = p
+        out[:, :, z] = t1[:, :, z] + d0[:, :, z] * p
+
+
+def last_buoy_kernel(ids, xs, p_s, t2, gy0, gz0, dk, gm, tm, out, bx_s, ms):
     split_mats(gm, tm, ms)
-    nx, ny, nz = d0.shape
+    nx, ny, nz = t2.shape
     half = nz // 2
     t = swap(xs[:, 16:24, :]).reshape(4, ny, half)
     for zh in range(2):
-        z = slice(zh * half, (zh + 1) * half)
-        p_s[:, :, z] = swap(xs[:, 8 * zh : 8 * zh + 8, :]).reshape(nx, ny, half)
-        bx_s[:, :, z] = t[2 * zh : 2 * zh + 2]
-
+        bx_s[:, :, zh * half : (zh + 1) * half] = t[2 * zh : 2 * zh + 2]
     q = [dk[i] * p_s[i] for i in range(nx)]
     gy = [left(ms, G, v) for v in q]
     gz = [right(v, ms, T) for v in q]
     for i in range(nx):
-        out[0, i] = t1[i] + d0[i] * p_s[i]
-        out[1, i] = t2[i] + gy0[i] * gy[i] + gz0[i] * gz[i]
-
+        out[i] = t2[i] + gy0[i] * gy[i] + gz0[i] * gz[i]
     for xm in range(2):
-        out[1, 2 * ids[0] + xm] += bx_s[xm]
-
-
-def last_call(ids, xs, fields, mats):
+        out[2 * ids[0] + xm] += bx_s[xm]
+
+
+def last_buoy_call(ids, xs, fields, mats):
     nat = fields[0].shape
     vmem = pl.BlockSpec(memory_space=pltpu.VMEM)
     args = (xs, *fields, *mats)
     return pl.pallas_call(
-        last_kernel,
+        last_buoy_kernel,
         in_specs=[pl.BlockSpec(memory_space=pltpu.SMEM)] + [vmem] * len(args),
         out_specs=vmem,
-        out_shape=jax.ShapeDtypeStruct((2,) + nat, F32),
-        scratch_shapes=[pltpu.VMEM(nat, F32), pltpu.VMEM((2,) + nat[1:], F32), mats_scratch(mats)],
+        out_shape=jax.ShapeDtypeStruct(nat, F32),
+        scratch_shapes=[pltpu.VMEM((2,) + nat[1:], F32), mats_scratch(mats)],
         compiler_params=pltpu.CompilerParams(vmem_limit_bytes=LIMIT["last"] * MIB),
-        cost_estimate=cost(800, 9),
-        name="slab_last",
+        cost_estimate=cost(800, 8),
+        name="slab_last_buoy",
     )(ids, *args)
+
+
+def speed_kernel(t1, other, c, rho, out, part, weight):
+    @pl.loop(0, t1.shape[0])
+    def _(i):
+        s1 = DT * (t1[i] + other[i])
+        b = 1.0 / rho[i]
+        out[i] = 2.0 * s1 * rho[i] * c[i]
+        part[i] = s1 * c[i] * c[i]
+        weight[i] = DT * b * b
+
+
+def density_kernel(t2, other, part, weight, out):
+    @pl.loop(0, t2.shape[0])
+    def _(i):
+        out[i] = part[i] + (t2[i] + other[i]) * weight[i]
+
+
+def finish(kernel, args, n_out, estimate, name):
+    nat = args[-1].shape
+    vmem = pl.BlockSpec(memory_space=pltpu.VMEM)
+    return pl.pallas_call(
+        kernel,
+        in_specs=[vmem] * len(args),
+        out_specs=[vmem] * n_out,
+        out_shape=[jax.ShapeDtypeStruct(nat, F32)] * n_out,
+        compiler_params=pltpu.CompilerParams(vmem_limit_bytes=LIMIT["last"] * MIB),
+        cost_estimate=estimate,
+        name=name,
+    )(*args)
 
 
 def change_layout(v):
@@ -525,12 +560,14 @@
     qw = change_layout(qw).reshape(n_slab, n_emit, 3, 8, nz)
     xs = adjoint_call(qw, bk, gx0, gx1, line_mats)
     xs = change_layout(xs.reshape(ndev, 24, nz // 2))
-    t = last_call(ids, xs, [d0, t1, t2, fields[8], fields[9], fields[0]], mats)
-    other = swap_groups(t)
-    s1, s2 = t[0] + other[0], t[1] + other[1]
-    b = 1.0 / density
-    speed_total = (2.0 * DT) * s1 * density * sound_speed
-    density_total = DT * (s1 * sound_speed * sound_speed + s2 * b * b)
+    t1, p0 = finish(last_bulk_kernel, (xs, d0, t1), 2, cost(1, 5), "slab_last_bulk")
+    t2 = last_buoy_call(ids, xs, [p0, t2, fields[8], fields[9], fields[0]], mats)
+    speed_total, part, weight = finish(
+        speed_kernel, (t1, swap_groups(t1), sound_speed, density), 3, cost(3, 100), "finish_speed"
+    )
+    (density_total,) = finish(
+        density_kernel, (t2, swap_groups(t2), part, weight), 1, cost(3, 5), "finish_density"
+    )
     return speed_total, density_total
 
 

time: 248 us -> 246 us (level)
  waiting for transfers between devices: 80.2 us -> 75.1 us
  Pallas kernels: 42.2 us -> 45.1 us
    ppermute x1 -> x2, waiting for transfers between devices: 46.9 us -> 41.8 us  [swap_groups(): return lax.ppermute(v, 'emit', [(0, 1), (1, 0)])]
    pallas_call x1 -> x4, Pallas kernels: 1.88 us -> 4.73 us  [the longest x3 3 us: finish(): pl.pallas_call(kernel, in_specs=[vmem] * len(args), out_specs=[vmem] * n_...]
  transfers between devices with their start and end apart: 2 -> 3, of which waited for: 2 -> 3; matrix products, arithmetic and copies ran while one was open for 0% -> 0% of each run, Pallas kernels for 7% -> 9%
where the time goes in v8:
time: 246 us; the launch traced here: 245 us
  blocking collectives  108 us (44%)
  waiting for transfers between devices  75.1 us (31%)
  Pallas kernels  45.1 us (18%)
  starting transfers between devices  15.4 us (6%)
    all_to_all x3, blocking collectives, change_layout(): return lax.all_to_all(v, ALL, split_axis=0, concat_axis=0, tiled=True)  108 us
    ppermute x2, waiting for transfers between devices, swap_groups(): return lax.ppermute(v, 'emit', [(0, 1), (1, 0)])  41.8 us
    all_to_all x1, waiting for transfers between devices, change_layout(): return lax.all_to_all(v, ALL, split_axis=0, concat_axis=0, tiled=True)  33.2 us
    pallas_call x1, Pallas kernels, prepare_call(): pl.pallas_call(prepare_kernel, grid_spec=pltpu.PrefetchScalarGridSpec(num...  18.1 us
    pallas_call x3, Pallas kernels, on_chip(): pl.pallas_call(kernel, in_specs=[pl.BlockSpec(memory_space=pltpu.HBM)] *...  14.5 us
    all_to_all x1, starting transfers between devices, change_layout(): return lax.all_to_all(v, ALL, split_axis=0, concat_axis=0, tiled=True)  11.7 us
    pallas_call x1, Pallas kernels, start_call(): pl.pallas_call(start_kernel, in_specs=[smem] + [hbm] * 5 + [vmem] * 4, ou...  7.78 us
  transfers between devices with their start and end apart: 3, of which 3 were waited for; matrix products, arithmetic and copies ran while one was open for 0% of the time, Pallas kernels for 9%

profile of v8, /device:TPU:0, one launch (start us, length us, event | category | flops | bytes accessed | tf_op | source)
XLA Modules:
  0.0 245.4 jit_solution(6703118183853168945)
XLA Ops:
  0.6 7.8 %start.1 = f32[128,4,8,256]{3,2,1,0:T(8,128)} custom-call(f32[64]{0:T(128)} %drive.3, f32[4,256,256]{2,1,0:T(8,128)} %c.5, f32[4,256,256]{2,1,0:T(8,128)} %rho.5, f32[4,256,256]{2,1,0:T(8,128)} %alpha.3, f32[1,4,256,256]{3,2,1,0:T(8,128)} %p0.3, f32[1,3,4,256,256]{4,3,2,1,0:T(8,128)} %uz.1, s32[1,256]{1,0:T(1,128)} %epos.3, s32[1,256]{1,0:T(1,128)} %delay.3, ...), custom_call_target="tpu_custom_call" | custom-call | flops 2000000000 | bytes 13631488 | tf_op jit(solution)/shard_map/start/pallas_call | solution.py:191
  8.4 11.7 %all-to-all-start = ((f32[128,4,8,256]{3,2,1,0:T(8,128)}), f32[128,4,8,256]{3,2,1,0:T(8,128)}, u32[]{:S(2)}, u32[]{:S(2)}) async-start(f32[128,4,8,256]{3,2,1,0:T(8,128)} %start.1), calls=%async_computation | async-start | bytes 8388608 | tf_op jit(solution)/shard_map/all_to_all | solution.py:524
  20.1 0.6 pad_add_fusion.ids
  20.7 18.1 %prepare.1 = (f32[4,256,256]{2,1,0:T(8,128)}, f32[4,256,256]{2,1,0:T(8,128)}, f32[4,256,256]{2,1,0:T(8,128)}, f32[4,256,256]{2,1,0:T(8,128)}, f32[4,256,256]{2,1...) custom-call(s32[2]{0:T(128)} %pad_add_fusion.ids, ...), custom_call_target="tpu_custom_call" | custom-call | flops 8000000000 | bytes 23068672 | tf_op jit(solution)/shard_map/prepare/pallas_call | solution.py:263
  38.8 33.2 %all-to-all-done = f32[128,4,8,256]{3,2,1,0:T(8,128)} async-done(((f32[128,4,8,256]{3,2,1,0:T(8,128)}), f32[128,4,8,256]{3,2,1,0:T(8,128)}, u32[]{:S(2)}, u32[]{:S(2)}) %all-to-all-start) | async-done | bytes 4194336 | tf_op jit(solution)/shard_map/all_to_all | solution.py:524
  72.0 0.0 copy-done.14
  72.0 0.0 copy-done.15
  72.0 0.0 copy-start.11
  72.0 0.0 copy-start.12
  72.0 0.0 copy-start.13
  72.1 5.0 %lines_forward.1 = (f32[64,2,2,8,256]{4,3,2,1,0:T(8,128)S(1)}, f32[4,256,256]{2,1,0:T(8,128)S(1)}, f32[4,256,256]{2,1,0:T(8,128)S(1)}, f32[4,256,256]{2,1,0:T(8,128)S(1)}) custom-call(f32[64,2,4,8,256]{4,3,2,1,0:T(8,128)} %bitcast.3.lines, f32[256,256]{1,0:T(8,128)S(1)} %copy-done.15, f32[256,256]{1,0:T(8,128)S(1)} %copy-done.14), custom_call_target="tpu_custom_call" | custom-call | flops 1600000000 | bytes 9437184 | tf_op jit(solution)/shard_map/lines_forward/pallas_call | solution.py:291
  77.1 0.0 copy-start
  77.1 0.0 copy-start.3
  77.1 0.0 copy-start.4
  77.1 0.0 copy-start.7
  77.1 0.0 copy-start.8
  77.2 34.1 %all_to_all.20.xs = f32[128,2,8,256]{3,2,1,0:T(8,128)S(1)} all-to-all(f32[128,2,8,256]{3,2,1,0:T(8,128)S(1)} %bitcast.9), channel_id=1, replica_groups=mesh['emit'=2,'slab'=64] {'slab','emit'}, dimensions={0} | all-to-all | bytes 4194304 | tf_op jit(solution)/shard_map/all_to_all | solution.py:524
  111.2 0.0 copy-done.9
  111.3 7.2 %slab_middle.1 = (f32[128,3,8,256]{3,2,1,0:T(8,128)}, f32[4,256,256]{2,1,0:T(8,128)S(1)}, f32[4,256,256]{2,1,0:T(8,128)S(1)}, f32[4,256,256]{2,1,0:T(8,128)S(1)}) custom-call(f32[4,5,256,256]{3,2,1,0:T(8,128)} %get-tuple-element.49.late, f32[128,8,256]{2,1,0:T(8,128)S(1)} %copy-done.13, f32[128,2,8,256]{3,2,1,0:T(8,128)S(1)} %all_to_all.20.xs, ...), custom_call_target="tpu_custom_call" | custom-call | flops 3200000000 | bytes 18874368 | tf_op jit(solution)/shard_map/slab_middle/pallas_call | solution.py:291
  118.5 45.7 %all_to_all.21 = f32[128,3,8,256]{3,2,1,0:T(8,128)S(1)} all-to-all(f32[128,3,8,256]{3,2,1,0:T(8,128)} %get-tuple-element.60), channel_id=1, replica_groups=mesh['emit'=2,'slab'=64] {'slab','emit'}, dimensions={0} | all-to-all | bytes 6291456 | tf_op jit(solution)/shard_map/all_to_all | solution.py:524
  164.3 2.3 lines_adjoint.1
  166.6 28.5 %all_to_all.22.xs = f32[128,24,128]{2,1,0:T(8,128)S(1)} all-to-all(f32[128,24,128]{2,1,0:T(8,128)S(1)} %bitcast.8), channel_id=1, replica_groups=mesh['emit'=2,'slab'=64] {'slab','emit'}, dimensions={0} | all-to-all | bytes 3145728 | tf_op jit(solution)/shard_map/all_to_all | solution.py:524
  195.1 0.4 slab_last_bulk.1
  195.4 1.9 collective-permute-start
  197.3 0.0 copy-done.16
  197.3 0.0 copy-start.2
  197.3 1.7 slab_last_buoy.1.t2
  199.1 1.8 collective-permute-start.1
  200.9 22.2 %collective-permute-done.other = f32[4,256,256]{2,1,0:T(8,128)S(1)} collective-permute-done((f32[4,256,256]{2,1,0:T(8,128)S(1)}, f32[4,256,256]{2,1,0:T(8,128)S(1)}, u32[]{:S(2)}, u32[]{:S(2)}) %collective-permute-start) | collective-permute-done | bytes 1048608 | tf_op jit(solution)/shard_map/ppermute | solution.py:528
  223.1 1.5 finish_speed.1
  224.6 19.6 %collective-permute-done.1.other = f32[4,256,256]{2,1,0:T(8,128)S(1)} collective-permute-done((f32[4,256,256]{2,1,0:T(8,128)S(1)}, f32[4,256,256]{2,1,0:T(8,128)S(1)}, u32[]{:S(2)}, u32[]{:S(2)}) %collective-permute-start.1) | collective-permute-done | bytes 1048608 | tf_op jit(solution)/shard_map/ppermute | solution.py:528
  244.2 1.2 finish_density.1
  (21 shorter events, 0.0 us)
Async XLA Ops:
  8.4 63.6 %all-to-all-start = ((f32[128,4,8,256]{3,2,1,0:T(8,128)}), f32[128,4,8,256]{3,2,1,0:T(8,128)}, u32[]{:S(2)}, u32[]{:S(2)}) async-start(f32[128,4,8,256]{3,2,1,0:T(8,128)} %start.1), calls=%async_computation | async-start | bytes 8388608 | tf_op jit(solution)/shard_map/all_to_all | solution.py:524
  20.7 51.3 %copy-start.14 = (f32[256,256]{1,0:T(8,128)S(1)}, f32[256,256]{1,0:T(8,128)}, u32[]{:S(2)}) copy-start(f32[256,256]{1,0:T(8,128)} %constant.20.clone.tm) | copy-start | bytes 786436
  20.7 51.3 %copy-start.15 = (f32[256,256]{1,0:T(8,128)S(1)}, f32[256,256]{1,0:T(8,128)}, u32[]{:S(2)}) copy-start(f32[256,256]{1,0:T(8,128)} %constant.19.clone.gm) | copy-start | bytes 786436
  72.0 39.2 %copy-start.9 = (f32[4,256,256]{2,1,0:T(8,128)S(1)}, f32[4,256,256]{2,1,0:T(8,128)}, u32[]{:S(2)}) copy-start(f32[4,256,256]{2,1,0:T(8,128)} %get-tuple-element.56.pm) | copy-start | bytes 3145732
  72.0 39.2 %copy-start.10 = (f32[4,256,256]{2,1,0:T(8,128)S(1)}, f32[4,256,256]{2,1,0:T(8,128)}, u32[]{:S(2)}) copy-start(f32[4,256,256]{2,1,0:T(8,128)} %get-tuple-element.57.cdk) | copy-start | bytes 3145732
  72.0 39.2 %copy-start.11 = (f32[4,256,256]{2,1,0:T(8,128)S(1)}, f32[4,256,256]{2,1,0:T(8,128)}, u32[]{:S(2)}) copy-start(f32[4,256,256]{2,1,0:T(8,128)} %get-tuple-element.58.wb) | copy-start | bytes 3145732
  72.0 39.2 %copy-start.12 = (f32[4,256,256]{2,1,0:T(8,128)S(1)}, f32[4,256,256]{2,1,0:T(8,128)}, u32[]{:S(2)}) copy-start(f32[4,256,256]{2,1,0:T(8,128)} %get-tuple-element.59.yz1) | copy-start | bytes 3145732
  72.0 39.2 %copy-start.13 = (f32[128,8,256]{2,1,0:T(8,128)S(1)}, f32[128,8,256]{2,1,0:T(8,128)}, u32[]{:S(2)}) copy-start(f32[128,8,256]{2,1,0:T(8,128)} %get-tuple-element.50.axs) | copy-start | bytes 3145732
  77.1 34.2 %copy-start = (f32[4,256,256]{2,1,0:T(8,128)S(1)}, f32[4,256,256]{2,1,0:T(8,128)}, u32[]{:S(2)}) copy-start(f32[4,256,256]{2,1,0:T(8,128)} %get-tuple-element.53.dk) | copy-start | bytes 3145732
  77.1 34.2 %copy-start.3 = (f32[256,256]{1,0:T(8,128)S(1)}, f32[256,256]{1,0:T(8,128)}, u32[]{:S(2)}) copy-start(f32[256,256]{1,0:T(8,128)} %constant.18.clone.tm) | copy-start | bytes 786436
  77.1 34.2 %copy-start.4 = (f32[256,256]{1,0:T(8,128)S(1)}, f32[256,256]{1,0:T(8,128)}, u32[]{:S(2)}) copy-start(f32[256,256]{1,0:T(8,128)} %constant.17.clone.gm) | copy-start | bytes 786436
  77.1 34.2 %copy-start.7 = (f32[4,256,256]{2,1,0:T(8,128)S(1)}, f32[4,256,256]{2,1,0:T(8,128)}, u32[]{:S(2)}) copy-start(f32[4,256,256]{2,1,0:T(8,128)} %get-tuple-element.54.stay) | copy-start | bytes 3145732
  77.1 34.2 %copy-start.8 = (f32[4,256,256]{2,1,0:T(8,128)S(1)}, f32[4,256,256]{2,1,0:T(8,128)}, u32[]{:S(2)}) copy-start(f32[4,256,256]{2,1,0:T(8,128)} %get-tuple-element.55.b) | copy-start | bytes 3145732
  166.6 30.7 %copy-start.5 = (f32[4,256,256]{2,1,0:T(8,128)S(1)}, f32[4,256,256]{2,1,0:T(8,128)}, u32[]{:S(2)}) copy-start(f32[4,256,256]{2,1,0:T(8,128)} %get-tuple-element.70.gy0) | copy-start | bytes 3145732
  166.6 30.7 %copy-start.6 = (f32[4,256,256]{2,1,0:T(8,128)S(1)}, f32[4,256,256]{2,1,0:T(8,128)}, u32[]{:S(2)}) copy-start(f32[4,256,256]{2,1,0:T(8,128)} %get-tuple-element.71.gz0) | copy-start | bytes 3145732
  166.6 30.7 %copy-start.16 = (s32[2]{0:T(128)S(1)}, s32[2]{0:T(128)}, u32[]{:S(2)}) copy-start(s32[2]{0:T(128)} %pad_add_fusion.ids) | copy-start | bytes 28
  195.4 27.7 %collective-permute-start = (f32[4,256,256]{2,1,0:T(8,128)S(1)}, f32[4,256,256]{2,1,0:T(8,128)S(1)}, u32[]{:S(2)}, u32[]{:S(2)}) collective-permute-start(f32[4,256,256]{2,1,0:T(8,128)S(1)} %get-tuple-element.66.t1), channel_id=1, source_target_pairs={{0,64},{64,0},{1,65},{65,1},{2,66},{66,2},{3,67},{67,3},{4,68},{68... | collective-permute-start | bytes 3145736 | tf_op jit(solution)/shard_map/ppermute | solution.py:528
  197.3 25.8 %copy-start.1 = (f32[4,256,256]{2,1,0:T(8,128)S(1)}, f32[4,256,256]{2,1,0:T(8,128)}, u32[]{:S(2)}) copy-start(f32[4,256,256]{2,1,0:T(8,128)} %c.5) | copy-start | bytes 3145732
  197.3 25.8 %copy-start.2 = (f32[4,256,256]{2,1,0:T(8,128)S(1)}, f32[4,256,256]{2,1,0:T(8,128)}, u32[]{:S(2)}) copy-start(f32[4,256,256]{2,1,0:T(8,128)} %rho.5) | copy-start | bytes 3145732
  199.1 45.1 %collective-permute-start.1 = (f32[4,256,256]{2,1,0:T(8,128)S(1)}, f32[4,256,256]{2,1,0:T(8,128)S(1)}, u32[]{:S(2)}, u32[]{:S(2)}) collective-permute-start(f32[4,256,256]{2,1,0:T(8,128)S(1)} %slab_last_buoy.1.t2), channel_id=1, source_target_pairs={{0,64},{64,0},{1,65},{65,1},{2,66},{66,2},{3,67},{67,3},{4,68},{68... | collective-permute-start | bytes 3145736 | tf_op jit(solution)/shard_map/ppermute | solution.py:528

commit v9 on v8

--- a/solution.py
+++ b/solution.py
@@ -12,7 +12,7 @@
 BF16 = jnp.bfloat16
 ALL = ("slab", "emit")
 MIB = 2**20
-LIMIT = {"start": 60, "prepare": 60, "forward": 24, "middle": 40, "adjoint": 20, "last": 20}
+LIMIT = {"start": 60, "prepare": 60, "forward": 24, "middle": 32, "adjoint": 20, "last": 20}
 
 
 def deriv_matrix(n):
@@ -205,7 +205,7 @@
 
 def prepare_kernel(
     ids, drive, c, rho, alpha, p0, uy, uz, pa, ax, ay, az, spos, rec, epos, delay, gm, tm,
-    dk, stay, b, pm, cdk, wb, yz1, late, gy0, gz0, axs, ones, scols, ecols, pack, ms,
+    dk, stay, b, pm, cdk, wb, yz1, yz0_out, late, gy0, gz0, axs, ones, scols, ecols, pack, ms,
 ):
     i = pl.program_id(0)
     ny, nz = c.shape[1], c.shape[2]
@@ -242,7 +242,8 @@
     pm[0] = pa[0] + (count * (keep * v0 + (DT * bulk) * yz + shot) - m1)
     wb[0] = (count * v0 - m0) - DT * back
     yz1[0] = yz
-    for k, field in enumerate((yz0, gy + gyv, gz + gzv, ay[0], az[0])):
+    yz0_out[0] = yz0
+    for k, field in enumerate((gy + gyv, gz + gzv, ay[0], az[0])):
         late[0, k] = field
     gy0[0] = gy
     gz0[0] = gz
@@ -271,14 +272,14 @@
             + [whole((1, n_s)), pl.BlockSpec((None, STEPS, n_s), lambda i, ids: (0, 0, 0)),
                whole((1, n_e)), whole((1, n_e))]
             + [whole((ny, ny))] * 2,
-            out_specs=[plane] * 7 + [pl.BlockSpec((1, 5, ny, nz), lambda i, ids: (i, 0, 0, 0))]
+            out_specs=[plane] * 8 + [pl.BlockSpec((1, 4, ny, nz), lambda i, ids: (i, 0, 0, 0))]
             + [plane] * 2 + [whole((ny // 2, 2 * nx, nz))],
             scratch_shapes=[pltpu.VMEM((n_s, nz), BF16), pltpu.VMEM((STEPS, 3 * n_s, nz), BF16),
                             pltpu.VMEM((STEPS, 3 * n_e, nz), BF16),
                             pltpu.VMEM((2 * nx, ny // 2, nz), F32), mats_scratch(mats)],
         ),
-        out_shape=[jax.ShapeDtypeStruct(c.shape, F32)] * 7
-        + [jax.ShapeDtypeStruct((nx, 5, ny, nz), F32)] + [jax.ShapeDtypeStruct(c.shape, F32)] * 2
+        out_shape=[jax.ShapeDtypeStruct(c.shape, F32)] * 8
+        + [jax.ShapeDtypeStruct((nx, 4, ny, nz), F32)] + [jax.ShapeDtypeStruct(c.shape, F32)] * 2
         + [jax.ShapeDtypeStruct((ny // 2, 2 * nx, nz), F32)],
         compiler_params=params(LIMIT["prepare"]),
         cost_estimate=cost(8000, 22),
@@ -352,42 +353,34 @@
 
 
 def middle_kernel(
-    late, axs, xs, dk, stay, b, pm, cdk, wb, yz1, gm, tm,
-    buf, d0, t1, t2, x_s, o_s, ins, sems, ms,
+    axs, xs, dk, stay, b, pm, cdk, wb, yz1, yz0, gm, tm, buf, d0, t1, x_s, o_s, sem, ms
 ):
     nx, ny, nz = dk.shape
-    fetch = lambda i: pltpu.make_async_copy(late.at[i], ins.at[i], sems.at[i])
-    for i in range(nx):
-        fetch(i).start()
-    fetch_ax = pltpu.make_async_copy(axs, buf.at[:, 2], sems.at[nx])
+    fetch_ax = pltpu.make_async_copy(axs, buf.at[:, 2], sem)
     fetch_ax.start()
     split_mats(gm, tm, ms)
     for h in range(2):
         x_s[4 * h : 4 * h + 4] = swap(xs[:, h]).reshape(4, ny, nz)
 
-    def some(planes):
-        add = [dk[i] * x_s[2 * i] for i in planes]
-        ey = [left(ms, G, a) for a in add]
-        ez = [right(a, ms, T) for a in add]
-        gy = [left(ms, T, (DT * b[i]) * e) for i, e in zip(planes, ey)]
-        gz = [right((DT * b[i]) * e, ms, G) for i, e in zip(planes, ez)]
-        rest = [x_s[2 * i + 1] - (e + f) for i, e, f in zip(planes, gy, gz)]
-        adj = [pm[i] + cdk[i] * (stay[i] * x_s[2 * i] + r) for i, r in zip(planes, rest)]
-        q = [dk[i] * a for i, a in zip(planes, adj)]
-        fy = [left(ms, G, a) for a in q]
-        fz = [right(a, ms, T) for a in q]
-        for k, i in enumerate(planes):
-            o_s[2 * i] = q[k]
-            t1[i] = (yz1[i] + rest[k]) * adj[k]
-        gy = [left(ms, T, b[i] * e) for i, e in zip(planes, fy)]
-        gz = [right(b[i] * e, ms, G) for i, e in zip(planes, fz)]
-        for k, i in enumerate(planes):
-            o_s[2 * i + 1] = stay[i] * adj[k] + (cdk[i] * x_s[2 * i] + wb[i]) - DT * (gy[k] + gz[k])
-            fetch(i).wait()
-            d0[i] = x_s[2 * i] + ins[i, 0]
-            t2[i] = (ins[i, 1] + ey[k]) * (ins[i, 3] + fy[k]) + (ins[i, 2] + ez[k]) * (ins[i, 4] + fz[k])
-
-    some(range(nx))
+    at = range(nx)
+    add = [dk[i] * x_s[2 * i] for i in at]
+    ey = [left(ms, G, a) for a in add]
+    ez = [right(a, ms, T) for a in add]
+    gy = [left(ms, T, (DT * b[i]) * ey[i]) for i in at]
+    gz = [right((DT * b[i]) * ez[i], ms, G) for i in at]
+    rest = [x_s[2 * i + 1] - (gy[i] + gz[i]) for i in at]
+    adj = [pm[i] + cdk[i] * (stay[i] * x_s[2 * i] + rest[i]) for i in at]
+    q = [dk[i] * adj[i] for i in at]
+    fy = [left(ms, G, a) for a in q]
+    fz = [right(a, ms, T) for a in q]
+    for i in at:
+        o_s[2 * i] = q[i]
+        t1[i] = (yz1[i] + rest[i]) * adj[i]
+        d0[i] = x_s[2 * i] + yz0[i]
+    gy = [left(ms, T, b[i] * fy[i]) for i in at]
+    gz = [right(b[i] * fz[i], ms, G) for i in at]
+    for i in at:
+        o_s[2 * i + 1] = stay[i] * adj[i] + (cdk[i] * x_s[2 * i] + wb[i]) - DT * (gy[i] + gz[i])
 
     for h in range(2):
         buf[:, h] = swap(o_s[4 * h : 4 * h + 4].reshape(8, ny // 2, nz))
@@ -396,12 +389,11 @@
 
 def middle_call(xs, fields, mats):
     nat = fields[0].shape
-    saved = (8,) + nat[1:]
+    saved = (2 * nat[0],) + nat[1:]
     return on_chip(
-        middle_kernel, (fields[7], fields[10]), (xs, *fields[:7], *mats),
-        [(xs.shape[0], 3) + xs.shape[2:], nat, nat, nat],
-        [saved, saved, (nat[0], 5) + nat[1:], pltpu.SemaphoreType.DMA((nat[0] + 1,))],
-        LIMIT["middle"], cost(3200, 18), "slab_middle",
+        middle_kernel, (fields[11],), (xs, *fields[:8], *mats),
+        [(xs.shape[0], 3) + xs.shape[2:], nat, nat, saved, saved],
+        [pltpu.SemaphoreType.DMA], LIMIT["middle"], cost(3200, 18), "slab_middle",
     )
 
 
@@ -458,18 +450,24 @@
         out[:, :, z] = t1[:, :, z] + d0[:, :, z] * p
 
 
-def last_buoy_kernel(ids, xs, p_s, t2, gy0, gz0, dk, gm, tm, out, bx_s, ms):
+def last_buoy_kernel(ids, xs, p_s, dk, gy0, gz0, x_s, o_s, late, gm, tm, out, bx_s, ms):
     split_mats(gm, tm, ms)
-    nx, ny, nz = t2.shape
+    nx, ny, nz = dk.shape
     half = nz // 2
     t = swap(xs[:, 16:24, :]).reshape(4, ny, half)
     for zh in range(2):
         bx_s[:, :, zh * half : (zh + 1) * half] = t[2 * zh : 2 * zh + 2]
-    q = [dk[i] * p_s[i] for i in range(nx)]
-    gy = [left(ms, G, v) for v in q]
-    gz = [right(v, ms, T) for v in q]
-    for i in range(nx):
-        out[i] = t2[i] + gy0[i] * gy[i] + gz0[i] * gz[i]
+
+    @pl.loop(0, nx)
+    def _(i):
+        add = dk[i] * x_s[2 * i]
+        q1 = o_s[2 * i]
+        q0 = dk[i] * p_s[i]
+        ey, fy, gy = (left(ms, G, v) for v in (add, q1, q0))
+        ez, fz, gz = (right(v, ms, T) for v in (add, q1, q0))
+        late_y = (late[i, 0] + ey) * (late[i, 2] + fy) + gy0[i] * gy
+        out[i] = late_y + (late[i, 1] + ez) * (late[i, 3] + fz) + gz0[i] * gz
+
     for xm in range(2):
         out[2 * ids[0] + xm] += bx_s[xm]
 
@@ -485,7 +483,7 @@
         out_shape=jax.ShapeDtypeStruct(nat, F32),
         scratch_shapes=[pltpu.VMEM((2,) + nat[1:], F32), mats_scratch(mats)],
         compiler_params=pltpu.CompilerParams(vmem_limit_bytes=LIMIT["last"] * MIB),
-        cost_estimate=cost(800, 8),
+        cost_estimate=cost(2400, 16),
         name="slab_last_buoy",
     )(ids, *args)
 
@@ -556,12 +554,14 @@
     lines = lines.reshape(n_slab, n_emit, 4, 8, nz)
     xs, gx0, gx1, bk = forward_call(lines, line_mats)
     xs = change_layout(xs.reshape(ndev, 2, 8, nz))
-    qw, d0, t1, t2 = middle_call(xs, fields, mats)
+    qw, d0, t1, x_s, o_s = middle_call(xs, fields, mats)
     qw = change_layout(qw).reshape(n_slab, n_emit, 3, 8, nz)
     xs = adjoint_call(qw, bk, gx0, gx1, line_mats)
     xs = change_layout(xs.reshape(ndev, 24, nz // 2))
     t1, p0 = finish(last_bulk_kernel, (xs, d0, t1), 2, cost(1, 5), "slab_last_bulk")
-    t2 = last_buoy_call(ids, xs, [p0, t2, fields[8], fields[9], fields[0]], mats)
+    t2 = last_buoy_call(
+        ids, xs, [p0, fields[0], fields[9], fields[10], x_s, o_s, fields[8]], mats
+    )
     speed_total, part, weight = finish(
         speed_kernel, (t1, swap_groups(t1), sound_speed, density), 3, cost(3, 100), "finish_speed"
     )

time: 246 us -> 243 us (0.988)
    pallas_call x3, Pallas kernels: 14.5 us -> 12 us  [on_chip(): pl.pallas_call(kernel, in_specs=[pl.BlockSpec(memory_space=pltpu.HBM)] *...]
  transfers between devices with their start and end apart: 3 -> 3, of which waited for: 3 -> 3; matrix products, arithmetic and copies ran while one was open for 0% -> 0% of each run, Pallas kernels for 9% -> 10%
where the time goes in v9:
time: 243 us; the launch traced here: 242 us
  blocking collectives  108 us (44%)
  waiting for transfers between devices  72.7 us (30%)
  Pallas kernels  44.8 us (18%)
  starting transfers between devices  15.4 us (6%)
    all_to_all x3, blocking collectives, change_layout(): return lax.all_to_all(v, ALL, split_axis=0, concat_axis=0, tiled=True)  108 us
    ppermute x2, waiting for transfers between devices, swap_groups(): return lax.ppermute(v, 'emit', [(0, 1), (1, 0)])  39.6 us
    all_to_all x1, waiting for transfers between devices, change_layout(): return lax.all_to_all(v, ALL, split_axis=0, concat_axis=0, tiled=True)  33.2 us
    pallas_call x1, Pallas kernels, prepare_call(): pl.pallas_call(prepare_kernel, grid_spec=pltpu.PrefetchScalarGridSpec(num...  18.1 us
    pallas_call x3, Pallas kernels, on_chip(): pl.pallas_call(kernel, in_specs=[pl.BlockSpec(memory_space=pltpu.HBM)] *...  12 us
    all_to_all x1, starting transfers between devices, change_layout(): return lax.all_to_all(v, ALL, split_axis=0, concat_axis=0, tiled=True)  11.7 us
    pallas_call x1, Pallas kernels, start_call(): pl.pallas_call(start_kernel, in_specs=[smem] + [hbm] * 5 + [vmem] * 4, ou...  7.77 us
  transfers between devices with their start and end apart: 3, of which 3 were waited for; matrix products, arithmetic and copies ran while one was open for 0% of the time, Pallas kernels for 10%

profile of v9, /device:TPU:0, one launch (start us, length us, event | category | flops | bytes accessed | tf_op | source)
XLA Modules:
  0.0 242.2 jit_solution(1900200665470802910)
XLA Ops:
  0.6 7.8 %start.1 = f32[128,4,8,256]{3,2,1,0:T(8,128)} custom-call(f32[64]{0:T(128)} %drive.3, f32[4,256,256]{2,1,0:T(8,128)} %c.5, f32[4,256,256]{2,1,0:T(8,128)} %rho.5, f32[4,256,256]{2,1,0:T(8,128)} %alpha.3, f32[1,4,256,256]{3,2,1,0:T(8,128)} %p0.3, f32[1,3,4,256,256]{4,3,2,1,0:T(8,128)} %uz.1, s32[1,256]{1,0:T(1,128)} %epos.3, s32[1,256]{1,0:T(1,128)} %delay.3, ...), custom_call_target="tpu_custom_call" | custom-call | flops 2000000000 | bytes 13631488 | tf_op jit(solution)/shard_map/start/pallas_call | solution.py:191
  8.4 11.7 %all-to-all-start = ((f32[128,4,8,256]{3,2,1,0:T(8,128)}), f32[128,4,8,256]{3,2,1,0:T(8,128)}, u32[]{:S(2)}, u32[]{:S(2)}) async-start(f32[128,4,8,256]{3,2,1,0:T(8,128)} %start.1), calls=%async_computation | async-start | bytes 8388608 | tf_op jit(solution)/shard_map/all_to_all | solution.py:522
  20.1 0.7 pad_add_fusion.ids
  20.8 18.1 %prepare.1 = (f32[4,256,256]{2,1,0:T(8,128)}, f32[4,256,256]{2,1,0:T(8,128)}, f32[4,256,256]{2,1,0:T(8,128)}, f32[4,256,256]{2,1,0:T(8,128)}, f32[4,256,256]{2,1...) custom-call(s32[2]{0:T(128)} %pad_add_fusion.ids, ...), custom_call_target="tpu_custom_call" | custom-call | flops 8000000000 | bytes 23068672 | tf_op jit(solution)/shard_map/prepare/pallas_call | solution.py:264
  38.8 33.2 %all-to-all-done = f32[128,4,8,256]{3,2,1,0:T(8,128)} async-done(((f32[128,4,8,256]{3,2,1,0:T(8,128)}), f32[128,4,8,256]{3,2,1,0:T(8,128)}, u32[]{:S(2)}, u32[]{:S(2)}) %all-to-all-start) | async-done | bytes 4194336 | tf_op jit(solution)/shard_map/all_to_all | solution.py:522
  72.1 5.0 %lines_forward.1 = (f32[64,2,2,8,256]{4,3,2,1,0:T(8,128)S(1)}, f32[4,256,256]{2,1,0:T(8,128)S(1)}, f32[4,256,256]{2,1,0:T(8,128)S(1)}, f32[4,256,256]{2,1,0:T(8,128)S(1)}) custom-call(f32[64,2,4,8,256]{4,3,2,1,0:T(8,128)} %bitcast.3.lines, f32[256,256]{1,0:T(8,128)S(1)} %copy-done.17, f32[256,256]{1,0:T(8,128)S(1)} %copy-done.16), custom_call_target="tpu_custom_call" | custom-call | flops 1600000000 | bytes 9437184 | tf_op jit(solution)/shard_map/lines_forward/pallas_call | solution.py:292
  77.1 0.0 copy-start.1
  77.1 0.0 copy-start.4
  77.1 0.0 copy-start.5
  77.1 0.0 copy-start.8
  77.1 0.0 copy-start.9
  77.2 34.1 %all_to_all.20.xs = f32[128,2,8,256]{3,2,1,0:T(8,128)S(1)} all-to-all(f32[128,2,8,256]{3,2,1,0:T(8,128)S(1)} %bitcast.9), channel_id=1, replica_groups=mesh['emit'=2,'slab'=64] {'slab','emit'}, dimensions={0} | all-to-all | bytes 4194304 | tf_op jit(solution)/shard_map/all_to_all | solution.py:522
  111.2 0.0 copy-done.11
  111.3 4.6 %slab_middle.1 = (f32[128,3,8,256]{3,2,1,0:T(8,128)S(1)}, f32[4,256,256]{2,1,0:T(8,128)S(1)}, f32[4,256,256]{2,1,0:T(8,128)S(1)}, f32[8,256,256]{2,1,0:T(8,128)S(1)}, f32[8,256,256]{2,1,0:T(8,128)S(1)}) custom-call(f32[128,8,256]{2,1,0:T(8,128)S(1)} %copy-done.15, f32[128,2,8,256]{3,2,1,0:T(8,128)S(1)} %all_to_all.20.xs, f32[4,256,256]{2,1,0:T(8,128)S(1)} %copy-done.1, ...), custom_call_target="tpu_custom_call" | custom-call | flops 3200000000 | bytes 18874368 | tf_op jit(solution)/shard_map/slab_middle/pallas_call | solution.py:292
  116.0 45.1 %all_to_all.21 = f32[128,3,8,256]{3,2,1,0:T(8,128)S(1)} all-to-all(f32[128,3,8,256]{3,2,1,0:T(8,128)S(1)} %get-tuple-element.64), channel_id=1, replica_groups=mesh['emit'=2,'slab'=64] {'slab','emit'}, dimensions={0} | all-to-all | bytes 6291456 | tf_op jit(solution)/shard_map/all_to_all | solution.py:522
  161.1 2.3 lines_adjoint.1
  163.4 0.0 copy-start
  163.4 0.0 copy-start.6
  163.4 0.0 copy-start.7
  163.4 0.0 copy-start.18
  163.5 28.4 %all_to_all.22.xs = f32[128,24,128]{2,1,0:T(8,128)S(1)} all-to-all(f32[128,24,128]{2,1,0:T(8,128)S(1)} %bitcast.8), channel_id=1, replica_groups=mesh['emit'=2,'slab'=64] {'slab','emit'}, dimensions={0} | all-to-all | bytes 3145728 | tf_op jit(solution)/shard_map/all_to_all | solution.py:522
  191.9 0.4 slab_last_bulk.1
  192.3 1.9 collective-permute-start
  194.1 0.0 copy-done.7
  194.2 0.0 copy-start.2
  194.2 0.0 copy-start.3
  194.2 4.0 %slab_last_buoy.1.t2 = f32[4,256,256]{2,1,0:T(8,128)S(1)} custom-call(s32[2]{0:T(128)S(1)} %copy-done.18, f32[128,24,128]{2,1,0:T(8,128)S(1)} %all_to_all.22.xs, f32[4,256,256]{2,1,0:T(8,128)S(1)} %get-tuple-element.72.p_s, f32[4,256,256]{2,1,0:T(8,128)S(1)} %copy-done.1, f32[4,256,256]{2,1,0:T(8,128)S(1)} %copy-done.6, f32[4,256,256]{2,1,0:T(8,128)S(1)} %copy-done.7, ...), custom_call_target="tpu_custom_call" | custom-call | flops 2400000000 | bytes 16777216 | tf_op jit(solution)/shard_map/slab_last_buoy/pallas_call | solution.py:479
  198.2 1.8 collective-permute-start.1
  200.0 19.9 %collective-permute-done.other = f32[4,256,256]{2,1,0:T(8,128)S(1)} collective-permute-done((f32[4,256,256]{2,1,0:T(8,128)S(1)}, f32[4,256,256]{2,1,0:T(8,128)S(1)}, u32[]{:S(2)}, u32[]{:S(2)}) %collective-permute-start) | collective-permute-done | bytes 1048608 | tf_op jit(solution)/shard_map/ppermute | solution.py:526
  219.9 1.4 finish_speed.1
  221.4 19.7 %collective-permute-done.1.other = f32[4,256,256]{2,1,0:T(8,128)S(1)} collective-permute-done((f32[4,256,256]{2,1,0:T(8,128)S(1)}, f32[4,256,256]{2,1,0:T(8,128)S(1)}, u32[]{:S(2)}, u32[]{:S(2)}) %collective-permute-start.1) | collective-permute-done | bytes 1048608 | tf_op jit(solution)/shard_map/ppermute | solution.py:526
  241.1 1.2 finish_density.1
  (25 shorter events, 0.1 us)
Async XLA Ops:
  8.4 63.6 %all-to-all-start = ((f32[128,4,8,256]{3,2,1,0:T(8,128)}), f32[128,4,8,256]{3,2,1,0:T(8,128)}, u32[]{:S(2)}, u32[]{:S(2)}) async-start(f32[128,4,8,256]{3,2,1,0:T(8,128)} %start.1), calls=%async_computation | async-start | bytes 8388608 | tf_op jit(solution)/shard_map/all_to_all | solution.py:522
  20.8 51.2 %copy-start.16 = (f32[256,256]{1,0:T(8,128)S(1)}, f32[256,256]{1,0:T(8,128)}, u32[]{:S(2)}) copy-start(f32[256,256]{1,0:T(8,128)} %constant.20.clone.tm) | copy-start | bytes 786436
  20.8 51.2 %copy-start.17 = (f32[256,256]{1,0:T(8,128)S(1)}, f32[256,256]{1,0:T(8,128)}, u32[]{:S(2)}) copy-start(f32[256,256]{1,0:T(8,128)} %constant.19.clone.gm) | copy-start | bytes 786436
  72.0 39.2 %copy-start.10 = (f32[4,256,256]{2,1,0:T(8,128)S(1)}, f32[4,256,256]{2,1,0:T(8,128)}, u32[]{:S(2)}) copy-start(f32[4,256,256]{2,1,0:T(8,128)} %get-tuple-element.59.pm) | copy-start | bytes 3145732
  72.0 39.2 %copy-start.11 = (f32[4,256,256]{2,1,0:T(8,128)S(1)}, f32[4,256,256]{2,1,0:T(8,128)}, u32[]{:S(2)}) copy-start(f32[4,256,256]{2,1,0:T(8,128)} %get-tuple-element.60.cdk) | copy-start | bytes 3145732
  72.0 39.2 %copy-start.12 = (f32[4,256,256]{2,1,0:T(8,128)S(1)}, f32[4,256,256]{2,1,0:T(8,128)}, u32[]{:S(2)}) copy-start(f32[4,256,256]{2,1,0:T(8,128)} %get-tuple-element.61.wb) | copy-start | bytes 3145732
  72.0 39.2 %copy-start.13 = (f32[4,256,256]{2,1,0:T(8,128)S(1)}, f32[4,256,256]{2,1,0:T(8,128)}, u32[]{:S(2)}) copy-start(f32[4,256,256]{2,1,0:T(8,128)} %get-tuple-element.62.yz1) | copy-start | bytes 3145732
  72.0 39.2 %copy-start.14 = (f32[4,256,256]{2,1,0:T(8,128)S(1)}, f32[4,256,256]{2,1,0:T(8,128)}, u32[]{:S(2)}) copy-start(f32[4,256,256]{2,1,0:T(8,128)} %get-tuple-element.63.yz0) | copy-start | bytes 3145732
  72.0 39.2 %copy-start.15 = (f32[128,8,256]{2,1,0:T(8,128)S(1)}, f32[128,8,256]{2,1,0:T(8,128)}, u32[]{:S(2)}) copy-start(f32[128,8,256]{2,1,0:T(8,128)} %get-tuple-element.53.axs) | copy-start | bytes 3145732
  77.1 34.2 %copy-start.1 = (f32[4,256,256]{2,1,0:T(8,128)S(1)}, f32[4,256,256]{2,1,0:T(8,128)}, u32[]{:S(2)}) copy-start(f32[4,256,256]{2,1,0:T(8,128)} %get-tuple-element.56.dk) | copy-start | bytes 3145732
  77.1 34.2 %copy-start.4 = (f32[256,256]{1,0:T(8,128)S(1)}, f32[256,256]{1,0:T(8,128)}, u32[]{:S(2)}) copy-start(f32[256,256]{1,0:T(8,128)} %constant.18.clone.tm) | copy-start | bytes 786436
  77.1 34.2 %copy-start.5 = (f32[256,256]{1,0:T(8,128)S(1)}, f32[256,256]{1,0:T(8,128)}, u32[]{:S(2)}) copy-start(f32[256,256]{1,0:T(8,128)} %constant.17.clone.gm) | copy-start | bytes 786436
  77.1 34.2 %copy-start.8 = (f32[4,256,256]{2,1,0:T(8,128)S(1)}, f32[4,256,256]{2,1,0:T(8,128)}, u32[]{:S(2)}) copy-start(f32[4,256,256]{2,1,0:T(8,128)} %get-tuple-element.57.stay) | copy-start | bytes 3145732
  77.1 34.2 %copy-start.9 = (f32[4,256,256]{2,1,0:T(8,128)S(1)}, f32[4,256,256]{2,1,0:T(8,128)}, u32[]{:S(2)}) copy-start(f32[4,256,256]{2,1,0:T(8,128)} %get-tuple-element.58.b) | copy-start | bytes 3145732
  163.4 30.7 %copy-start = (f32[4,4,256,256]{3,2,1,0:T(8,128)S(1)}, f32[4,4,256,256]{3,2,1,0:T(8,128)}, u32[]{:S(2)}) copy-start(f32[4,4,256,256]{3,2,1,0:T(8,128)} %get-tuple-element.77.late) | copy-start | bytes 12582916
  163.4 30.7 %copy-start.6 = (f32[4,256,256]{2,1,0:T(8,128)S(1)}, f32[4,256,256]{2,1,0:T(8,128)}, u32[]{:S(2)}) copy-start(f32[4,256,256]{2,1,0:T(8,128)} %get-tuple-element.73.gy0) | copy-start | bytes 3145732
  163.4 30.7 %copy-start.7 = (f32[4,256,256]{2,1,0:T(8,128)S(1)}, f32[4,256,256]{2,1,0:T(8,128)}, u32[]{:S(2)}) copy-start(f32[4,256,256]{2,1,0:T(8,128)} %get-tuple-element.74.gz0) | copy-start | bytes 3145732
  163.4 30.7 %copy-start.18 = (s32[2]{0:T(128)S(1)}, s32[2]{0:T(128)}, u32[]{:S(2)}) copy-start(s32[2]{0:T(128)} %pad_add_fusion.ids) | copy-start | bytes 28
  192.3 27.7 %collective-permute-start = (f32[4,256,256]{2,1,0:T(8,128)S(1)}, f32[4,256,256]{2,1,0:T(8,128)S(1)}, u32[]{:S(2)}, u32[]{:S(2)}) collective-permute-start(f32[4,256,256]{2,1,0:T(8,128)S(1)} %get-tuple-element.70.t1), channel_id=1, source_target_pairs={{0,64},{64,0},{1,65},{65,1},{2,66},{66,2},{3,67},{67,3},{4,68},{68... | collective-permute-start | bytes 3145736 | tf_op jit(solution)/shard_map/ppermute | solution.py:526
  194.2 25.8 %copy-start.2 = (f32[4,256,256]{2,1,0:T(8,128)S(1)}, f32[4,256,256]{2,1,0:T(8,128)}, u32[]{:S(2)}) copy-start(f32[4,256,256]{2,1,0:T(8,128)} %c.5) | copy-start | bytes 3145732
  194.2 25.8 %copy-start.3 = (f32[4,256,256]{2,1,0:T(8,128)S(1)}, f32[4,256,256]{2,1,0:T(8,128)}, u32[]{:S(2)}) copy-start(f32[4,256,256]{2,1,0:T(8,128)} %rho.5) | copy-start | bytes 3145732
  198.2 42.8 %collective-permute-start.1 = (f32[4,256,256]{2,1,0:T(8,128)S(1)}, f32[4,256,256]{2,1,0:T(8,128)S(1)}, u32[]{:S(2)}, u32[]{:S(2)}) collective-permute-start(f32[4,256,256]{2,1,0:T(8,128)S(1)} %slab_last_buoy.1.t2), channel_id=1, source_target_pairs={{0,64},{64,0},{1,65},{65,1},{2,66},{66,2},{3,67},{67,3},{4,68},{68... | collective-permute-start | bytes 3145736 | tf_op jit(solution)/shard_map/ppermute | solution.py:526

commit v10 on v9

--- a/solution.py
+++ b/solution.py
@@ -136,52 +136,48 @@
     return list(zip(gy, gz, wy, wz, yz, v0, b, bulk))
 
 
-def plane_copies(srcs, dst, sems, i):
-    return [
-        pltpu.make_async_copy(src.at[pl.ds(i, 1)], dst.at[i, pl.ds(k, 1)], sems.at[i, k])
-        for k, src in enumerate(srcs)
-    ]
-
-
 def start_kernel(
-    drive, c, rho, alpha, p0, u, epos, delay, gm, tm, buf, ins, sems, outs, out_sems, cols, pack, ms
+    drive, c, rho, alpha, p0, u, epos, delay, gm, tm, buf, ins, sems, outs, out_sems, cols, ms
 ):
     emit, slab = lax.axis_index("emit"), lax.axis_index("slab")
     nx, ny, nz = c.shape
-    half = ny // 2
-
-    def send(i):
-        return pltpu.make_async_copy(outs.at[i], buf.at[:, i], out_sems.at[i])
-
-    srcs = (p0.at[0], c, rho, alpha, u.at[0, 1], u.at[0, 2], u.at[0, 0])
-    for fields in (slice(0, 6), slice(6, 7)):
-        for i in range(nx):
-            for copy in plane_copies(srcs, ins, sems, i)[fields]:
-                copy.start()
+    at = range(nx)
+    srcs = (p0.at[0], rho, u.at[0, 1], u.at[0, 2], c, alpha, u.at[0, 0])
+    copies = [pltpu.make_async_copy(src, ins.at[k], sems.at[k]) for k, src in enumerate(srcs)]
+    for copy in copies:
+        copy.start()
+
+    def send(f, field):
+        outs[f] = swap(field.reshape(2 * nx, ny // 2, nz))
+        copy = pltpu.make_async_copy(outs.at[f], buf.at[:, f], out_sems.at[f])
+        copy.start()
+        return copy
+
     split_mats(gm, tm, ms)
     cols[...] = three(column_onehot(epos[...], nz), drive_at(delay[...], drive, 0))
-
-    @pl.loop(0, nx // 2)
-    def _(k):
-        pair = (2 * k, 2 * k + 1)
-        for i in pair:
-            for copy in plane_copies(srcs, ins, sems, i)[:6]:
-                copy.wait()
-        steps = first_step(
-            [tuple(ins[i, f] for f in (1, 2, 3, 0, 4, 5)) for i in pair],
-            cols, epos, [slab * nx + i for i in pair], ms,
-        )
-        for xm, i in enumerate(pair):
-            v0, b, bulk = steps[xm][5:]
-            for copy in plane_copies(srcs, ins, sems, i)[6:]:
-                copy.wait()
-            for f, field in enumerate((ins[i, 0], ins[i, 6], v0, jnp.where(emit == 0, b, bulk))):
-                pack[xm, 2 * f : 2 * f + 2] = field.reshape(2, half, nz)
-            outs[i] = swap(pack[xm])
-            send(i).start()
-
-    for i in range(nx):
-        send(i).wait()
+    shot = [spread(plane_onehot(epos[...], slab * nx + i, ny, nz), cols[...]) for i in at]
+    copies[0].wait()
+    gy = [left(ms, G, ins[0, i]) for i in at]
+    gz = [right(ins[0, i], ms, T) for i in at]
+    sent = [send(0, ins[0])]
+    for k in (1, 2, 3):
+        copies[k].wait()
+    b = [1.0 / ins[1, i] for i in at]
+    yz = [left(ms, T, ins[2, i] - DT * b[i] * gy[i]) for i in at]
+    zz = [right(ins[3, i] - DT * b[i] * gz[i], ms, G) for i in at]
+    copies[4].wait()
+    bulk = [ins[1, i] * ins[4, i] * ins[4, i] for i in at]
+    for i in at:
+        ins[1, i] = jnp.where(emit == 0, b[i], bulk[i])
+    sent.append(send(3, ins[1]))
+    copies[6].wait()
+    sent.append(send(1, ins[6]))
+    copies[5].wait()
+    for i in at:
+        ins[2, i] = (1.0 - DT * ins[5, i]) * ins[0, i] + (DT * bulk[i]) * (yz[i] + zz[i]) + shot[i]
+    sent.append(send(2, ins[2]))
+    for copy in sent:
+        copy.wait()
 
 
 def start_call(c, rho, alpha, p0, u, epos, delay, drive, mats, ndev):
@@ -192,11 +188,10 @@
         start_kernel,
         in_specs=[smem] + [hbm] * 5 + [vmem] * 4,
         out_specs=hbm,
-        out_shape=jax.ShapeDtypeStruct((ndev, nx, 8, nz), F32),
-        scratch_shapes=[pltpu.VMEM((nx, 7, ny, nz), F32), pltpu.SemaphoreType.DMA((nx, 7)),
-                        pltpu.VMEM((nx, ndev, 8, nz), F32), pltpu.SemaphoreType.DMA((nx,)),
-                        pltpu.VMEM((3 * n_e, nz), BF16),
-                        pltpu.VMEM((2, 8, ndev, nz), F32), mats_scratch(mats)],
+        out_shape=jax.ShapeDtypeStruct((ndev, 4, 2 * nx, nz), F32),
+        scratch_shapes=[pltpu.VMEM((7, nx, ny, nz), F32), pltpu.SemaphoreType.DMA((7,)),
+                        pltpu.VMEM((4, ndev, 2 * nx, nz), F32), pltpu.SemaphoreType.DMA((4,)),
+                        pltpu.VMEM((3 * n_e, nz), BF16), mats_scratch(mats)],
         compiler_params=pltpu.CompilerParams(vmem_limit_bytes=LIMIT["start"] * MIB),
         cost_estimate=cost(2000, 13),
         name="start",
@@ -311,23 +306,28 @@
 
 def forward_kernel(lines, gm, tm, out, gx0, gx1, bk, in_s, sems, f_s, o_s, ms):
     n = lines.shape[0]
-    fetch = lambda g: pltpu.make_async_copy(lines.at[:, g], in_s.at[g], sems.at[g])
     groups, at = range(2), range(4)
-    for g in groups:
-        fetch(g).start()
+    order = (0, 3, 1, 2)
+    copies = {f: pltpu.make_async_copy(lines.at[:, :, f], in_s.at[f], sems.at[f]) for f in order}
+    for f in order:
+        copies[f].start()
+
+    def take(f, dst):
+        copies[f].wait()
+        for g in groups:
+            t = swap(in_s[f, :, g])
+            for xl in range(4):
+                dst[2 * g : 2 * g + 2, xl * n : (xl + 1) * n, :] = t[2 * xl : 2 * xl + 2]
+
     split_mats(gm, tm, ms)
-    g0, u1, x0 = [], [], []
-    for g in groups:
-        fetch(g).wait()
-        for xl in range(4):
-            rows = slice(xl * n, (xl + 1) * n)
-            t = swap(in_s[g, :, xl])
-            f_s[g, :, rows, :] = t[:6]
-            bk[2 * g : 2 * g + 2, rows, :] = t[6:]
-        g0 += [left(ms, G, f_s[g, yl]) for yl in range(2)]
-        u1 += [f_s[g, 2 + yl] - (DT * bk[yl]) * g0[2 * g + yl] for yl in range(2)]
-        x0 += [left(ms, T, u1[2 * g + yl]) for yl in range(2)]
-    p1 = [f_s[j // 2, 4 + j % 2] + (DT * bk[2 + j % 2]) * x0[j] for j in at]
+    take(0, f_s.at[0])
+    g0 = [left(ms, G, f_s[0, j]) for j in at]
+    take(3, bk)
+    take(1, f_s.at[1])
+    u1 = [f_s[1, j] - (DT * bk[j % 2]) * g0[j] for j in at]
+    x0 = [left(ms, T, u1[j]) for j in at]
+    take(2, f_s.at[2])
+    p1 = [f_s[2, j] + (DT * bk[2 + j % 2]) * x0[j] for j in at]
     g1 = [left(ms, G, p1[j]) for j in at]
     x1 = [left(ms, T, u1[j] - (DT * bk[j % 2]) * g1[j]) for j in at]
     for j in at:
@@ -347,7 +347,7 @@
     full = (4, nx, nz)
     return on_chip(
         forward_kernel, (lines,), mats, [(ns, 2, 2, 8, nz), full, full, full],
-        [(2, ns, 4, 8, nz), pltpu.SemaphoreType.DMA((2,)), (2, 6, nx, nz), (2, 4, nx, nz)],
+        [(4, ns, 2, 8, nz), pltpu.SemaphoreType.DMA((4,)), (3, 4, nx, nz), (2, 4, nx, nz)],
         LIMIT["forward"], cost(1600, 9), "lines_forward",
     )
 

time: 243 us -> 241 us (level)
  no operation moved by 1% of the time
where the time goes in v10:
time: 241 us
  blocking collectives  108 us (45%)
  waiting for transfers between devices  72.6 us (30%)
  Pallas kernels  43.5 us (18%)
  starting transfers between devices  15.6 us (6%)
    all_to_all x3, blocking collectives, change_layout(): return lax.all_to_all(v, ALL, split_axis=0, concat_axis=0, tiled=True)  108 us
    ppermute x2, waiting for transfers between devices, swap_groups(): return lax.ppermute(v, 'emit', [(0, 1), (1, 0)])  39.6 us
    all_to_all x1, waiting for transfers between devices, change_layout(): return lax.all_to_all(v, ALL, split_axis=0, concat_axis=0, tiled=True)  33 us
    pallas_call x1, Pallas kernels, prepare_call(): pl.pallas_call(prepare_kernel, grid_spec=pltpu.PrefetchScalarGridSpec(num...  18 us
    all_to_all x1, starting transfers between devices, change_layout(): return lax.all_to_all(v, ALL, split_axis=0, concat_axis=0, tiled=True)  11.9 us
    pallas_call x3, Pallas kernels, on_chip(): pl.pallas_call(kernel, in_specs=[pl.BlockSpec(memory_space=pltpu.HBM)] *...  11.6 us
    pallas_call x1, Pallas kernels, start_call(): pl.pallas_call(start_kernel, in_specs=[smem] + [hbm] * 5 + [vmem] * 4, ou...  6.96 us
  transfers between devices with their start and end apart: 3, of which 3 were waited for; matrix products, arithmetic and copies ran while one was open for 0% of the time, Pallas kernels for 10%

profile of v10, /device:TPU:0, one launch (start us, length us, event | category | flops | bytes accessed | tf_op | source)
XLA Modules:
  0.0 241.0 jit_solution(9675812984773385404)
XLA Ops:
  0.6 7.0 %start.1 = f32[128,4,8,256]{3,2,1,0:T(8,128)} custom-call(f32[64]{0:T(128)} %drive.3, f32[4,256,256]{2,1,0:T(8,128)} %c.5, f32[4,256,256]{2,1,0:T(8,128)} %rho.5, f32[4,256,256]{2,1,0:T(8,128)} %alpha.3, f32[1,4,256,256]{3,2,1,0:T(8,128)} %p0.3, f32[1,3,4,256,256]{4,3,2,1,0:T(8,128)} %uz.1, s32[1,256]{1,0:T(1,128)} %epos.3, s32[1,256]{1,0:T(1,128)} %delay.3, ...), custom_call_target="tpu_custom_call" | custom-call | flops 2000000000 | bytes 13631488 | tf_op jit(solution)/shard_map/start/pallas_call | solution.py:187
  7.6 11.9 %all-to-all-start = ((f32[128,4,8,256]{3,2,1,0:T(8,128)}), f32[128,4,8,256]{3,2,1,0:T(8,128)}, u32[]{:S(2)}, u32[]{:S(2)}) async-start(f32[128,4,8,256]{3,2,1,0:T(8,128)} %start.1), calls=%async_computation | async-start | bytes 8388608 | tf_op jit(solution)/shard_map/all_to_all | solution.py:522
  19.5 0.7 pad_add_fusion.ids
  20.1 18.0 %prepare.1 = (f32[4,256,256]{2,1,0:T(8,128)}, f32[4,256,256]{2,1,0:T(8,128)}, f32[4,256,256]{2,1,0:T(8,128)}, f32[4,256,256]{2,1,0:T(8,128)}, f32[4,256,256]{2,1...) custom-call(s32[2]{0:T(128)} %pad_add_fusion.ids, ...), custom_call_target="tpu_custom_call" | custom-call | flops 8000000000 | bytes 23068672 | tf_op jit(solution)/shard_map/prepare/pallas_call | solution.py:259
  38.2 33.0 %all-to-all-done = f32[128,4,8,256]{3,2,1,0:T(8,128)} async-done(((f32[128,4,8,256]{3,2,1,0:T(8,128)}), f32[128,4,8,256]{3,2,1,0:T(8,128)}, u32[]{:S(2)}, u32[]{:S(2)}) %all-to-all-start) | async-done | bytes 4194336 | tf_op jit(solution)/shard_map/all_to_all | solution.py:522
  71.2 4.6 %lines_forward.1 = (f32[64,2,2,8,256]{4,3,2,1,0:T(8,128)S(1)}, f32[4,256,256]{2,1,0:T(8,128)S(1)}, f32[4,256,256]{2,1,0:T(8,128)S(1)}, f32[4,256,256]{2,1,0:T(8,128)S(1)}) custom-call(f32[64,2,4,8,256]{4,3,2,1,0:T(8,128)} %bitcast.3.lines, f32[256,256]{1,0:T(8,128)S(1)} %copy-done.17, f32[256,256]{1,0:T(8,128)S(1)} %copy-done.16), custom_call_target="tpu_custom_call" | custom-call | flops 1600000000 | bytes 9437184 | tf_op jit(solution)/shard_map/lines_forward/pallas_call | solution.py:287
  75.9 0.0 copy-start.1
  75.9 0.0 copy-start.4
  75.9 0.0 copy-start.5
  75.9 0.0 copy-start.8
  75.9 34.1 %all_to_all.20.xs = f32[128,2,8,256]{3,2,1,0:T(8,128)S(1)} all-to-all(f32[128,2,8,256]{3,2,1,0:T(8,128)S(1)} %bitcast.9), channel_id=1, replica_groups=mesh['emit'=2,'slab'=64] {'slab','emit'}, dimensions={0} | all-to-all | bytes 4194304 | tf_op jit(solution)/shard_map/all_to_all | solution.py:522
  110.0 0.0 copy-done.12
  110.0 0.0 copy-done.13
  110.0 0.0 copy-done.14
  110.0 0.0 copy-done.15
  110.1 0.0 copy-done.1
  110.1 0.0 copy-done.4
  110.1 0.0 copy-done.5
  110.1 4.6 %slab_middle.1 = (f32[128,3,8,256]{3,2,1,0:T(8,128)S(1)}, f32[4,256,256]{2,1,0:T(8,128)S(1)}, f32[4,256,256]{2,1,0:T(8,128)S(1)}, f32[8,256,256]{2,1,0:T(8,128)S(1)}, f32[8,256,256]{2,1,0:T(8,128)S(1)}) custom-call(f32[128,8,256]{2,1,0:T(8,128)S(1)} %copy-done.15, f32[128,2,8,256]{3,2,1,0:T(8,128)S(1)} %all_to_all.20.xs, f32[4,256,256]{2,1,0:T(8,128)S(1)} %copy-done.1, ...), custom_call_target="tpu_custom_call" | custom-call | flops 3200000000 | bytes 18874368 | tf_op jit(solution)/shard_map/slab_middle/pallas_call | solution.py:287
  114.7 45.1 %all_to_all.21 = f32[128,3,8,256]{3,2,1,0:T(8,128)S(1)} all-to-all(f32[128,3,8,256]{3,2,1,0:T(8,128)S(1)} %get-tuple-element.64), channel_id=1, replica_groups=mesh['emit'=2,'slab'=64] {'slab','emit'}, dimensions={0} | all-to-all | bytes 6291456 | tf_op jit(solution)/shard_map/all_to_all | solution.py:522
  159.9 2.3 lines_adjoint.1
  162.2 28.4 %all_to_all.22.xs = f32[128,24,128]{2,1,0:T(8,128)S(1)} all-to-all(f32[128,24,128]{2,1,0:T(8,128)S(1)} %bitcast.8), channel_id=1, replica_groups=mesh['emit'=2,'slab'=64] {'slab','emit'}, dimensions={0} | all-to-all | bytes 3145728 | tf_op jit(solution)/shard_map/all_to_all | solution.py:522
  190.7 0.4 slab_last_bulk.1
  191.0 1.9 collective-permute-start
  192.9 0.0 copy-start.2
  192.9 0.0 copy-start.3
  193.0 4.0 %slab_last_buoy.1.t2 = f32[4,256,256]{2,1,0:T(8,128)S(1)} custom-call(s32[2]{0:T(128)S(1)} %copy-done.18, f32[128,24,128]{2,1,0:T(8,128)S(1)} %all_to_all.22.xs, f32[4,256,256]{2,1,0:T(8,128)S(1)} %get-tuple-element.72.p_s, f32[4,256,256]{2,1,0:T(8,128)S(1)} %copy-done.1, f32[4,256,256]{2,1,0:T(8,128)S(1)} %copy-done.6, f32[4,256,256]{2,1,0:T(8,128)S(1)} %copy-done.7, ...), custom_call_target="tpu_custom_call" | custom-call | flops 2400000000 | bytes 16777216 | tf_op jit(solution)/shard_map/slab_last_buoy/pallas_call | solution.py:479
  197.0 1.8 collective-permute-start.1
  198.8 19.9 %collective-permute-done.other = f32[4,256,256]{2,1,0:T(8,128)S(1)} collective-permute-done((f32[4,256,256]{2,1,0:T(8,128)S(1)}, f32[4,256,256]{2,1,0:T(8,128)S(1)}, u32[]{:S(2)}, u32[]{:S(2)}) %collective-permute-start) | collective-permute-done | bytes 1048608 | tf_op jit(solution)/shard_map/ppermute | solution.py:526
  218.7 1.4 finish_speed.1
  220.1 19.7 %collective-permute-done.1.other = f32[4,256,256]{2,1,0:T(8,128)S(1)} collective-permute-done((f32[4,256,256]{2,1,0:T(8,128)S(1)}, f32[4,256,256]{2,1,0:T(8,128)S(1)}, u32[]{:S(2)}, u32[]{:S(2)}) %collective-permute-start.1) | collective-permute-done | bytes 1048608 | tf_op jit(solution)/shard_map/ppermute | solution.py:526
  239.8 1.2 finish_density.1
  (25 shorter events, 0.1 us)
Async XLA Ops:
  7.6 63.6 %all-to-all-start = ((f32[128,4,8,256]{3,2,1,0:T(8,128)}), f32[128,4,8,256]{3,2,1,0:T(8,128)}, u32[]{:S(2)}, u32[]{:S(2)}) async-start(f32[128,4,8,256]{3,2,1,0:T(8,128)} %start.1), calls=%async_computation | async-start | bytes 8388608 | tf_op jit(solution)/shard_map/all_to_all | solution.py:522
  20.1 51.1 %copy-start.16 = (f32[256,256]{1,0:T(8,128)S(1)}, f32[256,256]{1,0:T(8,128)}, u32[]{:S(2)}) copy-start(f32[256,256]{1,0:T(8,128)} %constant.20.clone.tm) | copy-start | bytes 786436
  20.1 51.1 %copy-start.17 = (f32[256,256]{1,0:T(8,128)S(1)}, f32[256,256]{1,0:T(8,128)}, u32[]{:S(2)}) copy-start(f32[256,256]{1,0:T(8,128)} %constant.19.clone.gm) | copy-start | bytes 786436
  71.2 38.8 %copy-start.10 = (f32[4,256,256]{2,1,0:T(8,128)S(1)}, f32[4,256,256]{2,1,0:T(8,128)}, u32[]{:S(2)}) copy-start(f32[4,256,256]{2,1,0:T(8,128)} %get-tuple-element.59.pm) | copy-start | bytes 3145732
  71.2 38.8 %copy-start.11 = (f32[4,256,256]{2,1,0:T(8,128)S(1)}, f32[4,256,256]{2,1,0:T(8,128)}, u32[]{:S(2)}) copy-start(f32[4,256,256]{2,1,0:T(8,128)} %get-tuple-element.60.cdk) | copy-start | bytes 3145732
  71.2 38.8 %copy-start.12 = (f32[4,256,256]{2,1,0:T(8,128)S(1)}, f32[4,256,256]{2,1,0:T(8,128)}, u32[]{:S(2)}) copy-start(f32[4,256,256]{2,1,0:T(8,128)} %get-tuple-element.61.wb) | copy-start | bytes 3145732
  71.2 38.8 %copy-start.13 = (f32[4,256,256]{2,1,0:T(8,128)S(1)}, f32[4,256,256]{2,1,0:T(8,128)}, u32[]{:S(2)}) copy-start(f32[4,256,256]{2,1,0:T(8,128)} %get-tuple-element.62.yz1) | copy-start | bytes 3145732
  71.2 38.8 %copy-start.14 = (f32[4,256,256]{2,1,0:T(8,128)S(1)}, f32[4,256,256]{2,1,0:T(8,128)}, u32[]{:S(2)}) copy-start(f32[4,256,256]{2,1,0:T(8,128)} %get-tuple-element.63.yz0) | copy-start | bytes 3145732
  71.2 38.8 %copy-start.15 = (f32[128,8,256]{2,1,0:T(8,128)S(1)}, f32[128,8,256]{2,1,0:T(8,128)}, u32[]{:S(2)}) copy-start(f32[128,8,256]{2,1,0:T(8,128)} %get-tuple-element.53.axs) | copy-start | bytes 3145732
  75.9 34.2 %copy-start.1 = (f32[4,256,256]{2,1,0:T(8,128)S(1)}, f32[4,256,256]{2,1,0:T(8,128)}, u32[]{:S(2)}) copy-start(f32[4,256,256]{2,1,0:T(8,128)} %get-tuple-element.56.dk) | copy-start | bytes 3145732
  75.9 34.2 %copy-start.4 = (f32[256,256]{1,0:T(8,128)S(1)}, f32[256,256]{1,0:T(8,128)}, u32[]{:S(2)}) copy-start(f32[256,256]{1,0:T(8,128)} %constant.18.clone.tm) | copy-start | bytes 786436
  75.9 34.2 %copy-start.5 = (f32[256,256]{1,0:T(8,128)S(1)}, f32[256,256]{1,0:T(8,128)}, u32[]{:S(2)}) copy-start(f32[256,256]{1,0:T(8,128)} %constant.17.clone.gm) | copy-start | bytes 786436
  75.9 34.2 %copy-start.8 = (f32[4,256,256]{2,1,0:T(8,128)S(1)}, f32[4,256,256]{2,1,0:T(8,128)}, u32[]{:S(2)}) copy-start(f32[4,256,256]{2,1,0:T(8,128)} %get-tuple-element.57.stay) | copy-start | bytes 3145732
  75.9 34.2 %copy-start.9 = (f32[4,256,256]{2,1,0:T(8,128)S(1)}, f32[4,256,256]{2,1,0:T(8,128)}, u32[]{:S(2)}) copy-start(f32[4,256,256]{2,1,0:T(8,128)} %get-tuple-element.58.b) | copy-start | bytes 3145732
  162.2 30.7 %copy-start = (f32[4,4,256,256]{3,2,1,0:T(8,128)S(1)}, f32[4,4,256,256]{3,2,1,0:T(8,128)}, u32[]{:S(2)}) copy-start(f32[4,4,256,256]{3,2,1,0:T(8,128)} %get-tuple-element.77.late) | copy-start | bytes 12582916
  162.2 30.7 %copy-start.6 = (f32[4,256,256]{2,1,0:T(8,128)S(1)}, f32[4,256,256]{2,1,0:T(8,128)}, u32[]{:S(2)}) copy-start(f32[4,256,256]{2,1,0:T(8,128)} %get-tuple-element.73.gy0) | copy-start | bytes 3145732
  162.2 30.7 %copy-start.7 = (f32[4,256,256]{2,1,0:T(8,128)S(1)}, f32[4,256,256]{2,1,0:T(8,128)}, u32[]{:S(2)}) copy-start(f32[4,256,256]{2,1,0:T(8,128)} %get-tuple-element.74.gz0) | copy-start | bytes 3145732
  162.2 30.7 %copy-start.18 = (s32[2]{0:T(128)S(1)}, s32[2]{0:T(128)}, u32[]{:S(2)}) copy-start(s32[2]{0:T(128)} %pad_add_fusion.ids) | copy-start | bytes 28
  191.0 27.7 %collective-permute-start = (f32[4,256,256]{2,1,0:T(8,128)S(1)}, f32[4,256,256]{2,1,0:T(8,128)S(1)}, u32[]{:S(2)}, u32[]{:S(2)}) collective-permute-start(f32[4,256,256]{2,1,0:T(8,128)S(1)} %get-tuple-element.70.t1), channel_id=1, source_target_pairs={{0,64},{64,0},{1,65},{65,1},{2,66},{66,2},{3,67},{67,3},{4,68},{68... | collective-permute-start | bytes 3145736 | tf_op jit(solution)/shard_map/ppermute | solution.py:526
  192.9 25.8 %copy-start.2 = (f32[4,256,256]{2,1,0:T(8,128)S(1)}, f32[4,256,256]{2,1,0:T(8,128)}, u32[]{:S(2)}) copy-start(f32[4,256,256]{2,1,0:T(8,128)} %c.5) | copy-start | bytes 3145732
  192.9 25.8 %copy-start.3 = (f32[4,256,256]{2,1,0:T(8,128)S(1)}, f32[4,256,256]{2,1,0:T(8,128)}, u32[]{:S(2)}) copy-start(f32[4,256,256]{2,1,0:T(8,128)} %rho.5) | copy-start | bytes 3145732
  197.0 42.8 %collective-permute-start.1 = (f32[4,256,256]{2,1,0:T(8,128)S(1)}, f32[4,256,256]{2,1,0:T(8,128)S(1)}, u32[]{:S(2)}, u32[]{:S(2)}) collective-permute-start(f32[4,256,256]{2,1,0:T(8,128)S(1)} %slab_last_buoy.1.t2), channel_id=1, source_target_pairs={{0,64},{64,0},{1,65},{65,1},{2,66},{66,2},{3,67},{67,3},{4,68},{68... | collective-permute-start | bytes 3145736 | tf_op jit(solution)/shard_map/ppermute | solution.py:526
